TPU v7x, 32 devices: a whole 2x2x4 slice. The times are simulated.
32 devices in a mesh: cfg: 2 (over x), ta: 2 (over core), sa: 8 (over z, y).
Axes of the slice: x: 2, y: 2, z: 4, core: 2. Of those that a mesh axis runs over, the one named last changes fastest.
Arguments:
- links: float32 [4, 3, 2, 3, 3, 32, 1024], P(None, None, None, None, None, 'sa', 'ta'), may hold values from -2.5 to 2.5
- vectors: float32 [4, 16, 2, 3, 32, 1024], P('ta', None, None, None, 'sa'), may hold values from -6 to 6
Outputs:
- filtered: float32 [8, 16, 2, 3, 32, 1024], P(('cfg', 'ta'), None, None, None, 'sa'), parts along dimension 0
- grams: float32 [8, 2, 2, 16, 16], P(('cfg', 'ta')), parts along dimension 0
There are 2 independent parts, one for each index of `cfg`. A program takes and returns all parts, laid end to end along the dimension named above; an argument that names none is the same for every part. Nothing has to cross between parts.
All inputs are finite; a program needn't handle non-finite values.
Results may differ from a plain program's by a relative error of at most 0.00011.
Values sent between devices are 32-bit elements; how exact they have to be, the bound alone decides.
A program may use at most 256 MiB of HBM per device.

v0:
```python
import jax
import jax.numpy as jnp
from jax import lax
from jax.sharding import PartitionSpec as P

LX = 32
DEG = 3


def from_behind(x, axis, by):
    devices = lax.axis_size(axis)
    return lax.ppermute(x, axis, [(i, (i + by) % devices) for i in range(devices)])


def extended(block, sides, width):
    for axis, dim in sides:
        count = lax.axis_size(axis)
        forward = [(i, i + 1) for i in range(count - 1)]
        forward.append((count - 1, 0))
        backward = [(target, source) for source, target in forward]
        low = lax.ppermute(
            lax.slice_in_dim(block, block.shape[dim] - width, None, axis=dim), axis, forward
        )
        high = lax.ppermute(lax.slice_in_dim(block, 0, width, axis=dim), axis, backward)
        block = jnp.concatenate([low, block, high], axis=dim)
    return block


def mat_vec(matrix, field):
    mat_re = matrix[:, None, 0]
    mat_im = matrix[:, None, 1]
    vec_re = field[:, :, 0][:, :, None]
    vec_im = field[:, :, 1][:, :, None]
    real_part = jnp.sum(mat_re * vec_re - mat_im * vec_im, axis=3)
    imag_part = jnp.sum(mat_re * vec_im + mat_im * vec_re, axis=3)
    return jnp.stack([real_part, imag_part], axis=2)


def adjoint(matrix):
    return jnp.stack([jnp.swapaxes(matrix[:, 0], 1, 2), -jnp.swapaxes(matrix[:, 1], 1, 2)], axis=1)


def plane_roll(array, offset, direction):
    shape = array.shape
    grid = array.reshape(shape[:-1] + (-1, LX))
    rolled = jnp.roll(grid, offset, axis=-1 if direction == 0 else -2)
    return rolled.reshape(shape)


def gram_pair(left, right):
    count_t, count_n = (left.shape[0], left.shape[1])
    left_flat = left.reshape(count_t, count_n, 2, -1)
    right_flat = right.reshape(count_t, count_n, 2, -1)

    def inner(first, second):
        return jnp.einsum("tik,tjk->tij", first, second, precision=lax.Precision.HIGHEST)

    real_part = inner(left_flat[:, :, 0], right_flat[:, :, 0]) + inner(
        left_flat[:, :, 1], right_flat[:, :, 1]
    )
    imag_part = inner(left_flat[:, :, 0], right_flat[:, :, 1]) - inner(
        left_flat[:, :, 1], right_flat[:, :, 0]
    )
    return (real_part, imag_part)


def stack_grams(field, image):
    over_re, over_im = gram_pair(field, field)
    lap_re, lap_im = gram_pair(field, image)
    return jnp.stack(
        [jnp.stack([over_re, over_im], axis=1), jnp.stack([lap_re, lap_im], axis=1)], axis=1
    )


def build_operator(link_set, depth_terms):

    def operator(field):
        total = jnp.zeros(field.shape, jnp.float32)
        for direction in range(2):
            matrix = link_set[:, direction]
            forward = mat_vec(matrix, plane_roll(field, -1, direction))
            backward = plane_roll(mat_vec(adjoint(matrix), field), 1, direction)
            total = total + forward
            total = total + backward
        forward, backward = depth_terms(field)
        total = total + forward
        total = total + backward
        return 6.0 * field - total

    return operator


def run_filter(operator, start):

    def scaled_apply(field):
        return (operator(field) - 7.0 * field) / 5.5

    previous = start
    current = scaled_apply(start)

    def advance(turn, carry):
        older, newer = carry
        return (newer, 2.0 * scaled_apply(newer) - older)

    previous, current = lax.fori_loop(0, DEG - 1, advance, (previous, current))
    return current


def on_device(links, vectors):
    local_links = lax.all_to_all(links, "ta", split_axis=0, concat_axis=6, tiled=True)
    depth_links = local_links[:, 2]
    below_links = from_behind(depth_links[:, :, :, :, -1:], "sa", 1)
    prior_links = adjoint(jnp.concatenate([below_links, depth_links[:, :, :, :, :-1]], axis=4))

    def depth_terms(field):
        padded = extended(field, (("sa", 4),), 1)
        forward = mat_vec(depth_links, padded[:, :, :, :, 2:])
        backward = mat_vec(prior_links, padded[:, :, :, :, :-2])
        return (forward, backward)

    operator = build_operator(local_links, depth_terms)
    current = run_filter(operator, vectors)
    image = operator(current)
    raw_sums = lax.psum(stack_grams(current, image), "sa")
    inverse = lax.rsqrt(jnp.diagonal(raw_sums[:, 0, 0], axis1=1, axis2=2))
    grams = raw_sums * inverse[:, None, None, :, None] * inverse[:, None, None, None, :]
    filtered = current * inverse[:, :, None, None, None, None]
    return (filtered, grams)


def solution(mesh):
    in_specs = (P(None, None, None, None, None, "sa", "ta"), P("ta", None, None, None, "sa", None))
    out_specs = (
        P(("cfg", "ta"), None, None, None, "sa", None),
        P(("cfg", "ta"), None, None, None, None),
    )
    return jax.shard_map(
        on_device, mesh=mesh, in_specs=in_specs, out_specs=out_specs, check_vma=False
    )
```

profile of v0, /device:TPU:0, one launch (start us, length us, event | category | flops | bytes accessed | tf_op | source)
XLA Modules:
  0.0 1089.9 jit_solution(13699124140673148691)
XLA Ops:
  35.1 12.5 %slice.498 = f32[2,16,2,3,4,32,31]{6,5,4,3,2,1,0:T(8,128)} slice(f32[2,16,2,3,4,32,32]{6,5,4,3,2,1,0:T(8,128)} %reshape.137), slice={[0:2], [0:16], [0:2], [0:3], [0:4], [0:32], [1:32]} | slice | bytes 6094848 | tf_op jit(solution)/shard_map/jit(_roll_static)/slice | solution.py:46
  49.8 12.2 %slice.507 = f32[2,16,2,3,4,31,32]{6,5,4,3,2,1,0:T(8,128)} slice(f32[2,16,2,3,4,32,32]{6,5,4,3,2,1,0:T(8,128)} %reshape.137), slice={[0:2], [0:16], [0:2], [0:3], [0:4], [1:32], [0:32]} | slice | bytes 6094848 | tf_op jit(solution)/shard_map/jit(_roll_static)/slice | solution.py:46
  62.0 14.7 %pad_maximum_fusion.4 = f32[2,16,2,3,4,32,32]{6,5,4,3,2,1,0:T(8,128)} fusion(f32[2,16,2,3,4,32,1]{6,5,4,3,2,1,0:T(8,128)} %bitcast.389, f32[2,16,2,3,4,32,31]{6,5,4,3,2,1,0:T(8,128)} %slice.498), kind=kLoop, calls=%fused_computation.54 | loop fusion | flops 786432 | bytes 6291456 | tf_op jit(solution)/shard_map/jit(_roll_static)/concatenate | solution.py:46
  91.7 12.2 %pad_maximum_fusion.6 = f32[2,16,2,3,4,32,32]{6,5,4,3,2,1,0:T(8,128)} fusion(f32[2,16,2,3,4,1,32]{6,5,4,3,2,1,0:T(1,128)S(1)} %slice.508, f32[2,16,2,3,4,31,32]{6,5,4,3,2,1,0:T(8,128)} %slice.507), kind=kLoop, calls=%fused_computation.56 | loop fusion | flops 786432 | bytes 6291456 | tf_op jit(solution)/shard_map/jit(_roll_static)/concatenate | solution.py:46
  177.5 11.6 %pad_maximum_fusion.7 = f32[2,16,2,3,4,32,32]{6,5,1,4,3,0,2:T(8,128)} fusion(f32[2,16,2,3,4,31,32]{6,5,1,4,3,0,2:T(8,128)} %bitcast.404, f32[2,16,2,3,4,1,32]{6,5,1,4,3,0,2:T(1,128)S(1)} %slice.512), kind=kLoop, calls=%fused_computation.57 | loop fusion | flops 786432 | bytes 6291456 | tf_op jit(solution)/shard_map/jit(_roll_static)/concatenate | solution.py:46
  189.2 11.0 %reshape.141 = f32[2,16,2,3,4,1024]{5,1,4,3,0,2:T(8,128)} reshape(f32[2,16,2,3,4,32,32]{6,5,1,4,3,0,2:T(8,128)} %pad_maximum_fusion.7) | data formatting | bytes 6291456 | tf_op jit(solution)/shard_map/reshape | solution.py:47
  221.4 12.5 %slice.503 = f32[2,16,2,3,4,32,1]{6,5,1,4,3,0,2:T(8,128)} slice(f32[2,16,2,3,4,32,32]{6,5,1,4,3,0,2:T(8,128)} %constant_dynamic-update-slice_fusion.8), slice={[0:2], [0:16], [0:2], [0:3], [0:4], [0:32], [31:32]} | slice | bytes 196608 | tf_op jit(solution)/shard_map/jit(_roll_static)/slice | solution.py:46
  233.9 14.7 %pad_maximum_fusion.5 = f32[2,16,2,3,4,32,32]{6,5,1,4,3,0,2:T(8,128)} fusion(f32[2,16,2,3,4,32,31]{6,5,1,4,3,0,2:T(8,128)} %bitcast.398, f32[2,16,2,3,4,32,1]{6,5,1,4,3,0,2:T(8,128)} %slice.503), kind=kLoop, calls=%fused_computation.55 | loop fusion | flops 786432 | bytes 6291456 | tf_op jit(solution)/shard_map/jit(_roll_static)/concatenate | solution.py:46
  273.0 487.8 %while.14 = (s32[]{:T(128)}, f32[2,16,2,3,4,1024]{5,1,4,3,0,2:T(8,128)}, f32[2,16,2,3,4,1024]{5,1,4,3,0,2:T(8,128)S(1)}, f32[2,3,2,3,3,4,1024]{6,5,3,4,0,2,1:T(4...) while((s32[]{:T(128)}, ...), condition=%wide.region_25.26_spmd, body=%wide.region_12.25_spmd.sunk | while | flops 66846720 | bytes 349962944 | solution.py:105
  288.2 12.5 %slice.690 = f32[2,16,2,3,4,32,31]{6,5,1,4,3,0,2:T(8,128)} slice(f32[2,16,2,3,4,32,32]{6,5,1,4,3,0,2:T(8,128)} %reshape.162), slice={[0:2], [0:16], [0:2], [0:3], [0:4], [0:32], [1:32]} | slice | bytes 6094848 | tf_op jit(solution)/shard_map/while/body/eval_jaxpr/jit(_roll_static)/slice | solution.py:46
  302.8 12.1 %slice.692 = f32[2,16,2,3,4,31,32]{6,5,1,4,3,0,2:T(8,128)} slice(f32[2,16,2,3,4,32,32]{6,5,1,4,3,0,2:T(8,128)} %reshape.162), slice={[0:2], [0:16], [0:2], [0:3], [0:4], [1:32], [0:32]} | slice | bytes 6094848 | tf_op jit(solution)/shard_map/while/body/eval_jaxpr/jit(_roll_static)/slice | solution.py:46
  376.6 12.4 %slice.689 = f32[2,16,2,3,4,32,1]{6,5,1,4,3,0,2:T(8,128)} slice(f32[2,16,2,3,4,32,32]{6,5,1,4,3,0,2:T(8,128)} %constant_dynamic-update-slice_fusion.30), slice={[0:2], [0:16], [0:2], [0:3], [0:4], [0:32], [31:32]} | slice | bytes 196608 | tf_op jit(solution)/shard_map/while/body/eval_jaxpr/jit(_roll_static)/slice | solution.py:46
  389.0 14.5 %pad_maximum_fusion.22 = f32[2,16,2,3,4,32,32]{6,5,1,4,3,0,2:T(8,128)} fusion(f32[2,16,2,3,4,32,1]{6,5,1,4,3,0,2:T(8,128)} %bitcast.385, f32[2,16,2,3,4,32,31]{6,5,1,4,3,0,2:T(8,128)} %slice.690), kind=kLoop, calls=%fused_computation.1.clone.1 | loop fusion | flops 786432 | bytes 6291456 | tf_op jit(solution)/shard_map/while/body/eval_jaxpr/jit(_roll_static)/concatenate | solution.py:46
  418.2 11.6 %pad_maximum_fusion.20 = f32[2,16,2,3,4,32,32]{6,5,1,4,3,0,2:T(8,128)} fusion(f32[2,16,2,3,4,31,32]{6,5,1,4,3,0,2:T(8,128)} %bitcast.387, f32[2,16,2,3,4,1,32]{6,5,1,4,3,0,2:T(1,128)} %slice.688), kind=kLoop, calls=%fused_computation.4.clone.1 | loop fusion | flops 786432 | bytes 6291456 | tf_op jit(solution)/shard_map/while/body/eval_jaxpr/jit(_roll_static)/concatenate | solution.py:46
  429.8 14.6 %pad_maximum_fusion.21 = f32[2,16,2,3,4,32,32]{6,5,1,4,3,0,2:T(8,128)} fusion(f32[2,16,2,3,4,32,31]{6,5,1,4,3,0,2:T(8,128)} %bitcast.386, f32[2,16,2,3,4,32,1]{6,5,1,4,3,0,2:T(8,128)} %slice.689), kind=kLoop, calls=%fused_computation.2.clone.1 | loop fusion | flops 786432 | bytes 6291456 | tf_op jit(solution)/shard_map/while/body/eval_jaxpr/jit(_roll_static)/concatenate | solution.py:46
  444.4 12.0 %pad_maximum_fusion.23 = f32[2,16,2,3,4,32,32]{6,5,1,4,3,0,2:T(8,128)} fusion(f32[2,16,2,3,4,1,32]{6,5,1,4,3,0,2:T(1,128)S(1)} %slice.691, f32[2,16,2,3,4,31,32]{6,5,1,4,3,0,2:T(8,128)} %slice.692), kind=kLoop, calls=%fused_computation.3.clone.1 | loop fusion | flops 786432 | bytes 6291456 | tf_op jit(solution)/shard_map/while/body/eval_jaxpr/jit(_roll_static)/concatenate | solution.py:46
  528.5 12.5 %slice.690 = f32[2,16,2,3,4,32,31]{6,5,1,4,3,0,2:T(8,128)} slice(f32[2,16,2,3,4,32,32]{6,5,1,4,3,0,2:T(8,128)} %reshape.162), slice={[0:2], [0:16], [0:2], [0:3], [0:4], [0:32], [1:32]} | slice | bytes 6094848 | tf_op jit(solution)/shard_map/while/body/eval_jaxpr/jit(_roll_static)/slice | solution.py:46
  543.1 12.1 %slice.692 = f32[2,16,2,3,4,31,32]{6,5,1,4,3,0,2:T(8,128)} slice(f32[2,16,2,3,4,32,32]{6,5,1,4,3,0,2:T(8,128)} %reshape.162), slice={[0:2], [0:16], [0:2], [0:3], [0:4], [1:32], [0:32]} | slice | bytes 6094848 | tf_op jit(solution)/shard_map/while/body/eval_jaxpr/jit(_roll_static)/slice | solution.py:46
  616.7 12.4 %slice.689 = f32[2,16,2,3,4,32,1]{6,5,1,4,3,0,2:T(8,128)} slice(f32[2,16,2,3,4,32,32]{6,5,1,4,3,0,2:T(8,128)} %constant_dynamic-update-slice_fusion.30), slice={[0:2], [0:16], [0:2], [0:3], [0:4], [0:32], [31:32]} | slice | bytes 196608 | tf_op jit(solution)/shard_map/while/body/eval_jaxpr/jit(_roll_static)/slice | solution.py:46
  629.1 14.5 %pad_maximum_fusion.22 = f32[2,16,2,3,4,32,32]{6,5,1,4,3,0,2:T(8,128)} fusion(f32[2,16,2,3,4,32,1]{6,5,1,4,3,0,2:T(8,128)} %bitcast.385, f32[2,16,2,3,4,32,31]{6,5,1,4,3,0,2:T(8,128)} %slice.690), kind=kLoop, calls=%fused_computation.1.clone.1 | loop fusion | flops 786432 | bytes 6291456 | tf_op jit(solution)/shard_map/while/body/eval_jaxpr/jit(_roll_static)/concatenate | solution.py:46
  658.3 11.6 %pad_maximum_fusion.20 = f32[2,16,2,3,4,32,32]{6,5,1,4,3,0,2:T(8,128)} fusion(f32[2,16,2,3,4,31,32]{6,5,1,4,3,0,2:T(8,128)} %bitcast.387, f32[2,16,2,3,4,1,32]{6,5,1,4,3,0,2:T(1,128)} %slice.688), kind=kLoop, calls=%fused_computation.4.clone.1 | loop fusion | flops 786432 | bytes 6291456 | tf_op jit(solution)/shard_map/while/body/eval_jaxpr/jit(_roll_static)/concatenate | solution.py:46
  669.9 14.6 %pad_maximum_fusion.21 = f32[2,16,2,3,4,32,32]{6,5,1,4,3,0,2:T(8,128)} fusion(f32[2,16,2,3,4,32,31]{6,5,1,4,3,0,2:T(8,128)} %bitcast.386, f32[2,16,2,3,4,32,1]{6,5,1,4,3,0,2:T(8,128)} %slice.689), kind=kLoop, calls=%fused_computation.2.clone.1 | loop fusion | flops 786432 | bytes 6291456 | tf_op jit(solution)/shard_map/while/body/eval_jaxpr/jit(_roll_static)/concatenate | solution.py:46
  684.5 12.0 %pad_maximum_fusion.23 = f32[2,16,2,3,4,32,32]{6,5,1,4,3,0,2:T(8,128)} fusion(f32[2,16,2,3,4,1,32]{6,5,1,4,3,0,2:T(1,128)S(1)} %slice.691, f32[2,16,2,3,4,31,32]{6,5,1,4,3,0,2:T(8,128)} %slice.692), kind=kLoop, calls=%fused_computation.3.clone.1 | loop fusion | flops 786432 | bytes 6291456 | tf_op jit(solution)/shard_map/while/body/eval_jaxpr/jit(_roll_static)/concatenate | solution.py:46
  723.3 10.9 reshape.164
  769.7 12.5 %slice.523 = f32[2,16,2,3,4,32,31]{6,5,1,4,3,0,2:T(8,128)} slice(f32[2,16,2,3,4,32,32]{6,5,1,4,3,0,2:T(8,128)} %reshape.143), slice={[0:2], [0:16], [0:2], [0:3], [0:4], [0:32], [1:32]} | slice | bytes 6094848 | tf_op jit(solution)/shard_map/jit(_roll_static)/slice | solution.py:46
  785.1 11.9 %slice.529 = f32[2,16,2,3,4,31,32]{6,5,1,4,3,0,2:T(8,128)} slice(f32[2,16,2,3,4,32,32]{6,5,1,4,3,0,2:T(8,128)} %reshape.143), slice={[0:2], [0:16], [0:2], [0:3], [0:4], [1:32], [0:32]} | slice | bytes 6094848 | tf_op jit(solution)/shard_map/jit(_roll_static)/slice | solution.py:46
  873.4 12.4 %slice.527 = f32[2,16,2,3,4,32,1]{6,5,1,4,3,0,2:T(8,128)} slice(f32[2,16,2,3,4,32,32]{6,5,1,4,3,0,2:T(8,128)} %constant_dynamic-update-slice_fusion.12), slice={[0:2], [0:16], [0:2], [0:3], [0:4], [0:32], [31:32]} | slice | bytes 196608 | tf_op jit(solution)/shard_map/jit(_roll_static)/slice | solution.py:46
  885.8 14.5 %pad_maximum_fusion.8 = f32[2,16,2,3,4,32,32]{6,5,1,4,3,0,2:T(8,128)} fusion(f32[2,16,2,3,4,32,1]{6,5,1,4,3,0,2:T(8,128)} %bitcast.388, f32[2,16,2,3,4,32,31]{6,5,1,4,3,0,2:T(8,128)} %slice.523), kind=kLoop, calls=%fused_computation.58 | loop fusion | flops 786432 | bytes 6291456 | tf_op jit(solution)/shard_map/jit(_roll_static)/concatenate | solution.py:46
  920.9 11.6 %pad_maximum_fusion.11 = f32[2,16,2,3,4,32,32]{6,5,1,4,3,0,2:T(8,128)} fusion(f32[2,16,2,3,4,31,32]{6,5,1,4,3,0,2:T(8,128)} %bitcast.405, f32[2,16,2,3,4,1,32]{6,5,1,4,3,0,2:T(1,128)S(1)} %slice.533), kind=kLoop, calls=%fused_computation.61 | loop fusion | flops 786432 | bytes 6291456 | tf_op jit(solution)/shard_map/jit(_roll_static)/concatenate | solution.py:46
  932.6 15.6 %pad_maximum_fusion.9 = f32[2,16,2,3,4,32,32]{6,5,1,4,3,0,2:T(8,128)} fusion(f32[2,16,2,3,4,32,31]{6,5,1,4,3,0,2:T(8,128)} %bitcast.399, f32[2,16,2,3,4,32,1]{6,5,1,4,3,0,2:T(8,128)} %slice.527), kind=kLoop, calls=%fused_computation.59 | loop fusion | flops 786432 | bytes 6291456 | tf_op jit(solution)/shard_map/jit(_roll_static)/concatenate | solution.py:46
  951.3 11.9 %pad_maximum_fusion.10 = f32[2,16,2,3,4,32,32]{6,5,1,4,3,0,2:T(8,128)} fusion(f32[2,16,2,3,4,1,32]{6,5,1,4,3,0,2:T(1,128)S(1)} %copy-done.72, f32[2,16,2,3,4,31,32]{6,5,1,4,3,0,2:T(8,128)} %slice.529), kind=kLoop, calls=%fused_computation.60 | loop fusion | flops 786432 | bytes 6291456 | tf_op jit(solution)/shard_map/jit(_roll_static)/concatenate | solution.py:46
  1046.0 38.4 %psum.7 = f32[2,2,2,16,16]{4,3,0,2,1:T(8,128)S(1)} all-reduce(f32[2,2,2,16,16]{4,3,0,2,1:T(8,128)S(1)} %pad_maximum_fusion.15), channel_id=1, replica_groups=mesh['cfg'=2,'ta'=2,'sa'=8] {'sa'}, use_global_device_ids=true, to_apply=%region_38.39 | all-reduce | flops 2048 | bytes 16384 | tf_op jit(solution)/shard_map/psum | solution.py:124
  (378 shorter events, 659.5 us)
Async XLA Ops:
  0.6 13.0 %copy-start.71 = (f32[4,3,2,3,3,4,512]{6,5,4,3,2,1,0:T(4,128)S(1)}, f32[4,3,2,3,3,4,512]{6,5,4,3,2,1,0:T(4,128)}, u32[]{:S(2)}) copy-start(f32[4,3,2,3,3,4,512]{6,5,4,3,2,1,0:T(4,128)} %param.4) | copy-start | bytes 5308420
  6.4 127.9 %collective-permute-start.4 = (f32[2,16,2,3,1,1024]{5,1,4,3,2,0:T(8,128)}, f32[2,16,2,3,1,1024]{5,1,4,3,2,0:T(8,128)}, u32[]{:S(2)}, u32[]{:S(2)}) collective-permute-start(f32[2,16,2,3,1,1024]{5,1,4,3,2,0:T(8,128)} %copy.91), channel_id=1, source_target_pairs={{0,1},{1,2},{2,3},{3,4},{4,5},{5,6},{6,7},{7,0},{8,9},{9,10},{10,1... | collective-permute-start | bytes 2359304 | tf_op jit(solution)/shard_map/ppermute | solution.py:21
  10.6 125.8 %collective-permute-start.2 = (f32[2,16,2,3,1,1024]{5,1,4,3,2,0:T(8,128)}, f32[2,16,2,3,1,1024]{5,1,4,3,2,0:T(8,128)}, u32[]{:S(2)}, u32[]{:S(2)}) collective-permute-start(f32[2,16,2,3,1,1024]{5,1,4,3,2,0:T(8,128)} %copy.88), channel_id=1, source_target_pairs={{1,0},{2,1},{3,2},{4,3},{5,4},{6,5},{7,6},{0,7},{9,8},{10,9},{11,1... | collective-permute-start | bytes 2359304 | tf_op jit(solution)/shard_map/ppermute | solution.py:24
  27.6 104.1 %collective-permute-start.3 = (f32[2,2,3,3,1,1024]{5,4,2,3,0,1:T(1,128)}, f32[2,2,3,3,1,1024]{5,4,2,3,0,1:T(1,128)}, u32[]{:S(2)}, u32[]{:S(2)}) collective-permute-start(f32[2,2,3,3,1,1024]{5,4,2,3,0,1:T(1,128)} %copy.89), channel_id=1, source_target_pairs={{0,1},{1,2},{2,3},{3,4},{4,5},{5,6},{6,7},{7,0},{8,9},{9,10},{10,1... | collective-permute-start | bytes 442376 | tf_op jit(solution)/shard_map/ppermute | solution.py:12
  118.6 7.6 copy-start.51
  118.6 7.6 copy-start.53
  189.2 11.0 %copy-start.47 = (f32[2,16,3,4,1024]{4,1,3,2,0:T(8,128)S(1)}, f32[2,16,3,4,1024]{4,1,3,2,0:T(8,128)}, u32[]{:S(2)}) copy-start(f32[2,16,3,4,1024]{4,1,3,2,0:T(8,128)} %get-tuple-element.153) | copy-start | bytes 4718596
  248.6 10.8 copy-start.41
  273.2 8.1 copy-start.21
  274.6 223.1 %collective-permute-start = (f32[2,16,2,3,1,1024]{5,1,4,3,0,2:T(8,128)}, f32[2,16,2,3,1,1024]{5,1,4,3,0,2:T(8,128)}, u32[]{:S(2)}, u32[]{:S(2)}) collective-permute-start(f32[2,16,2,3,1,1024]{5,1,4,3,0,2:T(8,128)} %get-tuple-element.372), channel_id=1, source_target_pairs={{0,1},{1,2},{2,3},{3,4},{4,5},{5,6},{6,7},{7,0},{8,9},{9,10},{10,1... | collective-permute-start | bytes 2359304 | tf_op jit(solution)/shard_map/while/body/eval_jaxpr/ppermute | solution.py:21
  275.9 223.9 %collective-permute-start.1 = (f32[2,16,2,3,1,1024]{5,1,4,3,0,2:T(8,128)}, f32[2,16,2,3,1,1024]{5,1,4,3,0,2:T(8,128)}, u32[]{:S(2)}, u32[]{:S(2)}) collective-permute-start(f32[2,16,2,3,1,1024]{5,1,4,3,0,2:T(8,128)} %get-tuple-element.374), channel_id=1, source_target_pairs={{1,0},{2,1},{3,2},{4,3},{5,4},{6,5},{7,6},{0,7},{9,8},{10,9},{11,1... | collective-permute-start | bytes 2359304 | tf_op jit(solution)/shard_map/while/body/eval_jaxpr/ppermute | solution.py:24
  302.8 12.1 %copy-start.13 = (f32[2,3,2,3,3,4,1024]{6,5,3,4,0,2,1:T(4,128)S(1)}, f32[2,3,2,3,3,4,1024]{6,5,3,4,0,2,1:T(4,128)}, u32[]{:S(2)}) copy-start(f32[2,3,2,3,3,4,1024]{6,5,3,4,0,2,1:T(4,128)} %get-tuple-element.409) | copy-start | bytes 5308420 | tf_op jit(solution)/shard_map/while
  444.3 12.0 %copy-start.4 = (f32[2,16,3,4,1024]{4,1,3,2,0:T(8,128)S(1)}, f32[2,16,3,4,1024]{4,1,3,2,0:T(8,128)}, u32[]{:S(2)}) copy-start(f32[2,16,3,4,1024]{4,1,3,2,0:T(8,128)} %get-tuple-element.361) | copy-start | bytes 4718596 | tf_op jit(solution)/shard_map/while
  513.6 8.1 copy-start.21
  514.9 223.1 %collective-permute-start = (f32[2,16,2,3,1,1024]{5,1,4,3,0,2:T(8,128)}, f32[2,16,2,3,1,1024]{5,1,4,3,0,2:T(8,128)}, u32[]{:S(2)}, u32[]{:S(2)}) collective-permute-start(f32[2,16,2,3,1,1024]{5,1,4,3,0,2:T(8,128)} %get-tuple-element.372), channel_id=1, source_target_pairs={{0,1},{1,2},{2,3},{3,4},{4,5},{5,6},{6,7},{7,0},{8,9},{9,10},{10,1... | collective-permute-start | bytes 2359304 | tf_op jit(solution)/shard_map/while/body/eval_jaxpr/ppermute | solution.py:21
  514.9 225.3 %collective-permute-start.1 = (f32[2,16,2,3,1,1024]{5,1,4,3,0,2:T(8,128)}, f32[2,16,2,3,1,1024]{5,1,4,3,0,2:T(8,128)}, u32[]{:S(2)}, u32[]{:S(2)}) collective-permute-start(f32[2,16,2,3,1,1024]{5,1,4,3,0,2:T(8,128)} %get-tuple-element.374), channel_id=1, source_target_pairs={{1,0},{2,1},{3,2},{4,3},{5,4},{6,5},{7,6},{0,7},{9,8},{10,9},{11,1... | collective-permute-start | bytes 2359304 | tf_op jit(solution)/shard_map/while/body/eval_jaxpr/ppermute | solution.py:24
  543.1 12.1 %copy-start.13 = (f32[2,3,2,3,3,4,1024]{6,5,3,4,0,2,1:T(4,128)S(1)}, f32[2,3,2,3,3,4,1024]{6,5,3,4,0,2,1:T(4,128)}, u32[]{:S(2)}) copy-start(f32[2,3,2,3,3,4,1024]{6,5,3,4,0,2,1:T(4,128)} %get-tuple-element.409) | copy-start | bytes 5308420 | tf_op jit(solution)/shard_map/while
  684.5 12.0 %copy-start.4 = (f32[2,16,3,4,1024]{4,1,3,2,0:T(8,128)S(1)}, f32[2,16,3,4,1024]{4,1,3,2,0:T(8,128)}, u32[]{:S(2)}) copy-start(f32[2,16,3,4,1024]{4,1,3,2,0:T(8,128)} %get-tuple-element.361) | copy-start | bytes 4718596 | tf_op jit(solution)/shard_map/while
  807.5 6.9 copy-start.25
  807.5 6.9 copy-start.68
  807.5 6.9 copy-start.70
  914.9 88.3 %collective-permute-start.6 = (f32[2,16,2,3,1,1024]{5,1,4,3,0,2:T(8,128)}, f32[2,16,2,3,1,1024]{5,1,4,3,0,2:T(8,128)}, u32[]{:S(2)}, u32[]{:S(2)}) collective-permute-start(f32[2,16,2,3,1,1024]{5,1,4,3,0,2:T(8,128)} %get-tuple-element.215), channel_id=1, source_target_pairs={{0,1},{1,2},{2,3},{3,4},{4,5},{5,6},{6,7},{7,0},{8,9},{9,10},{10,1... | collective-permute-start | bytes 2359304 | tf_op jit(solution)/shard_map/ppermute | solution.py:21
  932.6 15.6 %copy-start.44 = (f32[2,16,3,4,1024]{4,1,3,2,0:T(8,128)S(1)}, f32[2,16,3,4,1024]{4,1,3,2,0:T(8,128)}, u32[]{:S(2)}) copy-start(f32[2,16,3,4,1024]{4,1,3,2,0:T(8,128)} %get-tuple-element.219) | copy-start | bytes 4718596
  932.6 15.6 %copy-start.45 = (f32[2,16,3,4,1024]{4,1,3,2,0:T(8,128)S(1)}, f32[2,16,3,4,1024]{4,1,3,2,0:T(8,128)}, u32[]{:S(2)}) copy-start(f32[2,16,3,4,1024]{4,1,3,2,0:T(8,128)} %get-tuple-element.220) | copy-start | bytes 4718596
  932.6 15.6 %copy-start.56 = (f32[2,3,3,4,1024]{4,3,1,2,0:T(4,128)S(1)}, f32[2,3,3,4,1024]{4,3,1,2,0:T(4,128)}, u32[]{:S(2)}) copy-start(f32[2,3,3,4,1024]{4,3,1,2,0:T(4,128)} %copy-done.55) | copy-start | bytes 884740
  932.6 15.6 %copy-start.58 = (f32[2,3,3,4,1024]{4,3,1,2,0:T(4,128)S(1)}, f32[2,3,3,4,1024]{4,3,1,2,0:T(4,128)}, u32[]{:S(2)}) copy-start(f32[2,3,3,4,1024]{4,3,1,2,0:T(4,128)} %copy-done.57) | copy-start | bytes 884740
  951.3 11.9 %copy-start.75 = (f32[2,1,16,16]{3,2,0,1:T(8,128)S(1)}, f32[2,1,16,16]{3,2,0,1:T(8,128)}, u32[]{:S(2)}) copy-start(f32[2,1,16,16]{3,2,0,1:T(8,128)} %fusion.33) | copy-start | bytes 6148
  951.3 11.9 %copy-start.76 = (f32[2,1,16,16]{3,2,0,1:T(8,128)S(1)}, f32[2,1,16,16]{3,2,0,1:T(8,128)}, u32[]{:S(2)}) copy-start(f32[2,1,16,16]{3,2,0,1:T(8,128)} %fusion.31) | copy-start | bytes 6148
  994.8 6.8 copy-start.54
  994.8 20.7 %collective-permute-start.5 = (f32[2,16,2,3,1,1024]{5,1,4,3,0,2:T(8,128)}, f32[2,16,2,3,1,1024]{5,1,4,3,0,2:T(8,128)S(1)}, u32[]{:S(2)}, u32[]{:S(2)}) collective-permute-start(f32[2,16,2,3,1,1024]{5,1,4,3,0,2:T(8,128)} %get-tuple-element.216), channel_id=1, source_target_pairs={{1,0},{2,1},{3,2},{4,3},{5,4},{6,5},{7,6},{0,7},{9,8},{10,9},{11,1... | collective-permute-start | bytes 2359304 | tf_op jit(solution)/shard_map/ppermute | solution.py:24
  1033.8 7.7 copy-start.20
  1041.5 43.1 %copy-start.73 = (s32[16]{0:T(128)S(1)}, s32[16]{0:T(128)}, u32[]{:S(2)}) copy-start(s32[16]{0:T(128)} %or_bitcast_fusion) | copy-start | bytes 196
  (72 other events, 214.1 us)
where the time goes:
time: 1100 us; the launch traced here: 1090 us
  local copies, waits for them, and re-layouts  668 us (61%)
  other arithmetic  312 us (28%)
  blocking collectives  43.5 us (4%)
  matrix products  25 us (2%)
  starting transfers between devices  20.7 us (2%)
    concatenate x16, other arithmetic, plane_roll(): rolled = jnp.roll(grid, offset, axis=-1 if direction == 0 else -2)  212 us
    reshape x16, local copies, waits for them, and re-layouts, plane_roll(): return rolled.reshape(shape)  170 us
    slice x20, local copies, waits for them, and re-layouts, plane_roll(): rolled = jnp.roll(grid, offset, axis=-1 if direction == 0 else -2)  168 us
    another operation x24, local copies, waits for them, and re-layouts, mat_vec(): return jnp.stack([real_part, imag_part], axis=2)  134 us
    mul x29, local copies, waits for them, and re-layouts, mat_vec(): real_part = jnp.sum(mat_re * vec_re - mat_im * vec_im, axis=3)  42.5 us
    reduce_sum x16, other arithmetic, mat_vec(): real_part = jnp.sum(mat_re * vec_re - mat_im * vec_im, axis=3)  39.7 us
    while x82, local copies, waits for them, and re-layouts  39.3 us
    psum x1, blocking collectives, on_device(): raw_sums = lax.psum(stack_grams(current, image), 'sa')  38.4 us
  transfers between devices with their start and end apart: 9, of which 1 were waited for; matrix products, arithmetic and copies ran while one was open for 59% of the time, Pallas kernels for 0%

commit v1 on v0

v1 whole, which is shorter than its diff:
```python
import functools

import jax
import jax.numpy as jnp
from jax import lax
from jax.experimental import pallas as pl
from jax.experimental.pallas import tpu as pltpu
from jax.sharding import PartitionSpec as P

LX = 32
DEG = 3
LANES = 128
TILE = 8
F32 = jnp.float32


def from_behind(x, axis, by):
    devices = lax.axis_size(axis)
    return lax.ppermute(x, axis, [(i, (i + by) % devices) for i in range(devices)])


def butterfly(x, axis):
    devices = lax.axis_size(axis)
    if devices & (devices - 1):
        return lax.psum(x, axis)
    step = 1
    while step < devices:
        x = x + lax.ppermute(x, axis, [(i, i ^ step) for i in range(devices)])
        step *= 2
    return x


def iota(dim):
    return lax.broadcasted_iota(jnp.int32, (TILE, LANES), dim)


def rows_at(get, total, start):
    if 0 <= start and start + TILE <= total:
        return get(start, TILE)
    base = (start // TILE) * TILE
    offset = start - base
    first, second = get(base % total, TILE), get((base + TILE) % total, TILE)
    return pltpu.roll(jnp.where(iota(0) < offset, second, first), TILE - offset, 0)


def halo_rows(get, nz, tile):
    if nz == 1:
        return get(tile * TILE, TILE)
    out = None
    for part in range(max(TILE // nz, 1)):
        row = jnp.broadcast_to(get((tile * TILE) // nz + part, 1), (TILE, LANES))
        out = row if out is None else jnp.where(iota(0) < part * nz, out, row)
    return out


def shifted(get, halo, total, nz, tile, direction, ahead):
    start, lane = tile * TILE, iota(1)
    if direction == 0:
        here = get(start, TILE)
        if ahead:
            return jnp.where(
                lane % LX == LX - 1, pltpu.roll(here, LX - 1, 1), pltpu.roll(here, LANES - 1, 1)
            )
        return jnp.where(lane % LX == 0, pltpu.roll(here, LANES - LX + 1, 1), pltpu.roll(here, 1, 1))
    if direction == 1:
        here = get(start, TILE)
        if ahead:
            other = rows_at(get, total, start + nz)
            return pltpu.roll(jnp.where(lane < LX, other, here), LANES - LX, 1)
        other = rows_at(get, total, start - nz)
        return pltpu.roll(jnp.where(lane >= LANES - LX, other, here), LX, 1)
    edge = halo_rows(halo, nz, tile)
    if nz == 1:
        return edge
    other = rows_at(get, total, start + (1 if ahead else -1))
    return jnp.where(iota(0) % nz == (nz - 1 if ahead else 0), edge, other)


def reader(ref, *index):
    return lambda start, count: ref[(*index, pl.ds(start, count), slice(None))]


def back_links_kernel(nz, links, below, out):
    total = links.shape[2]
    comps = links.shape[1] // 3

    def body(comp, carry):
        for direction in range(3):
            where = direction * comps + comp
            for tile in range(total // TILE):
                out[0, where, pl.ds(tile * TILE, TILE), :] = shifted(
                    reader(links, 0, where), reader(below, 0, comp), total, nz, tile, direction, False
                )
        return carry

    lax.fori_loop(0, comps, body, 0)


def hop(links, vec, halo, n, total, nz, tile, direction, ahead, acc):
    here = pl.ds(tile * TILE, TILE)
    for col in range(3):
        part = [
            shifted(
                reader(vec, 0, n, p * 3 + col),
                None if halo is None else reader(halo, 0, n, p * 3 + col),
                total, nz, tile, direction, ahead,
            )
            for p in range(2)
        ]
        for row in range(3):
            at = (row * 3 + col) if ahead else (col * 3 + row)
            re = links[0, direction * 18 + at, here, :]
            im = links[0, direction * 18 + 9 + at, here, :]
            if ahead:
                acc[row] = acc[row] + re * part[0] - im * part[1]
                acc[3 + row] = acc[3 + row] + re * part[1] + im * part[0]
            else:
                acc[row] = acc[row] + re * part[0] + im * part[1]
                acc[3 + row] = acc[3 + row] + re * part[1] - im * part[0]


def apply_kernel(nz, first, *refs):
    links, back, vec, low, high = refs[:5]
    prev = None if first else refs[5]
    out, top, bottom = refs[-3:]
    total = vec.shape[3]
    chunks = total // nz

    def body(n, carry):
        for tile in range(total // TILE):
            here = pl.ds(tile * TILE, TILE)
            acc = [jnp.zeros((TILE, LANES), F32)] * 6
            for direction in range(3):
                hop(links, vec, high, n, total, nz, tile, direction, True, acc)
                hop(back, vec, low, n, total, nz, tile, direction, False, acc)
            for comp in range(6):
                own = vec[0, n, comp, here, :]
                value = ((6.0 * own - acc[comp]) - 7.0 * own) * (1.0 / 5.5)
                if not first:
                    value = 2.0 * value - prev[0, n, comp, here, :]
                out[0, n, comp, here, :] = value
        for comp in range(6):
            top[0, n, comp] = out[0, n, comp, pl.ds(nz - 1, chunks, stride=nz), :]
            bottom[0, n, comp] = out[0, n, comp, pl.ds(0, chunks, stride=nz), :]
        return carry

    lax.fori_loop(0, vec.shape[1], body, 0)


def ahead_kernel(nz, links, vec, high, out):
    total = vec.shape[3]

    def body(n, carry):
        for tile in range(total // TILE):
            acc = [jnp.zeros((TILE, LANES), F32)] * 6
            for direction in range(3):
                hop(links, vec, high, n, total, nz, tile, direction, True, acc)
            for comp in range(6):
                out[0, n, comp, pl.ds(tile * TILE, TILE), :] = acc[comp]
        return carry

    lax.fori_loop(0, vec.shape[1], body, 0)


def call(kernel, args, outs, flops):
    def spec(shape):
        return pl.BlockSpec((1,) + tuple(shape[1:]), lambda t: (t,) + (0,) * (len(shape) - 1))

    moved = 4 * sum(a.size for a in args) + 4 * sum(functools.reduce(lambda x, y: x * y, o) for o in outs)
    return pl.pallas_call(
        kernel,
        grid=(args[0].shape[0],),
        in_specs=[spec(a.shape) for a in args],
        out_specs=[spec(o) for o in outs],
        out_shape=[jax.ShapeDtypeStruct(o, F32) for o in outs],
        compiler_params=pltpu.CompilerParams(vmem_limit_bytes=40 * 2**20),
        cost_estimate=pl.CostEstimate(flops=flops, bytes_accessed=moved, transcendentals=0),
    )(*args)


def to_rows(x):
    lead, (nz, sites) = x.shape[:-2], x.shape[-2:]
    x = x.reshape(lead + (nz, sites // LANES, LANES))
    return jnp.swapaxes(x, -3, -2).reshape(lead + (-1, LANES))


def from_rows(x, nz):
    lead, rows = x.shape[:-2], x.shape[-2]
    x = x.reshape(lead + (rows // nz, nz, LANES))
    return jnp.swapaxes(x, -3, -2).reshape(lead + (nz, rows // nz * LANES))


def split(x):
    high = lax.reduce_precision(x, exponent_bits=8, mantissa_bits=7)
    return high.astype(jnp.bfloat16), (x - high).astype(jnp.bfloat16)


def raw_gram(left, right):
    (lh, ll), (rh, rl) = split(left), split(right)

    def dot(a, b):
        return jnp.einsum("tipk,tjqk->tipjq", a, b, preferred_element_type=F32)

    full = dot(lh, rh) + (dot(lh, rl) + dot(ll, rh))
    return full[:, :, 0, :, 0] + full[:, :, 1, :, 1], full[:, :, 0, :, 1] - full[:, :, 1, :, 0]


def on_device(links, vectors):
    nz = vectors.shape[4]
    count_t, count_n = vectors.shape[:2]
    groups = lax.axis_size("cfg")
    me = lax.axis_index("cfg")
    own_n = count_n // groups
    pieces = 2 if own_n % 2 == 0 else 1
    part_n = own_n // pieces

    own = lax.dynamic_slice_in_dim(vectors, me * own_n, own_n, axis=1)
    own = own.reshape(own.shape[:2] + (6,) + own.shape[4:])
    own = [own[:, k * part_n : (k + 1) * part_n] for k in range(pieces)]
    lows, highs = [], []
    for field in own:
        plane = (count_t, part_n, 6, -1, LANES)
        lows.append(from_behind(field[:, :, :, nz - 1].reshape(plane), "sa", 1))
        highs.append(from_behind(field[:, :, :, 0].reshape(plane), "sa", -1))
    fields = [to_rows(field) for field in own]

    rows = to_rows(links.reshape((links.shape[0], 54) + links.shape[5:]))
    rows = lax.all_to_all(rows, "ta", split_axis=0, concat_axis=2, tiled=True)
    below = from_behind(rows[:, 36:, nz - 1 :: nz], "sa", 1)
    (back,) = call(functools.partial(back_links_kernel, nz), (rows, below), [rows.shape], rows.size * 4)

    work = fields[0].size // 6
    older = [None] * pieces
    for turn in range(DEG):
        for k in range(pieces):
            args = (rows, back, fields[k], lows[k], highs[k])
            if turn:
                args = args + (older[k],)
            new, top, bottom = call(
                functools.partial(apply_kernel, nz, turn == 0),
                args,
                [fields[k].shape, lows[k].shape, lows[k].shape],
                work * 450,
            )
            older[k], fields[k] = fields[k], new
            highs[k] = from_behind(bottom, "sa", -1)
            if turn + 1 < DEG:
                lows[k] = from_behind(top, "sa", 1)

    images = [
        call(functools.partial(ahead_kernel, nz), (rows, fields[k], highs[k]), [fields[k].shape], work * 220)[0]
        for k in range(pieces)
    ]
    field = jnp.concatenate(fields, axis=1)
    image = jnp.concatenate(images, axis=1)
    every = lax.all_gather(field, "cfg", axis=1, tiled=True)

    def flat(x):
        return x.reshape(x.shape[:2] + (2, -1))

    both = jnp.concatenate([flat(field), flat(image)], axis=1)
    re, im = raw_gram(flat(every), both)
    raw = jnp.stack([re, im], axis=1).reshape(count_t, 2, count_n, 2, own_n)
    raw = jnp.moveaxis(raw, 3, 1)
    wide = jnp.zeros((count_t, 2, 2, count_n, count_n), F32)
    raw = lax.dynamic_update_slice_in_dim(wide, raw, me * own_n, axis=4)
    raw = butterfly(butterfly(raw, "sa"), "cfg")
    over, ahead = raw[:, 0], raw[:, 1]
    turned = jnp.swapaxes(ahead, 2, 3)
    lap = 6.0 * over - jnp.stack([ahead[:, 0] + turned[:, 0], ahead[:, 1] - turned[:, 1]], axis=1)
    inverse = lax.rsqrt(jnp.diagonal(over[:, 0], axis1=1, axis2=2))
    grams = jnp.stack([over, lap], axis=1)
    grams = grams * inverse[:, None, None, :, None] * inverse[:, None, None, None, :]
    filtered = every * inverse[:, :, None, None, None]
    filtered = from_rows(filtered, nz).reshape(vectors.shape)
    return (filtered, grams)


def solution(mesh):
    in_specs = (P(None, None, None, None, None, "sa", "ta"), P("ta", None, None, None, "sa", None))
    out_specs = (
        P(("cfg", "ta"), None, None, None, "sa", None),
        P(("cfg", "ta"), None, None, None, None),
    )
    return jax.shard_map(
        on_device, mesh=mesh, in_specs=in_specs, out_specs=out_specs, check_vma=False
    )
```

time: 1100 us -> 208 us (0.19)
  local copies, waits for them, and re-layouts: 668 us -> 58.8 us
  other arithmetic: 312 us -> 6.3 us
  blocking collectives: 43.5 us -> 6.6 us
  waiting for transfers between devices: 10.1 us -> 42.1 us
  Pallas kernels: 0 us -> 29 us
  starting transfers between devices: 20.7 us -> 40 us
  matrix products: 25 us -> 10.3 us
  between operations: 1.68 us -> 14.4 us
    concatenate x17 -> x2, other arithmetic: 213 us -> 1.33 us  [the longest x1 1.33 us: on_device(): image = jnp.concatenate(images, axis=1)]
    reshape x22 -> x5, local copies, waits for them, and re-layouts: 208 us -> 15.8 us  [the longest x3 11.2 us: flat(): return x.reshape(x.shape[:2] + (2, -1))]
    slice x28 -> x4, local copies, waits for them, and re-layouts: 187 us -> 6.18 us  [the longest x1 3.51 us: on_device(): own = [own[:, k * part_n:(k + 1) * part_n] for k in range(pieces)]]
    another operation x24 -> x8, local copies, waits for them, and re-layouts: 134 us -> 11.4 us  [the longest x4 5.69 us: on_device(): highs.append(from_behind(field[:, :, :, 0].reshape(plane), 'sa', -1))]
    reduce_sum x20 -> x0, other arithmetic: 74.2 us -> none  [the longest x16 39.7 us: mat_vec(): real_part = jnp.sum(mat_re * vec_re - mat_im * vec_im, axis=3)]
    while x83 -> x0, local copies, waits for them, and re-layouts: 43 us -> none
    mul x29 -> x0, local copies, waits for them, and re-layouts: 42.5 us -> none  [mat_vec(): real_part = jnp.sum(mat_re * vec_re - mat_im * vec_im, axis=3)]
    psum x1 -> x0, blocking collectives: 38.4 us -> none  [on_device(): raw_sums = lax.psum(stack_grams(current, image), 'sa')]
  transfers between devices with their start and end apart: 9 -> 20, of which waited for: 1 -> 7; matrix products, arithmetic and copies ran while one was open for 59% -> 18% of each run, Pallas kernels for 0% -> 12%
where the time goes in v1:
time: 208 us; the launch traced here: 207 us
  local copies, waits for them, and re-layouts  58.8 us (28%)
  waiting for transfers between devices  42.1 us (20%)
  starting transfers between devices  40 us (19%)
  Pallas kernels  29 us (14%)
  between operations  14.4 us (7%)
  matrix products  10.3 us (5%)
  blocking collectives  6.6 us (3%)
  other arithmetic  6.3 us (3%)
    ppermute x15, starting transfers between devices, from_behind(): lax.ppermute(x, axis, [(i, (i + by) % devices) for i in range(devices)])  31.8 us
    pallas_call x9, Pallas kernels, call(): pl.pallas_call(kernel, grid=(args[0].shape[0],), in_specs=[spec(a.shape)...  29 us
    all_gather x1, waiting for transfers between devices, on_device(): every = lax.all_gather(field, 'cfg', axis=1, tiled=True)  26.6 us
    unnamed x37, local copies, waits for them, and re-layouts  14.2 us
    reshape x3, local copies, waits for them, and re-layouts, flat(): return x.reshape(x.shape[:2] + (2, -1))  11.2 us
    ppermute x4, waiting for transfers between devices, butterfly(): x = x + lax.ppermute(x, axis, [(i, i ^ step) for i in range(devices)])  10.6 us
    dot_general x3, matrix products, dot(): return jnp.einsum('tipk,tjqk->tipjq', a, b, preferred_element_type=F32)  10.3 us
    ppermute x4, starting transfers between devices, butterfly(): x = x + lax.ppermute(x, axis, [(i, i ^ step) for i in range(devices)])  8.09 us
  transfers between devices with their start and end apart: 20, of which 7 were waited for; matrix products, arithmetic and copies ran while one was open for 18% of the time, Pallas kernels for 12%

profile of v1, /device:TPU:0, one launch (start us, length us, event | category | flops | bytes accessed | tf_op | source)
XLA Modules:
  0.0 207.5 jit_solution(11605763924912094507)
XLA Ops:
  7.2 6.6 %all_to_all.18 = f32[4,54,16,128]{3,2,1,0:T(8,128)S(1)} all-to-all(f32[4,54,16,128]{3,2,1,0:T(8,128)} %bitcast.108), channel_id=1, replica_groups=mesh['cfg'=2,'ta'=2,'sa'=8] {'ta'}, dimensions={0} | all-to-all | bytes 3538944 | tf_op jit(solution)/shard_map/all_to_all | solution.py:228
  17.0 3.0 %collective-permute-start = (f32[2,18,8,128]{3,2,1,0:T(8,128)}, f32[2,18,8,128]{3,2,1,0:T(8,128)}, u32[]{:S(2)}, u32[]{:S(2)}) collective-permute-start(f32[2,18,8,128]{3,2,1,0:T(8,128)} %slice.58), channel_id=1, source_target_pairs={{0,1},{1,2},{2,3},{3,4},{4,5},{5,6},{6,7},{7,0},{8,9},{9,10},{10,1... | collective-permute-start | bytes 442376 | tf_op jit(solution)/shard_map/ppermute | solution.py:19
  31.5 3.2 %collective-permute-start.2 = (f32[2,4,6,8,128]{4,3,2,1,0:T(8,128)}, f32[2,4,6,8,128]{4,3,2,1,0:T(8,128)}, u32[]{:S(2)}, u32[]{:S(2)}) collective-permute-start(f32[2,4,6,8,128]{4,3,2,1,0:T(8,128)} %copy.100), channel_id=1, source_target_pairs={{0,7},{1,0},{2,1},{3,2},{4,3},{5,4},{6,5},{7,6},{8,15},{9,8},{10,9... | collective-permute-start | bytes 589832 | tf_op jit(solution)/shard_map/ppermute | solution.py:19
  39.4 4.7 %collective-permute-start.8 = (f32[2,4,6,8,128]{4,3,2,1,0:T(8,128)}, f32[2,4,6,8,128]{4,3,2,1,0:T(8,128)S(1)}, u32[]{:S(2)}, u32[]{:S(2)}) collective-permute-start(f32[2,4,6,8,128]{4,3,2,1,0:T(8,128)} %copy.104), channel_id=1, source_target_pairs={{0,7},{1,0},{2,1},{3,2},{4,3},{5,4},{6,5},{7,6},{8,15},{9,8},{10,9... | collective-permute-start | bytes 589832 | tf_op jit(solution)/shard_map/ppermute | solution.py:19
  44.1 3.5 %fusion.25 = (f32[2,4,6,4,1024]{4,1,3,2,0:T(4,128)}, f32[2,4,6,4,1024]{4,1,3,2,0:T(4,128)}) fusion(f32[2,8,6,4,1024]{4,1,3,2,0:T(8,128)} %bitcast.103), kind=kLoop, calls=%fused_computation.40 | loop fusion | bytes 3145728 | tf_op jit(solution)/shard_map/slice | solution.py:219
  53.4 3.8 %shard_map.41.refs_1_ = f32[2,54,32,128]{3,2,1,0:T(8,128)S(1)} custom-call(f32[2,54,32,128]{3,2,1,0:T(8,128)S(1)} %bitcast.89, f32[2,18,8,128]{3,2,1,0:T(8,128)} %collective-permute-done.below), custom_call_target="tpu_custom_call" | custom-call | flops 1769472 | bytes 3686400 | tf_op jit(solution)/shard_map/pallas_call | solution.py:170
  57.2 4.8 %shard_map.42 = (f32[2,4,6,32,128]{4,3,2,1,0:T(8,128)S(1)}, f32[2,4,6,8,128]{4,3,2,1,0:T(8,128)}, f32[2,4,6,8,128]{4,3,2,1,0:T(8,128)}) custom-call(f32[2,54,32,128]{3,2,1,0:T(8,128)S(1)} %bitcast.90, f32[2,54,32,128]{3,2,1,0:T(8,128)S(1)} %shard_map.41.refs_1_, f32[2,4,6,32,128]{4,3,2,1,0:T(8,128)S(1)} %bitcast.98, ...), custom_call_target="tpu_custom_call" | custom-call | flops 14745600 | bytes 5898240 | tf_op jit(solution)/shard_map/pallas_call | solution.py:170
  62.9 4.7 %collective-permute-start.4 = (f32[2,4,6,8,128]{4,3,2,1,0:T(8,128)}, f32[2,4,6,8,128]{4,3,2,1,0:T(8,128)}, u32[]{:S(2)}, u32[]{:S(2)}) collective-permute-start(f32[2,4,6,8,128]{4,3,2,1,0:T(8,128)} %get-tuple-element.20), channel_id=1, source_target_pairs={{0,7},{1,0},{2,1},{3,2},{4,3},{5,4},{6,5},{7,6},{8,15},{9,8},{10,9... | collective-permute-start | bytes 589832 | tf_op jit(solution)/shard_map/ppermute | solution.py:19
  74.7 3.0 %shard_map.45 = (f32[2,4,6,32,128]{4,3,2,1,0:T(8,128)S(1)}, f32[2,4,6,8,128]{4,3,2,1,0:T(8,128)S(1)}, f32[2,4,6,8,128]{4,3,2,1,0:T(8,128)S(1)}) custom-call(f32[2,54,32,128]{3,2,1,0:T(8,128)S(1)} %bitcast.91, f32[2,54,32,128]{3,2,1,0:T(8,128)S(1)} %copy-done.5, f32[2,4,6,32,128]{4,3,2,1,0:T(8,128)S(1)} %bitcast.100, ...), custom_call_target="tpu_custom_call" | custom-call | flops 14745600 | bytes 5898240 | tf_op jit(solution)/shard_map/pallas_call | solution.py:170
  79.8 4.0 %shard_map.43 = (f32[2,4,6,32,128]{4,3,2,1,0:T(8,128)S(1)}, f32[2,4,6,8,128]{4,3,2,1,0:T(8,128)S(1)}, f32[2,4,6,8,128]{4,3,2,1,0:T(8,128)S(1)}) custom-call(f32[2,54,32,128]{3,2,1,0:T(8,128)S(1)} %bitcast.92, f32[2,54,32,128]{3,2,1,0:T(8,128)S(1)} %copy-done.5, f32[2,4,6,32,128]{4,3,2,1,0:T(8,128)S(1)} %copy-done.13, ...), custom_call_target="tpu_custom_call" | custom-call | flops 14745600 | bytes 6684672 | tf_op jit(solution)/shard_map/pallas_call | solution.py:170
  83.9 4.7 %collective-permute-start.6 = (f32[2,4,6,8,128]{4,3,2,1,0:T(8,128)S(1)}, f32[2,4,6,8,128]{4,3,2,1,0:T(8,128)S(1)}, u32[]{:S(2)}, u32[]{:S(2)}) collective-permute-start(f32[2,4,6,8,128]{4,3,2,1,0:T(8,128)S(1)} %get-tuple-element.23), channel_id=1, source_target_pairs={{0,7},{1,0},{2,1},{3,2},{4,3},{5,4},{6,5},{7,6},{8,15},{9,8},{10,9... | collective-permute-start | bytes 589832 | tf_op jit(solution)/shard_map/ppermute | solution.py:19
  88.6 4.6 %collective-permute-done.10.refs_4_ = f32[2,4,6,8,128]{4,3,2,1,0:T(8,128)S(1)} collective-permute-done((f32[2,4,6,8,128]{4,3,2,1,0:T(8,128)S(1)}, f32[2,4,6,8,128]{4,3,2,1,0:T(8,128)S(1)}, u32[]{:S(2)}, u32[]{:S(2)}) %collective-permute-start.10) | collective-permute-done | bytes 196640 | tf_op jit(solution)/shard_map/ppermute | solution.py:19
  93.1 3.0 %shard_map.46 = (f32[2,4,6,32,128]{4,3,2,1,0:T(8,128)S(1)}, f32[2,4,6,8,128]{4,3,2,1,0:T(8,128)S(1)}, f32[2,4,6,8,128]{4,3,2,1,0:T(8,128)S(1)}) custom-call(f32[2,54,32,128]{3,2,1,0:T(8,128)S(1)} %bitcast.93, f32[2,54,32,128]{3,2,1,0:T(8,128)S(1)} %copy-done.5, f32[2,4,6,32,128]{4,3,2,1,0:T(8,128)S(1)} %get-tuple-element.25.refs_2_.refs_5_, ...), custom_call_target="tpu_custom_call" | custom-call | flops 14745600 | bytes 6684672 | tf_op jit(solution)/shard_map/pallas_call | solution.py:170
  96.7 4.2 %collective-permute-start.12 = (f32[2,4,6,8,128]{4,3,2,1,0:T(8,128)S(1)}, f32[2,4,6,8,128]{4,3,2,1,0:T(8,128)S(1)}, u32[]{:S(2)}, u32[]{:S(2)}) collective-permute-start(f32[2,4,6,8,128]{4,3,2,1,0:T(8,128)S(1)} %get-tuple-element.30), channel_id=1, source_target_pairs={{0,7},{1,0},{2,1},{3,2},{4,3},{5,4},{6,5},{7,6},{8,15},{9,8},{10,9... | collective-permute-start | bytes 589832 | tf_op jit(solution)/shard_map/ppermute | solution.py:19
  100.9 3.6 %shard_map.44 = (f32[2,4,6,32,128]{4,3,2,1,0:T(8,128)S(1)}, f32[2,4,6,8,128]{4,3,2,1,0:T(8,128)}, f32[2,4,6,8,128]{4,3,2,1,0:T(8,128)S(1)}) custom-call(f32[2,54,32,128]{3,2,1,0:T(8,128)S(1)} %bitcast.94, f32[2,54,32,128]{3,2,1,0:T(8,128)S(1)} %copy-done.5, f32[2,4,6,32,128]{4,3,2,1,0:T(8,128)S(1)} %get-tuple-element.21.refs_2_, ...), custom_call_target="tpu_custom_call" | custom-call | flops 14745600 | bytes 6684672 | tf_op jit(solution)/shard_map/pallas_call | solution.py:170
  106.5 3.6 %shard_map.47 = (f32[2,4,6,32,128]{4,3,2,1,0:T(8,128)S(1)}, f32[2,4,6,8,128]{4,3,2,1,0:T(8,128)}, f32[2,4,6,8,128]{4,3,2,1,0:T(8,128)S(1)}) custom-call(f32[2,54,32,128]{3,2,1,0:T(8,128)S(1)} %bitcast.95, f32[2,54,32,128]{3,2,1,0:T(8,128)S(1)} %copy-done.5, f32[2,4,6,32,128]{4,3,2,1,0:T(8,128)S(1)} %get-tuple-element.28.refs_2_, ...), custom_call_target="tpu_custom_call" | custom-call | flops 14745600 | bytes 6684672 | tf_op jit(solution)/shard_map/pallas_call | solution.py:170
  112.0 3.0 %reshape.95 = f32[2,8,2,12288]{3,2,1,0:T(2,128)} reshape(f32[2,8,6,32,128]{4,3,2,1,0:T(8,128)} %constant_dynamic-update-slice_fusion) | data formatting | bytes 3145728 | tf_op jit(solution)/shard_map/reshape | solution.py:259
  115.1 2.8 %collective-permute-start.13 = (f32[2,4,6,8,128]{4,3,2,1,0:T(8,128)S(1)}, f32[2,4,6,8,128]{4,3,2,1,0:T(8,128)S(1)}, u32[]{:S(2)}, u32[]{:S(2)}) collective-permute-start(f32[2,4,6,8,128]{4,3,2,1,0:T(8,128)S(1)} %get-tuple-element.32), channel_id=1, source_target_pairs={{0,7},{1,0},{2,1},{3,2},{4,3},{5,4},{6,5},{7,6},{8,15},{9,8},{10,9... | collective-permute-start | bytes 589832 | tf_op jit(solution)/shard_map/ppermute | solution.py:19
  118.2 3.5 %copy_dynamic-update-slice_fusion.1 = f32[2,16,2,12288]{3,1,2,0:T(8,128)} fusion(f32[2,8,2,12288]{3,2,1,0:T(2,128)} %reshape.95), kind=kLoop, calls=%fused_computation.15 | loop fusion | bytes 3145728
  126.6 3.0 %reshape.96 = f32[2,8,2,12288]{3,2,1,0:T(2,128)} reshape(f32[2,8,6,32,128]{4,3,2,1,0:T(8,128)} %pad_maximum_fusion) | data formatting | bytes 3145728 | tf_op jit(solution)/shard_map/reshape | solution.py:259
  129.6 3.5 %copy_dynamic-update-slice_fusion = f32[2,16,2,12288]{3,1,2,0:T(8,128)} fusion(f32[2,16,2,12288]{3,1,2,0:T(8,128)} %copy_dynamic-update-slice_fusion.1, f32[2,8,2,12288]{3,2,1,0:T(2,128)} %reshape.96), kind=kLoop, calls=%fused_computation.14 | loop fusion | bytes 3145728 | tf_op jit(solution)/shard_map/concatenate | solution.py:261
  133.1 26.6 %all-gather.2.cloned.1.call-done = f32[2,16,6,32,128]{4,3,2,1,0:T(8,128)} async-done(((f32[2,8,6,32,128]{4,3,2,1,0:T(8,128)}), f32[2,16,6,32,128]{4,3,2,1,0:T(8,128)}) %all-gather.2.cloned.1.call-update) | async-done | bytes 3145744 | tf_op jit(solution)/shard_map/all_gather | solution.py:256
  159.7 5.1 %reshape.94 = f32[2,16,2,12288]{3,2,1,0:T(2,128)} reshape(f32[2,16,6,32,128]{4,3,2,1,0:T(8,128)} %all-gather.2.cloned.1.call-done) | data formatting | bytes 6291456 | tf_op jit(solution)/shard_map/reshape | solution.py:259
  164.7 5.4 %fusion.6 = f32[2,16,2,16,2]{3,1,4,2,0:T(8,128)S(1)} fusion(f32[2,16,2,12288]{3,2,1,0:T(2,128)} %reshape.94, f32[2,16,2,12288]{3,1,2,0:T(8,128)} %copy_dynamic-update-slice_fusion), kind=kOutput, calls=%fused_computation.10 | convolution fusion | flops 54263808 | bytes 6299648 | tf_op jit(solution)/shard_map/tipk,tjqk->tipjq/dot_general | solution.py:202
  170.2 2.4 %fusion.17 = f32[2,16,2,16,2]{3,1,4,2,0:T(8,128)S(1)} fusion(f32[2,16,2,12288]{3,1,2,0:T(8,128)S(1)} %copy-done.15, f32[2,16,2,12288]{3,2,1,0:T(2,128)S(1)} %copy-done.14), kind=kOutput, calls=%fused_computation.19 | convolution fusion | flops 53477376 | bytes 6299648 | tf_op jit(solution)/shard_map/tipk,tjqk->tipjq/dot_general | solution.py:202
  172.6 2.4 %fusion.13 = f32[2,16,2,16,2]{3,1,4,2,0:T(8,128)S(1)} fusion(f32[2,16,2,16,2]{3,1,4,2,0:T(8,128)S(1)} %fusion.17, f32[2,16,2,16,2]{3,1,4,2,0:T(8,128)S(1)} %fusion.6, f32[2,16,2,12288]{3,1,2,0:T(8,128)S(1)} %copy-done.15, f32[2,16,2,12288]{3,2,1,0:T(2,128)S(1)} %copy-done.14), kind=kOutput, calls=%fused_computation.18 | convolution fusion | flops 54267904 | bytes 6316032 | tf_op jit(solution)/shard_map/tipk,tjqk->tipjq/dot_general | solution.py:202
  177.3 2.8 %collective-permute-done.15 = f32[2,2,2,16,16]{4,3,0,2,1:T(8,128)S(1)} collective-permute-done((f32[2,2,2,16,16]{4,3,0,2,1:T(8,128)S(1)}, f32[2,2,2,16,16]{4,3,0,2,1:T(8,128)S(1)}, u32[]{:S(2)}, u32[]{:S(2)}) %collective-permute-start.15) | collective-permute-done | bytes 8224 | tf_op jit(solution)/shard_map/ppermute | solution.py:28
  182.0 2.8 %collective-permute-done.16 = f32[2,2,2,16,16]{4,3,0,2,1:T(8,128)S(1)} collective-permute-done((f32[2,2,2,16,16]{4,3,0,2,1:T(8,128)S(1)}, f32[2,2,2,16,16]{4,3,0,2,1:T(8,128)S(1)}, u32[]{:S(2)}, u32[]{:S(2)}) %collective-permute-start.16) | collective-permute-done | bytes 8224 | tf_op jit(solution)/shard_map/ppermute | solution.py:28
  184.8 2.5 %collective-permute-start.17 = (f32[2,2,2,16,16]{4,3,0,2,1:T(8,128)S(1)}, f32[2,2,2,16,16]{4,3,0,2,1:T(8,128)S(1)}, u32[]{:S(2)}, u32[]{:S(2)}) collective-permute-start(f32[2,2,2,16,16]{4,3,0,2,1:T(8,128)S(1)} %add.51), channel_id=1, source_target_pairs={{0,4},{1,5},{2,6},{3,7},{4,0},{5,1},{6,2},{7,3},{8,12},{9,13},{10,... | collective-permute-start | bytes 24584 | tf_op jit(solution)/shard_map/ppermute | solution.py:28
  187.2 2.8 %collective-permute-done.17 = f32[2,2,2,16,16]{4,3,0,2,1:T(8,128)S(1)} collective-permute-done((f32[2,2,2,16,16]{4,3,0,2,1:T(8,128)S(1)}, f32[2,2,2,16,16]{4,3,0,2,1:T(8,128)S(1)}, u32[]{:S(2)}, u32[]{:S(2)}) %collective-permute-start.17) | collective-permute-done | bytes 8224 | tf_op jit(solution)/shard_map/ppermute | solution.py:28
  190.0 2.5 %collective-permute-start.18 = (f32[2,2,2,16,16]{4,3,0,2,1:T(8,128)S(1)}, f32[2,2,2,16,16]{4,3,0,2,1:T(8,128)S(1)}, u32[]{:S(2)}, u32[]{:S(2)}) collective-permute-start(f32[2,2,2,16,16]{4,3,0,2,1:T(8,128)S(1)} %add.52), channel_id=1, source_target_pairs={{0,16},{16,0},{1,17},{17,1},{2,18},{18,2},{3,19},{19,3},{4,20},{20... | collective-permute-start | bytes 24584 | tf_op jit(solution)/shard_map/ppermute | solution.py:28
  196.5 4.1 %broadcast_multiply_fusion = f32[2,16,6,32,128]{4,3,2,1,0:T(8,128)} fusion(f32[2,16,6,32,128]{4,3,2,1,0:T(8,128)} %all-gather.2.cloned.1.call-done, f32[2,16]{1,0:T(2,128)S(1)} %copy.114), kind=kLoop, calls=%fused_computation.16 | loop fusion | flops 786432 | bytes 6291584 | tf_op jit(solution)/shard_map/mul | solution.py:274
  (107 shorter events, 52.8 us)
Async XLA Ops:
  7.2 12.8 %copy-start = (f32[2,16,2,3,4,1024]{5,4,3,2,1,0:T(4,128)S(1)}, f32[2,16,2,3,4,1024]{5,4,3,2,1,0:T(4,128)}, u32[]{:S(2)}) copy-start(f32[2,16,2,3,4,1024]{5,4,3,2,1,0:T(4,128)} %param.3) | copy-start | bytes 9437188
  7.2 152.5 %all-gather.2.cloned.1.call-start = ((), (), s32[]{:S(2)}) async-start(), calls=%async_computation.1 | async-start | bytes 4718592 | tf_op jit(solution)/shard_map/all_gather | solution.py:256
  17.0 34.6 %collective-permute-start = (f32[2,18,8,128]{3,2,1,0:T(8,128)}, f32[2,18,8,128]{3,2,1,0:T(8,128)}, u32[]{:S(2)}, u32[]{:S(2)}) collective-permute-start(f32[2,18,8,128]{3,2,1,0:T(8,128)} %slice.58), channel_id=1, source_target_pairs={{0,1},{1,2},{2,3},{3,4},{4,5},{5,6},{6,7},{7,0},{8,9},{9,10},{10,1... | collective-permute-start | bytes 442376 | tf_op jit(solution)/shard_map/ppermute | solution.py:19
  26.6 30.6 %collective-permute-start.1 = (f32[2,4,6,8,128]{4,3,2,1,0:T(8,128)}, f32[2,4,6,8,128]{4,3,2,1,0:T(8,128)}, u32[]{:S(2)}, u32[]{:S(2)}) collective-permute-start(f32[2,4,6,8,128]{4,3,2,1,0:T(8,128)} %copy.99), channel_id=1, source_target_pairs={{0,1},{1,2},{2,3},{3,4},{4,5},{5,6},{6,7},{7,0},{8,9},{9,10},{10,1... | collective-permute-start | bytes 589832 | tf_op jit(solution)/shard_map/ppermute | solution.py:19
  31.5 25.7 %collective-permute-start.2 = (f32[2,4,6,8,128]{4,3,2,1,0:T(8,128)}, f32[2,4,6,8,128]{4,3,2,1,0:T(8,128)}, u32[]{:S(2)}, u32[]{:S(2)}) collective-permute-start(f32[2,4,6,8,128]{4,3,2,1,0:T(8,128)} %copy.100), channel_id=1, source_target_pairs={{0,7},{1,0},{2,1},{3,2},{4,3},{5,4},{6,5},{7,6},{8,15},{9,8},{10,9... | collective-permute-start | bytes 589832 | tf_op jit(solution)/shard_map/ppermute | solution.py:19
  37.0 34.7 %collective-permute-start.7 = (f32[2,4,6,8,128]{4,3,2,1,0:T(8,128)}, f32[2,4,6,8,128]{4,3,2,1,0:T(8,128)S(1)}, u32[]{:S(2)}, u32[]{:S(2)}) collective-permute-start(f32[2,4,6,8,128]{4,3,2,1,0:T(8,128)} %copy.103), channel_id=1, source_target_pairs={{0,1},{1,2},{2,3},{3,4},{4,5},{5,6},{6,7},{7,0},{8,9},{9,10},{10,1... | collective-permute-start | bytes 589832 | tf_op jit(solution)/shard_map/ppermute | solution.py:19
  39.4 32.3 %collective-permute-start.8 = (f32[2,4,6,8,128]{4,3,2,1,0:T(8,128)}, f32[2,4,6,8,128]{4,3,2,1,0:T(8,128)S(1)}, u32[]{:S(2)}, u32[]{:S(2)}) collective-permute-start(f32[2,4,6,8,128]{4,3,2,1,0:T(8,128)} %copy.104), channel_id=1, source_target_pairs={{0,7},{1,0},{2,1},{3,2},{4,3},{5,4},{6,5},{7,6},{8,15},{9,8},{10,9... | collective-permute-start | bytes 589832 | tf_op jit(solution)/shard_map/ppermute | solution.py:19
  51.6 10.4 %copy-start.6 = (f32[2,4,6,8,4,128]{5,4,3,2,1,0:T(4,128)}, f32[2,4,6,8,4,128]{5,4,3,2,1,0:T(4,128)S(1)}, u32[]{:S(2)}) copy-start(f32[2,4,6,8,4,128]{5,4,3,2,1,0:T(4,128)S(1)} %copy.98) | copy-start | bytes 2359300
  51.6 1.8 copy-start.1
  57.2 4.9 %copy-start.4 = (f32[2,54,32,128]{3,2,1,0:T(8,128)}, f32[2,54,32,128]{3,2,1,0:T(8,128)S(1)}, u32[]{:S(2)}) copy-start(f32[2,54,32,128]{3,2,1,0:T(8,128)S(1)} %shard_map.41.refs_1_) | copy-start | bytes 5308420
  62.9 16.8 %collective-permute-start.3 = (f32[2,4,6,8,128]{4,3,2,1,0:T(8,128)}, f32[2,4,6,8,128]{4,3,2,1,0:T(8,128)}, u32[]{:S(2)}, u32[]{:S(2)}) collective-permute-start(f32[2,4,6,8,128]{4,3,2,1,0:T(8,128)} %get-tuple-element.19), channel_id=1, source_target_pairs={{0,1},{1,2},{2,3},{3,4},{4,5},{5,6},{6,7},{7,0},{8,9},{9,10},{10,1... | collective-permute-start | bytes 589832 | tf_op jit(solution)/shard_map/ppermute | solution.py:19
  62.9 16.8 %collective-permute-start.4 = (f32[2,4,6,8,128]{4,3,2,1,0:T(8,128)}, f32[2,4,6,8,128]{4,3,2,1,0:T(8,128)}, u32[]{:S(2)}, u32[]{:S(2)}) collective-permute-start(f32[2,4,6,8,128]{4,3,2,1,0:T(8,128)} %get-tuple-element.20), channel_id=1, source_target_pairs={{0,7},{1,0},{2,1},{3,2},{4,3},{5,4},{6,5},{7,6},{8,15},{9,8},{10,9... | collective-permute-start | bytes 589832 | tf_op jit(solution)/shard_map/ppermute | solution.py:19
  70.0 9.8 %copy-start.7 = (f32[2,4,6,8,4,128]{5,4,3,2,1,0:T(4,128)S(1)}, f32[2,4,6,8,4,128]{5,4,3,2,1,0:T(4,128)}, u32[]{:S(2)}) copy-start(f32[2,4,6,8,4,128]{5,4,3,2,1,0:T(4,128)} %copy-done.6) | copy-start | bytes 2359300
  70.0 9.8 %copy-start.13 = (f32[2,4,6,32,128]{4,3,2,1,0:T(8,128)S(1)}, f32[2,4,6,32,128]{4,3,2,1,0:T(8,128)}, u32[]{:S(2)}) copy-start(f32[2,4,6,32,128]{4,3,2,1,0:T(8,128)} %copy-done.12) | copy-start | bytes 2359300
  71.8 1.5 copy-start.2
  77.7 15.4 %collective-permute-start.10 = (f32[2,4,6,8,128]{4,3,2,1,0:T(8,128)S(1)}, f32[2,4,6,8,128]{4,3,2,1,0:T(8,128)S(1)}, u32[]{:S(2)}, u32[]{:S(2)}) collective-permute-start(f32[2,4,6,8,128]{4,3,2,1,0:T(8,128)S(1)} %get-tuple-element.27), channel_id=1, source_target_pairs={{0,7},{1,0},{2,1},{3,2},{4,3},{5,4},{6,5},{7,6},{8,15},{9,8},{10,9... | collective-permute-start | bytes 589832 | tf_op jit(solution)/shard_map/ppermute | solution.py:19
  77.8 15.4 %collective-permute-start.9 = (f32[2,4,6,8,128]{4,3,2,1,0:T(8,128)S(1)}, f32[2,4,6,8,128]{4,3,2,1,0:T(8,128)S(1)}, u32[]{:S(2)}, u32[]{:S(2)}) collective-permute-start(f32[2,4,6,8,128]{4,3,2,1,0:T(8,128)S(1)} %get-tuple-element.26), channel_id=1, source_target_pairs={{0,1},{1,2},{2,3},{3,4},{4,5},{5,6},{6,7},{7,0},{8,9},{9,10},{10,1... | collective-permute-start | bytes 589832 | tf_op jit(solution)/shard_map/ppermute | solution.py:19
  83.8 17.1 %collective-permute-start.5 = (f32[2,4,6,8,128]{4,3,2,1,0:T(8,128)S(1)}, f32[2,4,6,8,128]{4,3,2,1,0:T(8,128)S(1)}, u32[]{:S(2)}, u32[]{:S(2)}) collective-permute-start(f32[2,4,6,8,128]{4,3,2,1,0:T(8,128)S(1)} %get-tuple-element.22), channel_id=1, source_target_pairs={{0,1},{1,2},{2,3},{3,4},{4,5},{5,6},{6,7},{7,0},{8,9},{9,10},{10,1... | collective-permute-start | bytes 589832 | tf_op jit(solution)/shard_map/ppermute | solution.py:19
  83.9 17.1 %collective-permute-start.6 = (f32[2,4,6,8,128]{4,3,2,1,0:T(8,128)S(1)}, f32[2,4,6,8,128]{4,3,2,1,0:T(8,128)S(1)}, u32[]{:S(2)}, u32[]{:S(2)}) collective-permute-start(f32[2,4,6,8,128]{4,3,2,1,0:T(8,128)S(1)} %get-tuple-element.23), channel_id=1, source_target_pairs={{0,7},{1,0},{2,1},{3,2},{4,3},{5,4},{6,5},{7,6},{8,15},{9,8},{10,9... | collective-permute-start | bytes 589832 | tf_op jit(solution)/shard_map/ppermute | solution.py:19
  96.2 10.4 %collective-permute-start.11 = (f32[2,4,6,8,128]{4,3,2,1,0:T(8,128)S(1)}, f32[2,4,6,8,128]{4,3,2,1,0:T(8,128)S(1)}, u32[]{:S(2)}, u32[]{:S(2)}) collective-permute-start(f32[2,4,6,8,128]{4,3,2,1,0:T(8,128)S(1)} %get-tuple-element.29), channel_id=1, source_target_pairs={{0,1},{1,2},{2,3},{3,4},{4,5},{5,6},{6,7},{7,0},{8,9},{9,10},{10,1... | collective-permute-start | bytes 589832 | tf_op jit(solution)/shard_map/ppermute | solution.py:19
  96.7 9.8 %collective-permute-start.12 = (f32[2,4,6,8,128]{4,3,2,1,0:T(8,128)S(1)}, f32[2,4,6,8,128]{4,3,2,1,0:T(8,128)S(1)}, u32[]{:S(2)}, u32[]{:S(2)}) collective-permute-start(f32[2,4,6,8,128]{4,3,2,1,0:T(8,128)S(1)} %get-tuple-element.30), channel_id=1, source_target_pairs={{0,7},{1,0},{2,1},{3,2},{4,3},{5,4},{6,5},{7,6},{8,15},{9,8},{10,9... | collective-permute-start | bytes 589832 | tf_op jit(solution)/shard_map/ppermute | solution.py:19
  115.1 6.6 %copy-start.3 = (f32[2,54,2,16,128]{4,3,2,1,0:T(8,128)S(1)}, f32[2,54,2,16,128]{4,3,2,1,0:T(8,128)}, u32[]{:S(2)}) copy-start(f32[2,54,2,16,128]{4,3,2,1,0:T(8,128)} %copy.95) | copy-start | bytes 5308420
  115.1 6.6 %copy-start.9 = (f32[2,4,6,32,128]{4,3,2,1,0:T(8,128)S(1)}, f32[2,4,6,32,128]{4,3,2,1,0:T(8,128)}, u32[]{:S(2)}) copy-start(f32[2,4,6,32,128]{4,3,2,1,0:T(8,128)} %copy-done.8) | copy-start | bytes 2359300
  115.1 6.6 %collective-permute-start.13 = (f32[2,4,6,8,128]{4,3,2,1,0:T(8,128)S(1)}, f32[2,4,6,8,128]{4,3,2,1,0:T(8,128)S(1)}, u32[]{:S(2)}, u32[]{:S(2)}) collective-permute-start(f32[2,4,6,8,128]{4,3,2,1,0:T(8,128)S(1)} %get-tuple-element.32), channel_id=1, source_target_pairs={{0,7},{1,0},{2,1},{3,2},{4,3},{5,4},{6,5},{7,6},{8,15},{9,8},{10,9... | collective-permute-start | bytes 589832 | tf_op jit(solution)/shard_map/ppermute | solution.py:19
  118.0 5.7 %copy-start.11 = (f32[2,4,6,32,128]{4,3,2,1,0:T(8,128)S(1)}, f32[2,4,6,32,128]{4,3,2,1,0:T(8,128)}, u32[]{:S(2)}) copy-start(f32[2,4,6,32,128]{4,3,2,1,0:T(8,128)} %copy-done.10) | copy-start | bytes 2359300
  118.0 5.7 %collective-permute-start.14 = (f32[2,4,6,8,128]{4,3,2,1,0:T(8,128)S(1)}, f32[2,4,6,8,128]{4,3,2,1,0:T(8,128)S(1)}, u32[]{:S(2)}, u32[]{:S(2)}) collective-permute-start(f32[2,4,6,8,128]{4,3,2,1,0:T(8,128)S(1)} %get-tuple-element.33), channel_id=1, source_target_pairs={{0,7},{1,0},{2,1},{3,2},{4,3},{5,4},{6,5},{7,6},{8,15},{9,8},{10,9... | collective-permute-start | bytes 589832 | tf_op jit(solution)/shard_map/ppermute | solution.py:19
  164.7 5.4 %copy-start.14 = (f32[2,16,2,12288]{3,2,1,0:T(2,128)S(1)}, f32[2,16,2,12288]{3,2,1,0:T(2,128)}, u32[]{:S(2)}) copy-start(f32[2,16,2,12288]{3,2,1,0:T(2,128)} %reshape.94) | copy-start | bytes 9437188
  164.7 5.4 %copy-start.15 = (f32[2,16,2,12288]{3,1,2,0:T(8,128)S(1)}, f32[2,16,2,12288]{3,1,2,0:T(8,128)}, u32[]{:S(2)}) copy-start(f32[2,16,2,12288]{3,1,2,0:T(8,128)} %copy_dynamic-update-slice_fusion) | copy-start | bytes 9437188
  175.7 4.3 %collective-permute-start.15 = (f32[2,2,2,16,16]{4,3,0,2,1:T(8,128)S(1)}, f32[2,2,2,16,16]{4,3,0,2,1:T(8,128)S(1)}, u32[]{:S(2)}, u32[]{:S(2)}) collective-permute-start(f32[2,2,2,16,16]{4,3,0,2,1:T(8,128)S(1)} %dynamic_update_slice.5), channel_id=1, source_target_pairs={{0,1},{1,0},{2,3},{3,2},{4,5},{5,4},{6,7},{7,6},{8,9},{9,8},{10,11... | collective-permute-start | bytes 24584 | tf_op jit(solution)/shard_map/ppermute | solution.py:28
  180.4 4.3 %collective-permute-start.16 = (f32[2,2,2,16,16]{4,3,0,2,1:T(8,128)S(1)}, f32[2,2,2,16,16]{4,3,0,2,1:T(8,128)S(1)}, u32[]{:S(2)}, u32[]{:S(2)}) collective-permute-start(f32[2,2,2,16,16]{4,3,0,2,1:T(8,128)S(1)} %add.50), channel_id=1, source_target_pairs={{0,2},{1,3},{2,0},{3,1},{4,6},{5,7},{6,4},{7,5},{8,10},{9,11},{10,... | collective-permute-start | bytes 24584 | tf_op jit(solution)/shard_map/ppermute | solution.py:28
  184.8 5.2 %collective-permute-start.17 = (f32[2,2,2,16,16]{4,3,0,2,1:T(8,128)S(1)}, f32[2,2,2,16,16]{4,3,0,2,1:T(8,128)S(1)}, u32[]{:S(2)}, u32[]{:S(2)}) collective-permute-start(f32[2,2,2,16,16]{4,3,0,2,1:T(8,128)S(1)} %add.51), channel_id=1, source_target_pairs={{0,4},{1,5},{2,6},{3,7},{4,0},{5,1},{6,2},{7,3},{8,12},{9,13},{10,... | collective-permute-start | bytes 24584 | tf_op jit(solution)/shard_map/ppermute | solution.py:28
  190.0 4.8 %collective-permute-start.18 = (f32[2,2,2,16,16]{4,3,0,2,1:T(8,128)S(1)}, f32[2,2,2,16,16]{4,3,0,2,1:T(8,128)S(1)}, u32[]{:S(2)}, u32[]{:S(2)}) collective-permute-start(f32[2,2,2,16,16]{4,3,0,2,1:T(8,128)S(1)} %add.52), channel_id=1, source_target_pairs={{0,16},{16,0},{1,17},{17,1},{2,18},{18,2},{3,19},{19,3},{4,20},{20... | collective-permute-start | bytes 24584 | tf_op jit(solution)/shard_map/ppermute | solution.py:28
  (5 other events, 5.4 us)
Sparse Core Ops, SparseCore 0:
  115.2 44.3 all-gather.1

commit v2 on v1

--- a/solution.py
+++ b/solution.py
@@ -80,6 +80,41 @@
     return lambda start, count: ref[(*index, pl.ds(start, count), slice(None))]
 
 
+def edges_kernel(nz, pieces, place, vec, *outs):
+    own_n, total = vec.shape[1], vec.shape[3]
+    chunks, part_n = total // nz, own_n // pieces
+    for k in range(pieces):
+        top, bottom = outs[2 * k], outs[2 * k + 1]
+
+        def body(n, carry):
+            for comp in range(6):
+                top[0, n, comp] = vec[0, k * part_n + n, comp, pl.ds(nz - 1, chunks, stride=nz), :]
+                bottom[0, n, comp] = vec[0, k * part_n + n, comp, pl.ds(0, chunks, stride=nz), :]
+            return carry
+
+        lax.fori_loop(0, part_n, body, 0)
+
+
+def join_links_kernel(nz, place, mine, theirs, out, top):
+    half = mine.shape[2]
+    chunks = 2 * half // nz
+    ahead = place[1] == 0
+
+    def body(comp, carry):
+        a, b = mine[0, comp], theirs[0, comp]
+        out[0, comp, pl.ds(0, half), :] = jnp.where(ahead, a, b)
+        out[0, comp, pl.ds(half, half), :] = jnp.where(ahead, b, a)
+        return carry
+
+    def edge(comp, carry):
+        first = out.shape[1] - top.shape[1]
+        top[0, comp] = out[0, first + comp, pl.ds(nz - 1, chunks, stride=nz), :]
+        return carry
+
+    lax.fori_loop(0, out.shape[1], body, 0)
+    lax.fori_loop(0, top.shape[1], edge, 0)
+
+
 def back_links_kernel(nz, links, below, out):
     total = links.shape[2]
     comps = links.shape[1] // 3
@@ -94,6 +129,23 @@
         return carry
 
     lax.fori_loop(0, comps, body, 0)
+
+
+def scale_kernel(groups, pieces, place, inverse, *refs):
+    out = refs[-1]
+    t = pl.program_id(0)
+    part_n = refs[0].shape[1]
+    for away in range(groups):
+        source = lax.rem(place[0] + away, groups)
+        for k in range(pieces):
+            piece = refs[away * pieces + k]
+            base = (source * pieces + k) * part_n
+
+            def body(n, carry):
+                out[0, base + n] = piece[0, n] * inverse[t, base + n]
+                return carry
+
+            lax.fori_loop(0, part_n, body, 0)
 
 
 def hop(links, vec, halo, n, total, nz, tile, direction, ahead, acc):
@@ -119,7 +171,7 @@
                 acc[3 + row] = acc[3 + row] + re * part[1] - im * part[0]
 
 
-def apply_kernel(nz, first, *refs):
+def apply_kernel(nz, first, place, *refs):
     links, back, vec, low, high = refs[:5]
     prev = None if first else refs[5]
     out, top, bottom = refs[-3:]
@@ -162,20 +214,30 @@
     lax.fori_loop(0, vec.shape[1], body, 0)
 
 
-def call(kernel, args, outs, flops):
-    def spec(shape):
-        return pl.BlockSpec((1,) + tuple(shape[1:]), lambda t: (t,) + (0,) * (len(shape) - 1))
-
-    moved = 4 * sum(a.size for a in args) + 4 * sum(functools.reduce(lambda x, y: x * y, o) for o in outs)
+def call(kernel, args, outs, flops=0, place=None, blocks=(), smem=()):
+    blocks = dict(blocks)
+
+    def plain(shape):
+        return pl.BlockSpec((1,) + tuple(shape[1:]), lambda t, *_: (t,) + (0,) * (len(shape) - 1))
+
+    def spec(at, arg):
+        return pl.BlockSpec(*blocks[at]) if at in blocks else plain(arg.shape)
+
+    in_specs = [pl.BlockSpec(memory_space=pltpu.SMEM)] * len(smem) + [spec(i, a) for i, a in enumerate(args)]
+    moved = 8 * sum(functools.reduce(lambda x, y: x * y, o) for o in outs)
+    scalars = () if place is None else (place,)
     return pl.pallas_call(
         kernel,
-        grid=(args[0].shape[0],),
-        in_specs=[spec(a.shape) for a in args],
-        out_specs=[spec(o) for o in outs],
+        grid_spec=pltpu.PrefetchScalarGridSpec(
+            num_scalar_prefetch=len(scalars),
+            grid=(outs[0][0],),
+            in_specs=in_specs,
+            out_specs=[plain(o) for o in outs],
+        ),
         out_shape=[jax.ShapeDtypeStruct(o, F32) for o in outs],
         compiler_params=pltpu.CompilerParams(vmem_limit_bytes=40 * 2**20),
         cost_estimate=pl.CostEstimate(flops=flops, bytes_accessed=moved, transcendentals=0),
-    )(*args)
+    )(*scalars, *smem, *args)
 
 
 def to_rows(x):
@@ -203,6 +265,26 @@
 
     full = dot(lh, rh) + (dot(lh, rl) + dot(ll, rh))
     return full[:, :, 0, :, 0] + full[:, :, 1, :, 1], full[:, :, 0, :, 1] - full[:, :, 1, :, 0]
+
+
+def join_links(links, place, nz):
+    rows = to_rows(links.reshape((links.shape[0], 54) + links.shape[5:]))
+    count = lax.axis_size("ta")
+    if count != 2:
+        rows = lax.all_to_all(rows, "ta", split_axis=0, concat_axis=2, tiled=True)
+        return rows, rows[:, 36:, nz - 1 :: nz]
+    half = rows.shape[0] // 2
+    sent = lax.dynamic_slice_in_dim(rows, (1 - place[1]) * half, half, axis=0)
+    theirs = from_behind(sent, "ta", 1)
+    total = 2 * rows.shape[2]
+    block = ((1,) + rows.shape[1:], lambda t, place: (place[1] * half + t, 0, 0, 0))
+    return call(
+        functools.partial(join_links_kernel, nz),
+        (rows, theirs),
+        [(half, 54, total, LANES), (half, 18, total // nz, LANES)],
+        place=place,
+        blocks={0: block},
+    )
 
 
 def on_device(links, vectors):
@@ -210,70 +292,90 @@
     count_t, count_n = vectors.shape[:2]
     groups = lax.axis_size("cfg")
     me = lax.axis_index("cfg")
+    place = jnp.stack([me, lax.axis_index("ta")]).astype(jnp.int32)
     own_n = count_n // groups
     pieces = 2 if own_n % 2 == 0 else 1
     part_n = own_n // pieces
 
-    own = lax.dynamic_slice_in_dim(vectors, me * own_n, own_n, axis=1)
-    own = own.reshape(own.shape[:2] + (6,) + own.shape[4:])
-    own = [own[:, k * part_n : (k + 1) * part_n] for k in range(pieces)]
-    lows, highs = [], []
-    for field in own:
-        plane = (count_t, part_n, 6, -1, LANES)
-        lows.append(from_behind(field[:, :, :, nz - 1].reshape(plane), "sa", 1))
-        highs.append(from_behind(field[:, :, :, 0].reshape(plane), "sa", -1))
-    fields = [to_rows(field) for field in own]
-
-    rows = to_rows(links.reshape((links.shape[0], 54) + links.shape[5:]))
-    rows = lax.all_to_all(rows, "ta", split_axis=0, concat_axis=2, tiled=True)
-    below = from_behind(rows[:, 36:, nz - 1 :: nz], "sa", 1)
+    every = to_rows(vectors.reshape((count_t, count_n, 6) + vectors.shape[4:]))
+    total = every.shape[3]
+    shape = (count_t, part_n, 6, total, LANES)
+    edge = (count_t, part_n, 6, total // nz, LANES)
+    own_block = ((1, own_n) + every.shape[2:], lambda t, place: (t, place[0], 0, 0, 0))
+    edges = call(
+        functools.partial(edges_kernel, nz, pieces), (every,), [edge] * (2 * pieces), place=place, blocks={0: own_block}
+    )
+    lows = [from_behind(edges[2 * k], "sa", 1) for k in range(pieces)]
+    highs = [from_behind(edges[2 * k + 1], "sa", -1) for k in range(pieces)]
+
+    rows, top_links = join_links(links, place, nz)
+    below = from_behind(top_links, "sa", 1)
     (back,) = call(functools.partial(back_links_kernel, nz), (rows, below), [rows.shape], rows.size * 4)
 
-    work = fields[0].size // 6
-    older = [None] * pieces
+    work = count_t * part_n * total * LANES
+    fields, older = [every] * pieces, [None] * pieces
+
+    def part(k):
+        return ((1, part_n) + every.shape[2:], lambda t, place: (t, place[0] * pieces + k, 0, 0, 0))
+
     for turn in range(DEG):
         for k in range(pieces):
-            args = (rows, back, fields[k], lows[k], highs[k])
+            args, blocks = (rows, back, fields[k], lows[k], highs[k]), {}
             if turn:
                 args = args + (older[k],)
+            if turn == 0:
+                blocks[2] = part(k)
+            if turn == 1:
+                blocks[5] = part(k)
             new, top, bottom = call(
                 functools.partial(apply_kernel, nz, turn == 0),
                 args,
-                [fields[k].shape, lows[k].shape, lows[k].shape],
+                [shape, edge, edge],
                 work * 450,
+                place,
+                blocks,
             )
             older[k], fields[k] = fields[k], new
             highs[k] = from_behind(bottom, "sa", -1)
             if turn + 1 < DEG:
                 lows[k] = from_behind(top, "sa", 1)
 
+    held = [fields] + [[from_behind(f, "cfg", -away) for f in fields] for away in range(1, groups)]
+    sums = jnp.concatenate([jnp.sum(f * f, axis=(2, 3, 4)) for f in fields], axis=1)
+    sums = lax.dynamic_update_slice_in_dim(jnp.zeros((count_t, count_n), F32), sums, me * own_n, axis=1)
+    inverse = lax.rsqrt(butterfly(butterfly(sums, "sa"), "cfg"))
+
     images = [
-        call(functools.partial(ahead_kernel, nz), (rows, fields[k], highs[k]), [fields[k].shape], work * 220)[0]
+        call(functools.partial(ahead_kernel, nz), (rows, fields[k], highs[k]), [shape], work * 220)[0]
         for k in range(pieces)
     ]
-    field = jnp.concatenate(fields, axis=1)
-    image = jnp.concatenate(images, axis=1)
-    every = lax.all_gather(field, "cfg", axis=1, tiled=True)
 
     def flat(x):
         return x.reshape(x.shape[:2] + (2, -1))
 
-    both = jnp.concatenate([flat(field), flat(image)], axis=1)
-    re, im = raw_gram(flat(every), both)
-    raw = jnp.stack([re, im], axis=1).reshape(count_t, 2, count_n, 2, own_n)
-    raw = jnp.moveaxis(raw, 3, 1)
-    wide = jnp.zeros((count_t, 2, 2, count_n, count_n), F32)
-    raw = lax.dynamic_update_slice_in_dim(wide, raw, me * own_n, axis=4)
+    both = jnp.concatenate([flat(x) for x in fields + images], axis=1)
+    raw = jnp.zeros((count_t, 2, 2, count_n, count_n), F32)
+    for away in range(groups):
+        source = lax.rem(me + away, groups)
+        for k in range(pieces):
+            re, im = raw_gram(flat(held[away][k]), both)
+            block = jnp.stack([re, im], axis=1).reshape(count_t, 2, part_n, 2, own_n)
+            block = jnp.moveaxis(block, 3, 1)
+            raw = lax.dynamic_update_slice(raw, block, (0, 0, 0, source * own_n + k * part_n, me * own_n))
     raw = butterfly(butterfly(raw, "sa"), "cfg")
     over, ahead = raw[:, 0], raw[:, 1]
     turned = jnp.swapaxes(ahead, 2, 3)
     lap = 6.0 * over - jnp.stack([ahead[:, 0] + turned[:, 0], ahead[:, 1] - turned[:, 1]], axis=1)
-    inverse = lax.rsqrt(jnp.diagonal(over[:, 0], axis1=1, axis2=2))
     grams = jnp.stack([over, lap], axis=1)
     grams = grams * inverse[:, None, None, :, None] * inverse[:, None, None, None, :]
-    filtered = every * inverse[:, :, None, None, None]
-    filtered = from_rows(filtered, nz).reshape(vectors.shape)
-    return (filtered, grams)
+    (filtered,) = call(
+        functools.partial(scale_kernel, groups, pieces),
+        [piece for source in held for piece in source],
+        [every.shape],
+        place=place,
+        smem=(inverse,),
+    )
+    return (from_rows(filtered, nz).reshape(vectors.shape), grams)
 
 
 def solution(mesh):

time: 208 us -> 182 us (0.88)
  local copies, waits for them, and re-layouts: 58.8 us -> 29.7 us
  matrix products: 10.3 us -> 29.5 us
  waiting for transfers between devices: 42.1 us -> 26.6 us
  starting transfers between devices: 40 us -> 53.8 us
  between operations: 14.4 us -> 1.13 us
  Pallas kernels: 29 us -> 36.7 us
  blocking collectives: 6.6 us -> 0 us
  other arithmetic: 6.3 us -> 3.59 us
    all_gather x1 -> x0, waiting for transfers between devices: 26.6 us -> none  [on_device(): every = lax.all_gather(field, 'cfg', axis=1, tiled=True)]
    dot_general x3 -> x12, matrix products: 10.3 us -> 29.5 us  [dot(): return jnp.einsum('tipk,tjqk->tipjq', a, b, preferred_element_type=F32)]
    another operation x8 -> x0, local copies, waits for them, and re-layouts: 11.4 us -> none  [the longest x4 5.69 us: on_device(): highs.append(from_behind(field[:, :, :, 0].reshape(plane), 'sa', -1))]
    ppermute x15 -> x18, waiting for transfers between devices: 4.95 us -> 13.9 us  [from_behind(): lax.ppermute(x, axis, [(i, (i + by) % devices) for i in range(devices)])]
    pallas_call x9 -> x12, Pallas kernels: 29 us -> 36.7 us  [call(): pl.pallas_call(kernel, grid_spec=pltpu.PrefetchScalarGridSpec(num_scalar_...]
    reshape x3 -> x10, local copies, waits for them, and re-layouts: 11.2 us -> 18.7 us  [flat(): return x.reshape(x.shape[:2] + (2, -1))]
    unnamed x37 -> x36, local copies, waits for them, and re-layouts: 14.2 us -> 6.62 us
    ppermute x4 -> x8, starting transfers between devices: 8.09 us -> 15.5 us  [butterfly(): x = x + lax.ppermute(x, axis, [(i, i ^ step) for i in range(devices)])]
  transfers between devices with their start and end apart: 20 -> 26, of which waited for: 7 -> 9; matrix products, arithmetic and copies ran while one was open for 18% -> 24% of each run, Pallas kernels for 12% -> 20%
where the time goes in v2:
time: 182 us; the launch traced here: 181 us
  starting transfers between devices  53.8 us (30%)
  Pallas kernels  36.7 us (20%)
  local copies, waits for them, and re-layouts  29.7 us (16%)
  matrix products  29.5 us (16%)
  waiting for transfers between devices  26.6 us (15%)
  other arithmetic  3.59 us (2%)
    ppermute x18, starting transfers between devices, from_behind(): lax.ppermute(x, axis, [(i, (i + by) % devices) for i in range(devices)])  38.4 us
    pallas_call x12, Pallas kernels, call(): pl.pallas_call(kernel, grid_spec=pltpu.PrefetchScalarGridSpec(num_scalar_...  36.7 us
    dot_general x12, matrix products, dot(): return jnp.einsum('tipk,tjqk->tipjq', a, b, preferred_element_type=F32)  29.5 us
    reshape x10, local copies, waits for them, and re-layouts, flat(): return x.reshape(x.shape[:2] + (2, -1))  18.7 us
    ppermute x8, starting transfers between devices, butterfly(): x = x + lax.ppermute(x, axis, [(i, i ^ step) for i in range(devices)])  15.5 us
    ppermute x18, waiting for transfers between devices, from_behind(): lax.ppermute(x, axis, [(i, (i + by) % devices) for i in range(devices)])  13.9 us
    ppermute x8, waiting for transfers between devices, butterfly(): x = x + lax.ppermute(x, axis, [(i, i ^ step) for i in range(devices)])  12.7 us
    unnamed x36, local copies, waits for them, and re-layouts  6.62 us
  transfers between devices with their start and end apart: 26, of which 9 were waited for; matrix products, arithmetic and copies ran while one was open for 24% of the time, Pallas kernels for 20%

profile of v2, /device:TPU:0, one launch (start us, length us, event | category | flops | bytes accessed | tf_op | source)
XLA Modules:
  0.0 181.1 jit_solution(7661698806470368853)
XLA Ops:
  5.0 2.6 %collective-permute-start.2 = (f32[2,4,6,8,128]{4,3,2,1,0:T(8,128)S(1)}, f32[2,4,6,8,128]{4,3,2,1,0:T(8,128)S(1)}, u32[]{:S(2)}, u32[]{:S(2)}) collective-permute-start(f32[2,4,6,8,128]{4,3,2,1,0:T(8,128)S(1)} %get-tuple-element.26), channel_id=1, source_target_pairs={{0,1},{1,2},{2,3},{3,4},{4,5},{5,6},{6,7},{7,0},{8,9},{9,10},{10,1... | collective-permute-start | bytes 589832 | tf_op jit(solution)/shard_map/ppermute | solution.py:19
  7.6 3.1 %collective-permute-start.3 = (f32[2,4,6,8,128]{4,3,2,1,0:T(8,128)S(1)}, f32[2,4,6,8,128]{4,3,2,1,0:T(8,128)S(1)}, u32[]{:S(2)}, u32[]{:S(2)}) collective-permute-start(f32[2,4,6,8,128]{4,3,2,1,0:T(8,128)S(1)} %get-tuple-element.27), channel_id=1, source_target_pairs={{0,7},{1,0},{2,1},{3,2},{4,3},{5,4},{6,5},{7,6},{8,15},{9,8},{10,9... | collective-permute-start | bytes 589832 | tf_op jit(solution)/shard_map/ppermute | solution.py:19
  10.7 4.7 %collective-permute-start.9 = (f32[2,4,6,8,128]{4,3,2,1,0:T(8,128)S(1)}, f32[2,4,6,8,128]{4,3,2,1,0:T(8,128)S(1)}, u32[]{:S(2)}, u32[]{:S(2)}) collective-permute-start(f32[2,4,6,8,128]{4,3,2,1,0:T(8,128)S(1)} %get-tuple-element.36), channel_id=1, source_target_pairs={{0,7},{1,0},{2,1},{3,2},{4,3},{5,4},{6,5},{7,6},{8,15},{9,8},{10,9... | collective-permute-start | bytes 589832 | tf_op jit(solution)/shard_map/ppermute | solution.py:19
  19.2 9.0 %collective-permute-done.1.below = f32[2,18,8,128]{3,2,1,0:T(8,128)S(1)} collective-permute-done((f32[2,18,8,128]{3,2,1,0:T(8,128)S(1)}, f32[2,18,8,128]{3,2,1,0:T(8,128)S(1)}, u32[]{:S(2)}, u32[]{:S(2)}) %collective-permute-start.1) | collective-permute-done | bytes 147488 | tf_op jit(solution)/shard_map/ppermute | solution.py:19
  28.3 2.9 %shard_map.42.refs_1_ = f32[2,54,32,128]{3,2,1,0:T(8,128)S(1)} custom-call(f32[2,54,32,128]{3,2,1,0:T(8,128)S(1)} %get-tuple-element.24.links.refs_0_, f32[2,18,8,128]{3,2,1,0:T(8,128)S(1)} %collective-permute-done.1.below), custom_call_target="tpu_custom_call" | custom-call | flops 1769472 | bytes 3538944 | tf_op jit(solution)/shard_map/pallas_call | solution.py:229
  31.2 3.7 %shard_map.44 = (f32[2,4,6,32,128]{4,3,2,1,0:T(8,128)S(1)}, f32[2,4,6,8,128]{4,3,2,1,0:T(8,128)S(1)}, f32[2,4,6,8,128]{4,3,2,1,0:T(8,128)S(1)}) custom-call(s32[2]{0:T(128)S(1)} %pad_add_fusion.place, f32[2,54,32,128]{3,2,1,0:T(8,128)S(1)} %get-tuple-element.24.links.refs_0_, f32[2,54,32,128]{3,2,1,0:T(8,128)S(1)} %shard_map.42.refs_1_, ...), custom_call_target="tpu_custom_call" | custom-call | flops 14745600 | bytes 2359296 | tf_op jit(solution)/shard_map/pallas_call | solution.py:229
  34.9 2.5 %collective-permute-start.4 = (f32[2,4,6,8,128]{4,3,2,1,0:T(8,128)S(1)}, f32[2,4,6,8,128]{4,3,2,1,0:T(8,128)S(1)}, u32[]{:S(2)}, u32[]{:S(2)}) collective-permute-start(f32[2,4,6,8,128]{4,3,2,1,0:T(8,128)S(1)} %get-tuple-element.29), channel_id=1, source_target_pairs={{0,1},{1,2},{2,3},{3,4},{4,5},{5,6},{6,7},{7,0},{8,9},{9,10},{10,1... | collective-permute-start | bytes 589832 | tf_op jit(solution)/shard_map/ppermute | solution.py:19
  37.4 3.1 %collective-permute-start.5 = (f32[2,4,6,8,128]{4,3,2,1,0:T(8,128)S(1)}, f32[2,4,6,8,128]{4,3,2,1,0:T(8,128)S(1)}, u32[]{:S(2)}, u32[]{:S(2)}) collective-permute-start(f32[2,4,6,8,128]{4,3,2,1,0:T(8,128)S(1)} %get-tuple-element.30), channel_id=1, source_target_pairs={{0,7},{1,0},{2,1},{3,2},{4,3},{5,4},{6,5},{7,6},{8,15},{9,8},{10,9... | collective-permute-start | bytes 589832 | tf_op jit(solution)/shard_map/ppermute | solution.py:19
  40.5 3.7 %shard_map.47 = (f32[2,4,6,32,128]{4,3,2,1,0:T(8,128)S(1)}, f32[2,4,6,8,128]{4,3,2,1,0:T(8,128)S(1)}, f32[2,4,6,8,128]{4,3,2,1,0:T(8,128)S(1)}) custom-call(s32[2]{0:T(128)S(1)} %pad_add_fusion.place, f32[2,54,32,128]{3,2,1,0:T(8,128)S(1)} %get-tuple-element.24.links.refs_0_, f32[2,54,32,128]{3,2,1,0:T(8,128)S(1)} %shard_map.42.refs_1_, ...), custom_call_target="tpu_custom_call" | custom-call | flops 14745600 | bytes 2359296 | tf_op jit(solution)/shard_map/pallas_call | solution.py:229
  44.2 4.7 %collective-permute-start.11 = (f32[2,4,6,8,128]{4,3,2,1,0:T(8,128)S(1)}, f32[2,4,6,8,128]{4,3,2,1,0:T(8,128)S(1)}, u32[]{:S(2)}, u32[]{:S(2)}) collective-permute-start(f32[2,4,6,8,128]{4,3,2,1,0:T(8,128)S(1)} %get-tuple-element.39), channel_id=1, source_target_pairs={{0,7},{1,0},{2,1},{3,2},{4,3},{5,4},{6,5},{7,6},{8,15},{9,8},{10,9... | collective-permute-start | bytes 589832 | tf_op jit(solution)/shard_map/ppermute | solution.py:19
  53.5 3.7 %shard_map.45 = (f32[2,4,6,32,128]{4,3,2,1,0:T(8,128)S(1)}, f32[2,4,6,8,128]{4,3,2,1,0:T(8,128)S(1)}, f32[2,4,6,8,128]{4,3,2,1,0:T(8,128)S(1)}) custom-call(s32[2]{0:T(128)S(1)} %pad_add_fusion.place, f32[2,54,32,128]{3,2,1,0:T(8,128)S(1)} %get-tuple-element.24.links.refs_0_, f32[2,54,32,128]{3,2,1,0:T(8,128)S(1)} %shard_map.42.refs_1_, ...), custom_call_target="tpu_custom_call" | custom-call | flops 14745600 | bytes 2359296 | tf_op jit(solution)/shard_map/pallas_call | solution.py:229
  57.4 4.6 %collective-permute-start.7 = (f32[2,4,6,8,128]{4,3,2,1,0:T(8,128)S(1)}, f32[2,4,6,8,128]{4,3,2,1,0:T(8,128)S(1)}, u32[]{:S(2)}, u32[]{:S(2)}) collective-permute-start(f32[2,4,6,8,128]{4,3,2,1,0:T(8,128)S(1)} %get-tuple-element.33), channel_id=1, source_target_pairs={{0,7},{1,0},{2,1},{3,2},{4,3},{5,4},{6,5},{7,6},{8,15},{9,8},{10,9... | collective-permute-start | bytes 589832 | tf_op jit(solution)/shard_map/ppermute | solution.py:19
  62.0 3.7 %shard_map.48 = (f32[2,4,6,32,128]{4,3,2,1,0:T(8,128)S(1)}, f32[2,4,6,8,128]{4,3,2,1,0:T(8,128)S(1)}, f32[2,4,6,8,128]{4,3,2,1,0:T(8,128)S(1)}) custom-call(s32[2]{0:T(128)S(1)} %pad_add_fusion.place, f32[2,54,32,128]{3,2,1,0:T(8,128)S(1)} %get-tuple-element.24.links.refs_0_, f32[2,54,32,128]{3,2,1,0:T(8,128)S(1)} %shard_map.42.refs_1_, ...), custom_call_target="tpu_custom_call" | custom-call | flops 14745600 | bytes 2359296 | tf_op jit(solution)/shard_map/pallas_call | solution.py:229
  65.8 4.7 %collective-permute-start.13 = (f32[2,4,6,8,128]{4,3,2,1,0:T(8,128)S(1)}, f32[2,4,6,8,128]{4,3,2,1,0:T(8,128)S(1)}, u32[]{:S(2)}, u32[]{:S(2)}) collective-permute-start(f32[2,4,6,8,128]{4,3,2,1,0:T(8,128)S(1)} %get-tuple-element.42), channel_id=1, source_target_pairs={{0,7},{1,0},{2,1},{3,2},{4,3},{5,4},{6,5},{7,6},{8,15},{9,8},{10,9... | collective-permute-start | bytes 589832 | tf_op jit(solution)/shard_map/ppermute | solution.py:19
  70.9 4.4 %shard_map.46 = (f32[2,4,6,32,128]{4,3,2,1,0:T(8,128)S(1)}, f32[2,4,6,8,128]{4,3,2,1,0:T(8,128)}, f32[2,4,6,8,128]{4,3,2,1,0:T(8,128)}) custom-call(s32[2]{0:T(128)S(1)} %pad_add_fusion.place, f32[2,54,32,128]{3,2,1,0:T(8,128)S(1)} %get-tuple-element.24.links.refs_0_, f32[2,54,32,128]{3,2,1,0:T(8,128)S(1)} %shard_map.42.refs_1_, ...), custom_call_target="tpu_custom_call" | custom-call | flops 14745600 | bytes 2359296 | tf_op jit(solution)/shard_map/pallas_call | solution.py:229
  75.3 2.6 %collective-permute-start.20 = (f32[2,4,6,8,128]{4,3,2,1,0:T(8,128)}, f32[2,4,6,8,128]{4,3,2,1,0:T(8,128)S(1)}, u32[]{:S(2)}, u32[]{:S(2)}) collective-permute-start(f32[2,4,6,8,128]{4,3,2,1,0:T(8,128)} %get-tuple-element.44), channel_id=1, source_target_pairs={{0,7},{1,0},{2,1},{3,2},{4,3},{5,4},{6,5},{7,6},{8,15},{9,8},{10,9... | collective-permute-start | bytes 589832 | tf_op jit(solution)/shard_map/ppermute | solution.py:19
  77.8 4.4 %shard_map.49 = (f32[2,4,6,32,128]{4,3,2,1,0:T(8,128)S(1)}, f32[2,4,6,8,128]{4,3,2,1,0:T(8,128)}, f32[2,4,6,8,128]{4,3,2,1,0:T(8,128)}) custom-call(s32[2]{0:T(128)S(1)} %pad_add_fusion.place, f32[2,54,32,128]{3,2,1,0:T(8,128)S(1)} %get-tuple-element.24.links.refs_0_, f32[2,54,32,128]{3,2,1,0:T(8,128)S(1)} %shard_map.42.refs_1_, ...), custom_call_target="tpu_custom_call" | custom-call | flops 14745600 | bytes 2359296 | tf_op jit(solution)/shard_map/pallas_call | solution.py:229
  82.2 2.8 %collective-permute-start.21 = (f32[2,4,6,8,128]{4,3,2,1,0:T(8,128)}, f32[2,4,6,8,128]{4,3,2,1,0:T(8,128)}, u32[]{:S(2)}, u32[]{:S(2)}) collective-permute-start(f32[2,4,6,8,128]{4,3,2,1,0:T(8,128)} %get-tuple-element.45), channel_id=1, source_target_pairs={{0,7},{1,0},{2,1},{3,2},{4,3},{5,4},{6,5},{7,6},{8,15},{9,8},{10,9... | collective-permute-start | bytes 589832 | tf_op jit(solution)/shard_map/ppermute | solution.py:19
  89.8 2.5 %copy.7 = f32[2,4,2,12288]{3,1,2,0:T(4,128)} copy(f32[2,4,2,12288]{3,2,1,0:T(2,128)} %reshape.212) | data formatting | bytes 1572864 | tf_op jit(solution)/shard_map/reshape | solution.py:354
  96.6 2.5 %reshape.214 = f32[2,4,2,12288]{3,2,1,0:T(2,128)} reshape(f32[2,4,6,32,128]{4,3,2,1,0:T(8,128)} %copy-done.4) | data formatting | bytes 1572864 | tf_op jit(solution)/shard_map/reshape | solution.py:354
  99.1 2.5 %copy.10 = f32[2,4,2,12288]{3,1,2,0:T(4,128)} copy(f32[2,4,2,12288]{3,2,1,0:T(2,128)} %reshape.214) | data formatting | bytes 1572864 | tf_op jit(solution)/shard_map/reshape | solution.py:354
  101.6 2.5 %shard_map.52 = f32[2,4,6,32,128]{4,3,2,1,0:T(8,128)S(1)} custom-call(f32[2,54,32,128]{3,2,1,0:T(8,128)S(1)} %get-tuple-element.24.links.refs_0_, f32[2,4,6,32,128]{4,3,2,1,0:T(8,128)S(1)} %get-tuple-element.43.refs_1_.vec, f32[2,4,6,8,128]{4,3,2,1,0:T(8,128)} %collective-permute-done.21.high), custom_call_target="tpu_custom_call" | custom-call | flops 7208960 | bytes 1572864 | tf_op jit(solution)/shard_map/pallas_call | solution.py:229
  119.0 3.8 %fusion.10 = f32[2,4,2,16,2]{3,1,4,2,0:T(4,128)S(1)} fusion(f32[2,4,2,16,2]{3,1,4,2,0:T(4,128)S(1)} %fusion.36, bf16[2,16,2,12288]{3,1,2,0:T(8,128)(2,1)} %copy-done.7, f32[2,4,2,12288]{3,2,1,0:T(2,128)} %reshape.212), kind=kOutput, calls=%fused_computation.13 | convolution fusion | flops 12976640 | bytes 2363392 | tf_op jit(solution)/shard_map/tipk,tjqk->tipjq/dot_general | solution.py:264
  126.4 2.5 %reshape.217 = f32[2,4,2,12288]{3,2,1,0:T(2,128)} reshape(f32[2,4,6,32,128]{4,3,2,1,0:T(8,128)} %collective-permute-done.19.refs_3_) | data formatting | bytes 1572864 | tf_op jit(solution)/shard_map/reshape | solution.py:354
  128.9 3.4 %fusion.27 = f32[2,4,2,16,2]{3,1,4,2,0:T(4,128)S(1)} fusion(bf16[2,16,2,12288,1]{3,1,2,4,0:T(8,128)(2,1)S(1)} %get-tuple-element.47, f32[2,4,2,12288]{3,2,1,0:T(2,128)} %reshape.217), kind=kOutput, calls=%fused_computation.36 | convolution fusion | flops 13172736 | bytes 2361344 | tf_op jit(solution)/shard_map/tipk,tjqk->tipjq/dot_general | solution.py:264
  136.7 2.5 %reshape.216 = f32[2,4,2,12288]{3,2,1,0:T(2,128)} reshape(f32[2,4,6,32,128]{4,3,2,1,0:T(8,128)} %collective-permute-done.18.refs_2_) | data formatting | bytes 1572864 | tf_op jit(solution)/shard_map/reshape | solution.py:354
  139.1 3.4 %fusion.30 = f32[2,4,2,16,2]{3,1,4,2,0:T(4,128)S(1)} fusion(bf16[2,16,2,12288,1]{3,1,2,4,0:T(8,128)(2,1)S(1)} %get-tuple-element.47, f32[2,4,2,12288]{3,2,1,0:T(2,128)} %reshape.216), kind=kOutput, calls=%fused_computation.38 | convolution fusion | flops 13172736 | bytes 2361344 | tf_op jit(solution)/shard_map/tipk,tjqk->tipjq/dot_general | solution.py:264
  148.1 4.1 %collective-permute-done.22 = f32[2,2,2,16,16]{4,3,0,2,1:T(8,128)S(1)} collective-permute-done((f32[2,2,2,16,16]{4,3,0,2,1:T(8,128)S(1)}, f32[2,2,2,16,16]{4,3,0,2,1:T(8,128)S(1)}, u32[]{:S(2)}, u32[]{:S(2)}) %collective-permute-start.22) | collective-permute-done | bytes 8224 | tf_op jit(solution)/shard_map/ppermute | solution.py:28
  153.1 3.5 %collective-permute-done.23 = f32[2,2,2,16,16]{4,3,0,2,1:T(8,128)S(1)} collective-permute-done((f32[2,2,2,16,16]{4,3,0,2,1:T(8,128)S(1)}, f32[2,2,2,16,16]{4,3,0,2,1:T(8,128)S(1)}, u32[]{:S(2)}, u32[]{:S(2)}) %collective-permute-start.23) | collective-permute-done | bytes 8224 | tf_op jit(solution)/shard_map/ppermute | solution.py:28
  160.5 2.9 %collective-permute-start.16 = (f32[2,16]{1,0:T(2,128)S(1)}, f32[2,16]{1,0:T(2,128)S(1)}, u32[]{:S(2)}, u32[]{:S(2)}) collective-permute-start(f32[2,16]{1,0:T(2,128)S(1)} %add.147), channel_id=1, source_target_pairs={{0,4},{1,5},{2,6},{3,7},{4,0},{5,1},{6,2},{7,3},{8,12},{9,13},{10,... | collective-permute-start | bytes 392 | tf_op jit(solution)/shard_map/ppermute | solution.py:28
  165.0 10.2 %collective-permute-start.17 = (f32[2,16]{1,0:T(2,128)S(1)}, f32[2,16]{1,0:T(2,128)S(1)}, u32[]{:S(2)}, u32[]{:S(2)}) collective-permute-start(f32[2,16]{1,0:T(2,128)S(1)} %add.148), channel_id=1, source_target_pairs={{0,16},{16,0},{1,17},{17,1},{2,18},{18,2},{3,19},{19,3},{4,20},{20... | collective-permute-start | bytes 392 | tf_op jit(solution)/shard_map/ppermute | solution.py:28
  176.7 3.6 %shard_map.50 = f32[2,16,6,32,128]{4,3,2,1,0:T(8,128)} custom-call(s32[2]{0:T(128)S(1)} %pad_add_fusion.place, f32[2,16]{1,0:T(2,128)S(1)} %add_rsqrt_fusion.inverse, f32[2,4,6,32,128]{4,3,2,1,0:T(8,128)S(1)} %get-tuple-element.34.refs_0_.vec, f32[2,4,6,32,128]{4,3,2,1,0:T(8,128)S(1)} %get-tuple-element.43.refs_1_.vec, ...), custom_call_target="tpu_custom_call" | custom-call | bytes 6291456 | tf_op jit(solution)/shard_map/pallas_call | solution.py:229
  (137 shorter events, 59.3 us)
Async XLA Ops:
  1.9 13.6 %collective-permute-start = (f32[2,54,16,128]{3,2,1,0:T(8,128)S(1)}, f32[2,54,16,128]{3,2,1,0:T(8,128)S(1)}, u32[]{:S(2)}, u32[]{:S(2)}) collective-permute-start(f32[2,54,16,128]{3,2,1,0:T(8,128)S(1)} %constant_dynamic-slice_fusion), channel_id=1, source_target_pairs={{0,8},{8,0},{1,9},{9,1},{2,10},{10,2},{3,11},{11,3},{4,12},{12,4},... | collective-permute-start | bytes 2654216 | tf_op jit(solution)/shard_map/ppermute | solution.py:19
  4.4 12.0 %copy-start.2 = (f32[4,3,2,3,3,4,512]{6,5,4,3,2,1,0:T(4,128)S(1)}, f32[4,3,2,3,3,4,512]{6,5,4,3,2,1,0:T(4,128)}, u32[]{:S(2)}) copy-start(f32[4,3,2,3,3,4,512]{6,5,4,3,2,1,0:T(4,128)} %param.2) | copy-start | bytes 5308420
  5.0 26.1 %collective-permute-start.2 = (f32[2,4,6,8,128]{4,3,2,1,0:T(8,128)S(1)}, f32[2,4,6,8,128]{4,3,2,1,0:T(8,128)S(1)}, u32[]{:S(2)}, u32[]{:S(2)}) collective-permute-start(f32[2,4,6,8,128]{4,3,2,1,0:T(8,128)S(1)} %get-tuple-element.26), channel_id=1, source_target_pairs={{0,1},{1,2},{2,3},{3,4},{4,5},{5,6},{6,7},{7,0},{8,9},{9,10},{10,1... | collective-permute-start | bytes 589832 | tf_op jit(solution)/shard_map/ppermute | solution.py:19
  7.6 23.5 %collective-permute-start.3 = (f32[2,4,6,8,128]{4,3,2,1,0:T(8,128)S(1)}, f32[2,4,6,8,128]{4,3,2,1,0:T(8,128)S(1)}, u32[]{:S(2)}, u32[]{:S(2)}) collective-permute-start(f32[2,4,6,8,128]{4,3,2,1,0:T(8,128)S(1)} %get-tuple-element.27), channel_id=1, source_target_pairs={{0,7},{1,0},{2,1},{3,2},{4,3},{5,4},{6,5},{7,6},{8,15},{9,8},{10,9... | collective-permute-start | bytes 589832 | tf_op jit(solution)/shard_map/ppermute | solution.py:19
  10.7 29.8 %collective-permute-start.8 = (f32[2,4,6,8,128]{4,3,2,1,0:T(8,128)S(1)}, f32[2,4,6,8,128]{4,3,2,1,0:T(8,128)S(1)}, u32[]{:S(2)}, u32[]{:S(2)}) collective-permute-start(f32[2,4,6,8,128]{4,3,2,1,0:T(8,128)S(1)} %get-tuple-element.35), channel_id=1, source_target_pairs={{0,1},{1,2},{2,3},{3,4},{4,5},{5,6},{6,7},{7,0},{8,9},{9,10},{10,1... | collective-permute-start | bytes 589832 | tf_op jit(solution)/shard_map/ppermute | solution.py:19
  10.7 29.8 %collective-permute-start.9 = (f32[2,4,6,8,128]{4,3,2,1,0:T(8,128)S(1)}, f32[2,4,6,8,128]{4,3,2,1,0:T(8,128)S(1)}, u32[]{:S(2)}, u32[]{:S(2)}) collective-permute-start(f32[2,4,6,8,128]{4,3,2,1,0:T(8,128)S(1)} %get-tuple-element.36), channel_id=1, source_target_pairs={{0,7},{1,0},{2,1},{3,2},{4,3},{5,4},{6,5},{7,6},{8,15},{9,8},{10,9... | collective-permute-start | bytes 589832 | tf_op jit(solution)/shard_map/ppermute | solution.py:19
  19.2 9.1 %collective-permute-start.1 = (f32[2,18,8,128]{3,2,1,0:T(8,128)S(1)}, f32[2,18,8,128]{3,2,1,0:T(8,128)S(1)}, u32[]{:S(2)}, u32[]{:S(2)}) collective-permute-start(f32[2,18,8,128]{3,2,1,0:T(8,128)S(1)} %get-tuple-element.25), channel_id=1, source_target_pairs={{0,1},{1,2},{2,3},{3,4},{4,5},{5,6},{6,7},{7,0},{8,9},{9,10},{10,1... | collective-permute-start | bytes 442376 | tf_op jit(solution)/shard_map/ppermute | solution.py:19
  34.9 16.3 %collective-permute-start.4 = (f32[2,4,6,8,128]{4,3,2,1,0:T(8,128)S(1)}, f32[2,4,6,8,128]{4,3,2,1,0:T(8,128)S(1)}, u32[]{:S(2)}, u32[]{:S(2)}) collective-permute-start(f32[2,4,6,8,128]{4,3,2,1,0:T(8,128)S(1)} %get-tuple-element.29), channel_id=1, source_target_pairs={{0,1},{1,2},{2,3},{3,4},{4,5},{5,6},{6,7},{7,0},{8,9},{9,10},{10,1... | collective-permute-start | bytes 589832 | tf_op jit(solution)/shard_map/ppermute | solution.py:19
  37.4 16.1 %collective-permute-start.5 = (f32[2,4,6,8,128]{4,3,2,1,0:T(8,128)S(1)}, f32[2,4,6,8,128]{4,3,2,1,0:T(8,128)S(1)}, u32[]{:S(2)}, u32[]{:S(2)}) collective-permute-start(f32[2,4,6,8,128]{4,3,2,1,0:T(8,128)S(1)} %get-tuple-element.30), channel_id=1, source_target_pairs={{0,7},{1,0},{2,1},{3,2},{4,3},{5,4},{6,5},{7,6},{8,15},{9,8},{10,9... | collective-permute-start | bytes 589832 | tf_op jit(solution)/shard_map/ppermute | solution.py:19
  44.2 17.8 %collective-permute-start.10 = (f32[2,4,6,8,128]{4,3,2,1,0:T(8,128)S(1)}, f32[2,4,6,8,128]{4,3,2,1,0:T(8,128)S(1)}, u32[]{:S(2)}, u32[]{:S(2)}) collective-permute-start(f32[2,4,6,8,128]{4,3,2,1,0:T(8,128)S(1)} %get-tuple-element.38), channel_id=1, source_target_pairs={{0,1},{1,2},{2,3},{3,4},{4,5},{5,6},{6,7},{7,0},{8,9},{9,10},{10,1... | collective-permute-start | bytes 589832 | tf_op jit(solution)/shard_map/ppermute | solution.py:19
  44.2 17.8 %collective-permute-start.11 = (f32[2,4,6,8,128]{4,3,2,1,0:T(8,128)S(1)}, f32[2,4,6,8,128]{4,3,2,1,0:T(8,128)S(1)}, u32[]{:S(2)}, u32[]{:S(2)}) collective-permute-start(f32[2,4,6,8,128]{4,3,2,1,0:T(8,128)S(1)} %get-tuple-element.39), channel_id=1, source_target_pairs={{0,7},{1,0},{2,1},{3,2},{4,3},{5,4},{6,5},{7,6},{8,15},{9,8},{10,9... | collective-permute-start | bytes 589832 | tf_op jit(solution)/shard_map/ppermute | solution.py:19
  57.2 13.6 %collective-permute-start.6 = (f32[2,4,6,8,128]{4,3,2,1,0:T(8,128)S(1)}, f32[2,4,6,8,128]{4,3,2,1,0:T(8,128)S(1)}, u32[]{:S(2)}, u32[]{:S(2)}) collective-permute-start(f32[2,4,6,8,128]{4,3,2,1,0:T(8,128)S(1)} %get-tuple-element.32), channel_id=1, source_target_pairs={{0,1},{1,2},{2,3},{3,4},{4,5},{5,6},{6,7},{7,0},{8,9},{9,10},{10,1... | collective-permute-start | bytes 589832 | tf_op jit(solution)/shard_map/ppermute | solution.py:19
  57.4 13.5 %collective-permute-start.7 = (f32[2,4,6,8,128]{4,3,2,1,0:T(8,128)S(1)}, f32[2,4,6,8,128]{4,3,2,1,0:T(8,128)S(1)}, u32[]{:S(2)}, u32[]{:S(2)}) collective-permute-start(f32[2,4,6,8,128]{4,3,2,1,0:T(8,128)S(1)} %get-tuple-element.33), channel_id=1, source_target_pairs={{0,7},{1,0},{2,1},{3,2},{4,3},{5,4},{6,5},{7,6},{8,15},{9,8},{10,9... | collective-permute-start | bytes 589832 | tf_op jit(solution)/shard_map/ppermute | solution.py:19
  65.7 12.1 %collective-permute-start.12 = (f32[2,4,6,8,128]{4,3,2,1,0:T(8,128)S(1)}, f32[2,4,6,8,128]{4,3,2,1,0:T(8,128)S(1)}, u32[]{:S(2)}, u32[]{:S(2)}) collective-permute-start(f32[2,4,6,8,128]{4,3,2,1,0:T(8,128)S(1)} %get-tuple-element.41), channel_id=1, source_target_pairs={{0,1},{1,2},{2,3},{3,4},{4,5},{5,6},{6,7},{7,0},{8,9},{9,10},{10,1... | collective-permute-start | bytes 589832 | tf_op jit(solution)/shard_map/ppermute | solution.py:19
  65.8 12.0 %collective-permute-start.13 = (f32[2,4,6,8,128]{4,3,2,1,0:T(8,128)S(1)}, f32[2,4,6,8,128]{4,3,2,1,0:T(8,128)S(1)}, u32[]{:S(2)}, u32[]{:S(2)}) collective-permute-start(f32[2,4,6,8,128]{4,3,2,1,0:T(8,128)S(1)} %get-tuple-element.42), channel_id=1, source_target_pairs={{0,7},{1,0},{2,1},{3,2},{4,3},{5,4},{6,5},{7,6},{8,15},{9,8},{10,9... | collective-permute-start | bytes 589832 | tf_op jit(solution)/shard_map/ppermute | solution.py:19
  75.3 18.6 %collective-permute-start.20 = (f32[2,4,6,8,128]{4,3,2,1,0:T(8,128)}, f32[2,4,6,8,128]{4,3,2,1,0:T(8,128)S(1)}, u32[]{:S(2)}, u32[]{:S(2)}) collective-permute-start(f32[2,4,6,8,128]{4,3,2,1,0:T(8,128)} %get-tuple-element.44), channel_id=1, source_target_pairs={{0,7},{1,0},{2,1},{3,2},{4,3},{5,4},{6,5},{7,6},{8,15},{9,8},{10,9... | collective-permute-start | bytes 589832 | tf_op jit(solution)/shard_map/ppermute | solution.py:19
  82.2 19.4 %collective-permute-start.21 = (f32[2,4,6,8,128]{4,3,2,1,0:T(8,128)}, f32[2,4,6,8,128]{4,3,2,1,0:T(8,128)}, u32[]{:S(2)}, u32[]{:S(2)}) collective-permute-start(f32[2,4,6,8,128]{4,3,2,1,0:T(8,128)} %get-tuple-element.45), channel_id=1, source_target_pairs={{0,7},{1,0},{2,1},{3,2},{4,3},{5,4},{6,5},{7,6},{8,15},{9,8},{10,9... | collective-permute-start | bytes 589832 | tf_op jit(solution)/shard_map/ppermute | solution.py:19
  86.4 40.0 %collective-permute-start.19 = (f32[2,4,6,32,128]{4,3,2,1,0:T(8,128)S(1)}, f32[2,4,6,32,128]{4,3,2,1,0:T(8,128)}, u32[]{:S(2)}, u32[]{:S(2)}) collective-permute-start(f32[2,4,6,32,128]{4,3,2,1,0:T(8,128)S(1)} %get-tuple-element.43.refs_1_.vec), channel_id=1, source_target_pairs={{0,16},{16,0},{1,17},{17,1},{2,18},{18,2},{3,19},{19,3},{4,20},{20... | collective-permute-start | bytes 2359304 | tf_op jit(solution)/shard_map/ppermute | solution.py:19
  89.3 47.4 %collective-permute-start.18 = (f32[2,4,6,32,128]{4,3,2,1,0:T(8,128)S(1)}, f32[2,4,6,32,128]{4,3,2,1,0:T(8,128)}, u32[]{:S(2)}, u32[]{:S(2)}) collective-permute-start(f32[2,4,6,32,128]{4,3,2,1,0:T(8,128)S(1)} %get-tuple-element.34.refs_0_.vec), channel_id=1, source_target_pairs={{0,16},{16,0},{1,17},{17,1},{2,18},{18,2},{3,19},{19,3},{4,20},{20... | collective-permute-start | bytes 2359304 | tf_op jit(solution)/shard_map/ppermute | solution.py:19
  110.2 4.3 %copy-start.7 = (bf16[2,16,2,12288]{3,1,2,0:T(8,128)(2,1)}, bf16[2,16,2,12288]{3,1,2,0:T(8,128)(2,1)S(1)}, u32[]{:S(2)}) copy-start(bf16[2,16,2,12288]{3,1,2,0:T(8,128)(2,1)S(1)} %get-tuple-element.46) | copy-start | bytes 4718596
  118.9 3.8 %copy-start.11 = (f32[2,4,2,12288]{3,2,1,0:T(2,128)S(1)}, f32[2,4,2,12288]{3,2,1,0:T(2,128)}, u32[]{:S(2)}) copy-start(f32[2,4,2,12288]{3,2,1,0:T(2,128)} %reshape.212) | copy-start | bytes 2359300
  128.9 3.4 %copy-start.8 = (bf16[2,16,2,12288]{3,1,2,0:T(8,128)(2,1)S(1)}, bf16[2,16,2,12288]{3,1,2,0:T(8,128)(2,1)}, u32[]{:S(2)}) copy-start(bf16[2,16,2,12288]{3,1,2,0:T(8,128)(2,1)} %copy-done.7) | copy-start | bytes 4718596
  128.9 3.4 %copy-start.15 = (f32[2,4,2,12288]{3,2,1,0:T(2,128)S(1)}, f32[2,4,2,12288]{3,2,1,0:T(2,128)}, u32[]{:S(2)}) copy-start(f32[2,4,2,12288]{3,2,1,0:T(2,128)} %reshape.217) | copy-start | bytes 2359300
  139.1 3.4 %copy-start.14 = (f32[2,4,2,12288]{3,2,1,0:T(2,128)S(1)}, f32[2,4,2,12288]{3,2,1,0:T(2,128)}, u32[]{:S(2)}) copy-start(f32[2,4,2,12288]{3,2,1,0:T(2,128)} %reshape.216) | copy-start | bytes 2359300
  147.9 4.3 %collective-permute-start.22 = (f32[2,2,2,16,16]{4,3,0,2,1:T(8,128)S(1)}, f32[2,2,2,16,16]{4,3,0,2,1:T(8,128)S(1)}, u32[]{:S(2)}, u32[]{:S(2)}) collective-permute-start(f32[2,2,2,16,16]{4,3,0,2,1:T(8,128)S(1)} %dynamic_update_slice.22), channel_id=1, source_target_pairs={{0,1},{1,0},{2,3},{3,2},{4,5},{5,4},{6,7},{7,6},{8,9},{9,8},{10,11... | collective-permute-start | bytes 24584 | tf_op jit(solution)/shard_map/ppermute | solution.py:28
  152.2 4.3 %collective-permute-start.23 = (f32[2,2,2,16,16]{4,3,0,2,1:T(8,128)S(1)}, f32[2,2,2,16,16]{4,3,0,2,1:T(8,128)S(1)}, u32[]{:S(2)}, u32[]{:S(2)}) collective-permute-start(f32[2,2,2,16,16]{4,3,0,2,1:T(8,128)S(1)} %add.173), channel_id=1, source_target_pairs={{0,2},{1,3},{2,0},{3,1},{4,6},{5,7},{6,4},{7,5},{8,10},{9,11},{10,... | collective-permute-start | bytes 24584 | tf_op jit(solution)/shard_map/ppermute | solution.py:28
  152.5 4.2 %collective-permute-start.14 = (f32[2,16]{1,0:T(2,128)S(1)}, f32[2,16]{1,0:T(2,128)S(1)}, u32[]{:S(2)}, u32[]{:S(2)}) collective-permute-start(f32[2,16]{1,0:T(2,128)S(1)} %dynamic_update_slice.17), channel_id=1, source_target_pairs={{0,1},{1,0},{2,3},{3,2},{4,5},{5,4},{6,7},{7,6},{8,9},{9,8},{10,11... | collective-permute-start | bytes 392 | tf_op jit(solution)/shard_map/ppermute | solution.py:28
  156.6 18.5 %collective-permute-start.24 = (f32[2,2,2,16,16]{4,3,0,2,1:T(8,128)S(1)}, f32[2,2,2,16,16]{4,3,0,2,1:T(8,128)S(1)}, u32[]{:S(2)}, u32[]{:S(2)}) collective-permute-start(f32[2,2,2,16,16]{4,3,0,2,1:T(8,128)S(1)} %add.174), channel_id=1, source_target_pairs={{0,4},{1,5},{2,6},{3,7},{4,0},{5,1},{6,2},{7,3},{8,12},{9,13},{10,... | collective-permute-start | bytes 24584 | tf_op jit(solution)/shard_map/ppermute | solution.py:28
  156.8 3.6 %collective-permute-start.15 = (f32[2,16]{1,0:T(2,128)S(1)}, f32[2,16]{1,0:T(2,128)S(1)}, u32[]{:S(2)}, u32[]{:S(2)}) collective-permute-start(f32[2,16]{1,0:T(2,128)S(1)} %add.146), channel_id=1, source_target_pairs={{0,2},{1,3},{2,0},{3,1},{4,6},{5,7},{6,4},{7,5},{8,10},{9,11},{10,... | collective-permute-start | bytes 392 | tf_op jit(solution)/shard_map/ppermute | solution.py:28
  160.5 4.5 %collective-permute-start.16 = (f32[2,16]{1,0:T(2,128)S(1)}, f32[2,16]{1,0:T(2,128)S(1)}, u32[]{:S(2)}, u32[]{:S(2)}) collective-permute-start(f32[2,16]{1,0:T(2,128)S(1)} %add.147), channel_id=1, source_target_pairs={{0,4},{1,5},{2,6},{3,7},{4,0},{5,1},{6,2},{7,3},{8,12},{9,13},{10,... | collective-permute-start | bytes 392 | tf_op jit(solution)/shard_map/ppermute | solution.py:28
  165.0 11.7 %collective-permute-start.17 = (f32[2,16]{1,0:T(2,128)S(1)}, f32[2,16]{1,0:T(2,128)S(1)}, u32[]{:S(2)}, u32[]{:S(2)}) collective-permute-start(f32[2,16]{1,0:T(2,128)S(1)} %add.148), channel_id=1, source_target_pairs={{0,16},{16,0},{1,17},{17,1},{2,18},{18,2},{3,19},{19,3},{4,20},{20... | collective-permute-start | bytes 392 | tf_op jit(solution)/shard_map/ppermute | solution.py:28
  175.1 5.1 %collective-permute-start.25 = (f32[2,2,2,16,16]{4,3,0,2,1:T(8,128)S(1)}, f32[2,2,2,16,16]{4,3,0,2,1:T(8,128)S(1)}, u32[]{:S(2)}, u32[]{:S(2)}) collective-permute-start(f32[2,2,2,16,16]{4,3,0,2,1:T(8,128)S(1)} %add.175), channel_id=1, source_target_pairs={{0,16},{16,0},{1,17},{17,1},{2,18},{18,2},{3,19},{19,3},{4,20},{20... | collective-permute-start | bytes 24584 | tf_op jit(solution)/shard_map/ppermute | solution.py:28
  (12 other events, 22.0 us)

commit v3 on v2

--- a/solution.py
+++ b/solution.py
@@ -17,17 +17,6 @@
 def from_behind(x, axis, by):
     devices = lax.axis_size(axis)
     return lax.ppermute(x, axis, [(i, (i + by) % devices) for i in range(devices)])
-
-
-def butterfly(x, axis):
-    devices = lax.axis_size(axis)
-    if devices & (devices - 1):
-        return lax.psum(x, axis)
-    step = 1
-    while step < devices:
-        x = x + lax.ppermute(x, axis, [(i, i ^ step) for i in range(devices)])
-        step *= 2
-    return x
 
 
 def iota(dim):
@@ -214,7 +203,104 @@
     lax.fori_loop(0, vec.shape[1], body, 0)
 
 
-def call(kernel, args, outs, flops=0, place=None, blocks=(), smem=()):
+def gram_kernel(count, *refs):
+    left, right, out, total = refs[:count], refs[count:-2], refs[-2], refs[-1]
+    tiles = left[0].shape[3] // TILE
+    wide = 2 if tiles % 2 == 0 else 1
+
+    def gather(pieces, colour, first):
+        rows = []
+        for p in range(2):
+            for piece in pieces:
+                lanes = [
+                    piece[0, :, p * 3 + colour, pl.ds((first + j) * TILE, TILE), :].reshape(-1, LANES)
+                    for j in range(wide)
+                ]
+                rows.append(jnp.concatenate(lanes, axis=1) if wide > 1 else lanes[0])
+        value = jnp.concatenate(rows, axis=0)
+        high = value.astype(jnp.bfloat16)
+        return high, (value - high.astype(F32)).astype(jnp.bfloat16)
+
+    def dot(a, b):
+        return lax.dot_general(a, b, (((1,), (1,)), ((), ())), preferred_element_type=F32)
+
+    total[...] = jnp.zeros_like(total)
+    for colour in range(3):
+        for first in range(0, tiles, wide):
+            lh, ll = gather(left, colour, first)
+            rh, rl = gather(right, colour, first)
+            total[...] += dot(lh, rh) + (dot(lh, rl) + dot(ll, rh))
+
+    rows, cols = total.shape
+    at_row = lax.broadcasted_iota(jnp.int32, (rows, cols), 0) % TILE
+    at_col = lax.broadcasted_iota(jnp.int32, (rows, cols), 1) % TILE
+    value = jnp.where(at_row == at_col, total[...], 0.0)
+
+    def picks(n):
+        i = lax.broadcasted_iota(jnp.int32, (n // TILE, n), 0)
+        j = lax.broadcasted_iota(jnp.int32, (n // TILE, n), 1)
+        return jnp.where(j // TILE == i, 1.0, 0.0)
+
+    value = jnp.dot(picks(rows), value, precision=lax.Precision.HIGHEST, preferred_element_type=F32)
+    out[0] = lax.dot_general(
+        value, picks(cols), (((1,), (1,)), ((), ())),
+        precision=lax.Precision.HIGHEST, preferred_element_type=F32,
+    )
+
+
+def sum_kernel(groups, size, mine, out, slots, send_sem, recv_sem):
+    count = groups * size
+    me = lax.axis_index("cfg") * size + lax.axis_index("sa")
+
+    def device(away):
+        other = lax.rem(me + away, count)
+        return {"cfg": other // size, "sa": lax.rem(other, size)}
+
+    barrier = pltpu.get_barrier_semaphore()
+    for away in range(1, count):
+        pl.semaphore_signal(barrier, inc=1, device_id=device(away), device_id_type=pl.DeviceIdType.MESH)
+    pl.semaphore_wait(barrier, count - 1)
+    copies = []
+    for away in range(1, count):
+        copy = pltpu.make_async_remote_copy(
+            src_ref=mine,
+            dst_ref=slots.at[away],
+            send_sem=send_sem.at[away],
+            recv_sem=recv_sem.at[away],
+            device_id=device(away),
+            device_id_type=pl.DeviceIdType.MESH,
+        )
+        copy.start()
+        copies.append(copy)
+    slots[0] = mine[...]
+    for copy in copies:
+        copy.wait()
+    for group in range(groups):
+        value = slots[lax.rem(me + count - group * size, count)]
+        for source in range(1, size):
+            value = value + slots[lax.rem(me + 2 * count - group * size - source, count)]
+        out[group] = value
+
+
+def sum_blocks(block, groups, size):
+    count = groups * size
+    return pl.pallas_call(
+        functools.partial(sum_kernel, groups, size),
+        out_shape=jax.ShapeDtypeStruct((groups,) + block.shape, F32),
+        in_specs=[pl.BlockSpec(memory_space=pltpu.VMEM)],
+        out_specs=pl.BlockSpec(memory_space=pltpu.VMEM),
+        scratch_shapes=[
+            pltpu.VMEM((count,) + block.shape, F32),
+            pltpu.SemaphoreType.DMA((count,)),
+            pltpu.SemaphoreType.DMA((count,)),
+        ],
+        compiler_params=pltpu.CompilerParams(
+            collective_id=0, has_side_effects=True, vmem_limit_bytes=40 * 2**20
+        ),
+    )(block)
+
+
+def call(kernel, args, outs, flops=0, place=None, blocks=(), smem=(), scratch=()):
     blocks = dict(blocks)
 
     def plain(shape):
@@ -233,6 +319,7 @@
             grid=(outs[0][0],),
             in_specs=in_specs,
             out_specs=[plain(o) for o in outs],
+            scratch_shapes=list(scratch),
         ),
         out_shape=[jax.ShapeDtypeStruct(o, F32) for o in outs],
         compiler_params=pltpu.CompilerParams(vmem_limit_bytes=40 * 2**20),
@@ -250,21 +337,6 @@
     lead, rows = x.shape[:-2], x.shape[-2]
     x = x.reshape(lead + (rows // nz, nz, LANES))
     return jnp.swapaxes(x, -3, -2).reshape(lead + (nz, rows // nz * LANES))
-
-
-def split(x):
-    high = lax.reduce_precision(x, exponent_bits=8, mantissa_bits=7)
-    return high.astype(jnp.bfloat16), (x - high).astype(jnp.bfloat16)
-
-
-def raw_gram(left, right):
-    (lh, ll), (rh, rl) = split(left), split(right)
-
-    def dot(a, b):
-        return jnp.einsum("tipk,tjqk->tipjq", a, b, preferred_element_type=F32)
-
-    full = dot(lh, rh) + (dot(lh, rl) + dot(ll, rh))
-    return full[:, :, 0, :, 0] + full[:, :, 1, :, 1], full[:, :, 0, :, 1] - full[:, :, 1, :, 0]
 
 
 def join_links(links, place, nz):
@@ -341,29 +413,39 @@
                 lows[k] = from_behind(top, "sa", 1)
 
     held = [fields] + [[from_behind(f, "cfg", -away) for f in fields] for away in range(1, groups)]
-    sums = jnp.concatenate([jnp.sum(f * f, axis=(2, 3, 4)) for f in fields], axis=1)
-    sums = lax.dynamic_update_slice_in_dim(jnp.zeros((count_t, count_n), F32), sums, me * own_n, axis=1)
-    inverse = lax.rsqrt(butterfly(butterfly(sums, "sa"), "cfg"))
-
     images = [
         call(functools.partial(ahead_kernel, nz), (rows, fields[k], highs[k]), [shape], work * 220)[0]
         for k in range(pieces)
     ]
 
-    def flat(x):
-        return x.reshape(x.shape[:2] + (2, -1))
-
-    both = jnp.concatenate([flat(x) for x in fields + images], axis=1)
-    raw = jnp.zeros((count_t, 2, 2, count_n, count_n), F32)
-    for away in range(groups):
-        source = lax.rem(me + away, groups)
-        for k in range(pieces):
-            re, im = raw_gram(flat(held[away][k]), both)
-            block = jnp.stack([re, im], axis=1).reshape(count_t, 2, part_n, 2, own_n)
-            block = jnp.moveaxis(block, 3, 1)
-            raw = lax.dynamic_update_slice(raw, block, (0, 0, 0, source * own_n + k * part_n, me * own_n))
-    raw = butterfly(butterfly(raw, "sa"), "cfg")
+    right = fields + images
+    side, across = 2 * own_n, 2 * 2 * own_n
+    grams = [
+        call(
+            functools.partial(gram_kernel, pieces),
+            held[away] + right,
+            [(count_t, side, across)],
+            2 * 3 * side * TILE * across * work // part_n,
+            scratch=[pltpu.VMEM((side * TILE, across * TILE), F32)],
+        )[0]
+        for away in range(groups)
+    ]
+    block = jnp.stack(grams).reshape(-1, LANES)
+    raw = sum_blocks(block, groups, lax.axis_size("sa"))
+    raw = raw.reshape(groups, groups, count_t, 2, own_n, 2, 2, own_n)
+    re = raw[:, :, :, 0, :, 0] + raw[:, :, :, 1, :, 1]
+    im = raw[:, :, :, 0, :, 1] - raw[:, :, :, 1, :, 0]
+    raw = jnp.moveaxis(jnp.stack([re, im], axis=3), 5, 3)
+    raw = jnp.concatenate(
+        [
+            jnp.concatenate([raw[g, (source - g) % groups] for source in range(groups)], axis=3)
+            for g in range(groups)
+        ],
+        axis=4,
+    )
     over, ahead = raw[:, 0], raw[:, 1]
+    own_entry = jnp.eye(count_n, dtype=bool)
+    inverse = lax.rsqrt(jnp.sum(jnp.where(own_entry, over[:, 0], 0.0), axis=2))
     turned = jnp.swapaxes(ahead, 2, 3)
     lap = 6.0 * over - jnp.stack([ahead[:, 0] + turned[:, 0], ahead[:, 1] - turned[:, 1]], axis=1)
     grams = jnp.stack([over, lap], axis=1)

time: 182 us -> 128 us (0.70)
  matrix products: 29.5 us -> 0 us
  local copies, waits for them, and re-layouts: 29.7 us -> 4.91 us
  Pallas kernels: 36.7 us -> 54.5 us
  starting transfers between devices: 53.8 us -> 37.9 us
  other arithmetic: 3.59 us -> 1.04 us
  waiting for transfers between devices: 26.6 us -> 29 us
    dot_general x12 -> x0, matrix products: 29.5 us -> none  [dot(): return jnp.einsum('tipk,tjqk->tipjq', a, b, preferred_element_type=F32)]
    reshape x10 -> x2, local copies, waits for them, and re-layouts: 18.7 us -> 0.53 us  [the longest x1 0.42 us: on_device(): raw = raw.reshape(groups, groups, count_t, 2, own_n, 2, 2, own_n)]
    ppermute x8 -> x0, starting transfers between devices: 15.5 us -> none  [butterfly(): x = x + lax.ppermute(x, axis, [(i, i ^ step) for i in range(devices)])]
    ppermute x18, waiting for transfers between devices: 13.9 us -> 29 us  [from_behind(): lax.ppermute(x, axis, [(i, (i + by) % devices) for i in range(devices)])]
    pallas_call x0 -> x1, Pallas kernels: none -> 14.3 us  [sum_blocks(): pl.pallas_call(functools.partial(sum_kernel, groups, size), out_shape=jax...]
    ppermute x8 -> x0, waiting for transfers between devices: 12.7 us -> none  [butterfly(): x = x + lax.ppermute(x, axis, [(i, i ^ step) for i in range(devices)])]
    unnamed x36 -> x6, local copies, waits for them, and re-layouts: 6.62 us -> 1.9 us
    pallas_call x12 -> x14, Pallas kernels: 36.7 us -> 40.2 us  [call(): pl.pallas_call(kernel, grid_spec=pltpu.PrefetchScalarGridSpec(num_scalar_...]
  transfers between devices with their start and end apart: 26 -> 18, of which waited for: 9 -> 8; matrix products, arithmetic and copies ran while one was open for 24% -> 0% of each run, Pallas kernels for 20% -> 27%
where the time goes in v3:
time: 128 us
  Pallas kernels  54.5 us (43%)
  starting transfers between devices  37.9 us (30%)
  waiting for transfers between devices  29 us (23%)
  local copies, waits for them, and re-layouts  4.91 us (4%)
    pallas_call x14, Pallas kernels, call(): pl.pallas_call(kernel, grid_spec=pltpu.PrefetchScalarGridSpec(num_scalar_...  40.2 us
    ppermute x18, starting transfers between devices, from_behind(): lax.ppermute(x, axis, [(i, (i + by) % devices) for i in range(devices)])  37.9 us
    ppermute x18, waiting for transfers between devices, from_behind(): lax.ppermute(x, axis, [(i, (i + by) % devices) for i in range(devices)])  29 us
    pallas_call x1, Pallas kernels, sum_blocks(): pl.pallas_call(functools.partial(sum_kernel, groups, size), out_shape=jax...  14.3 us
  transfers between devices with their start and end apart: 18, of which 8 were waited for; matrix products, arithmetic and copies ran while one was open for 0% of the time, Pallas kernels for 27%

profile of v3, /device:TPU:0, one launch (start us, length us, event | category | flops | bytes accessed | tf_op | source)
XLA Modules:
  0.0 128.3 jit_solution(10410815010511273980)
XLA Ops:
  0.6 2.3 %constant_dynamic-slice_fusion = f32[2,54,16,128]{3,2,1,0:T(8,128)} fusion(f32[4,54,16,128]{3,2,1,0:T(8,128)} %bitcast.57, s32[]{:T(128)S(6)} %select_n.7), kind=kLoop, calls=%fused_computation.25 | loop fusion | bytes 1769476 | tf_op jit(solution)/shard_map/dynamic_slice | solution.py:349
  3.4 1.9 %copy-done = f32[2,16,2,3,4,1024]{5,4,3,2,1,0:T(4,128)S(1)} copy-done((f32[2,16,2,3,4,1024]{5,4,3,2,1,0:T(4,128)S(1)}, f32[2,16,2,3,4,1024]{5,4,3,2,1,0:T(4,128)}, u32[]{:S(2)}) %copy-start) | copy-done | bytes 3145752
  6.0 2.6 %collective-permute-start.8 = (f32[2,4,6,8,128]{4,3,2,1,0:T(8,128)S(1)}, f32[2,4,6,8,128]{4,3,2,1,0:T(8,128)S(1)}, u32[]{:S(2)}, u32[]{:S(2)}) collective-permute-start(f32[2,4,6,8,128]{4,3,2,1,0:T(8,128)S(1)} %get-tuple-element.35), channel_id=1, source_target_pairs={{0,1},{1,2},{2,3},{3,4},{4,5},{5,6},{6,7},{7,0},{8,9},{9,10},{10,1... | collective-permute-start | bytes 589832 | tf_op jit(solution)/shard_map/ppermute | solution.py:19
  8.6 3.1 %collective-permute-start.9 = (f32[2,4,6,8,128]{4,3,2,1,0:T(8,128)S(1)}, f32[2,4,6,8,128]{4,3,2,1,0:T(8,128)S(1)}, u32[]{:S(2)}, u32[]{:S(2)}) collective-permute-start(f32[2,4,6,8,128]{4,3,2,1,0:T(8,128)S(1)} %get-tuple-element.36), channel_id=1, source_target_pairs={{0,7},{1,0},{2,1},{3,2},{4,3},{5,4},{6,5},{7,6},{8,15},{9,8},{10,9... | collective-permute-start | bytes 589832 | tf_op jit(solution)/shard_map/ppermute | solution.py:19
  11.7 4.7 %collective-permute-start.3 = (f32[2,4,6,8,128]{4,3,2,1,0:T(8,128)S(1)}, f32[2,4,6,8,128]{4,3,2,1,0:T(8,128)S(1)}, u32[]{:S(2)}, u32[]{:S(2)}) collective-permute-start(f32[2,4,6,8,128]{4,3,2,1,0:T(8,128)S(1)} %get-tuple-element.27), channel_id=1, source_target_pairs={{0,7},{1,0},{2,1},{3,2},{4,3},{5,4},{6,5},{7,6},{8,15},{9,8},{10,9... | collective-permute-start | bytes 589832 | tf_op jit(solution)/shard_map/ppermute | solution.py:19
  16.4 1.6 %shard_map.41 = (f32[2,54,32,128]{3,2,1,0:T(8,128)S(1)}, f32[2,18,8,128]{3,2,1,0:T(8,128)S(1)}) custom-call(s32[2]{0:T(128)S(1)} %pad_add_fusion.place, f32[4,54,16,128]{3,2,1,0:T(8,128)S(1)} %bitcast.58, f32[2,54,16,128]{3,2,1,0:T(8,128)S(1)} %collective-permute-done.theirs), custom_call_target="tpu_custom_call" | custom-call | bytes 3833856 | tf_op jit(solution)/shard_map/pallas_call | solution.py:315
  18.1 11.1 %collective-permute-done.1.below = f32[2,18,8,128]{3,2,1,0:T(8,128)S(1)} collective-permute-done((f32[2,18,8,128]{3,2,1,0:T(8,128)S(1)}, f32[2,18,8,128]{3,2,1,0:T(8,128)S(1)}, u32[]{:S(2)}, u32[]{:S(2)}) %collective-permute-start.1) | collective-permute-done | bytes 147488 | tf_op jit(solution)/shard_map/ppermute | solution.py:19
  29.2 2.9 %shard_map.42.refs_1_ = f32[2,54,32,128]{3,2,1,0:T(8,128)S(1)} custom-call(f32[2,54,32,128]{3,2,1,0:T(8,128)S(1)} %get-tuple-element.24.links.refs_0_, f32[2,18,8,128]{3,2,1,0:T(8,128)S(1)} %collective-permute-done.1.below), custom_call_target="tpu_custom_call" | custom-call | flops 1769472 | bytes 3538944 | tf_op jit(solution)/shard_map/pallas_call | solution.py:315
  32.2 3.6 %shard_map.47 = (f32[2,4,6,32,128]{4,3,2,1,0:T(8,128)S(1)}, f32[2,4,6,8,128]{4,3,2,1,0:T(8,128)S(1)}, f32[2,4,6,8,128]{4,3,2,1,0:T(8,128)S(1)}) custom-call(s32[2]{0:T(128)S(1)} %pad_add_fusion.place, f32[2,54,32,128]{3,2,1,0:T(8,128)S(1)} %get-tuple-element.24.links.refs_0_, f32[2,54,32,128]{3,2,1,0:T(8,128)S(1)} %shard_map.42.refs_1_, ...), custom_call_target="tpu_custom_call" | custom-call | flops 14745600 | bytes 2359296 | tf_op jit(solution)/shard_map/pallas_call | solution.py:315
  35.8 2.5 %collective-permute-start.10 = (f32[2,4,6,8,128]{4,3,2,1,0:T(8,128)S(1)}, f32[2,4,6,8,128]{4,3,2,1,0:T(8,128)S(1)}, u32[]{:S(2)}, u32[]{:S(2)}) collective-permute-start(f32[2,4,6,8,128]{4,3,2,1,0:T(8,128)S(1)} %get-tuple-element.38), channel_id=1, source_target_pairs={{0,1},{1,2},{2,3},{3,4},{4,5},{5,6},{6,7},{7,0},{8,9},{9,10},{10,1... | collective-permute-start | bytes 589832 | tf_op jit(solution)/shard_map/ppermute | solution.py:19
  38.3 3.1 %collective-permute-start.11 = (f32[2,4,6,8,128]{4,3,2,1,0:T(8,128)S(1)}, f32[2,4,6,8,128]{4,3,2,1,0:T(8,128)S(1)}, u32[]{:S(2)}, u32[]{:S(2)}) collective-permute-start(f32[2,4,6,8,128]{4,3,2,1,0:T(8,128)S(1)} %get-tuple-element.39), channel_id=1, source_target_pairs={{0,7},{1,0},{2,1},{3,2},{4,3},{5,4},{6,5},{7,6},{8,15},{9,8},{10,9... | collective-permute-start | bytes 589832 | tf_op jit(solution)/shard_map/ppermute | solution.py:19
  41.4 3.6 %shard_map.44 = (f32[2,4,6,32,128]{4,3,2,1,0:T(8,128)S(1)}, f32[2,4,6,8,128]{4,3,2,1,0:T(8,128)S(1)}, f32[2,4,6,8,128]{4,3,2,1,0:T(8,128)S(1)}) custom-call(s32[2]{0:T(128)S(1)} %pad_add_fusion.place, f32[2,54,32,128]{3,2,1,0:T(8,128)S(1)} %get-tuple-element.24.links.refs_0_, f32[2,54,32,128]{3,2,1,0:T(8,128)S(1)} %shard_map.42.refs_1_, ...), custom_call_target="tpu_custom_call" | custom-call | flops 14745600 | bytes 2359296 | tf_op jit(solution)/shard_map/pallas_call | solution.py:315
  45.2 4.7 %collective-permute-start.5 = (f32[2,4,6,8,128]{4,3,2,1,0:T(8,128)S(1)}, f32[2,4,6,8,128]{4,3,2,1,0:T(8,128)S(1)}, u32[]{:S(2)}, u32[]{:S(2)}) collective-permute-start(f32[2,4,6,8,128]{4,3,2,1,0:T(8,128)S(1)} %get-tuple-element.30), channel_id=1, source_target_pairs={{0,7},{1,0},{2,1},{3,2},{4,3},{5,4},{6,5},{7,6},{8,15},{9,8},{10,9... | collective-permute-start | bytes 589832 | tf_op jit(solution)/shard_map/ppermute | solution.py:19
  49.9 2.2 %collective-permute-done.10.refs_3_ = f32[2,4,6,8,128]{4,3,2,1,0:T(8,128)S(1)} collective-permute-done((f32[2,4,6,8,128]{4,3,2,1,0:T(8,128)S(1)}, f32[2,4,6,8,128]{4,3,2,1,0:T(8,128)S(1)}, u32[]{:S(2)}, u32[]{:S(2)}) %collective-permute-start.10) | collective-permute-done | bytes 196640 | tf_op jit(solution)/shard_map/ppermute | solution.py:19
  52.1 2.4 %collective-permute-done.11.refs_4_ = f32[2,4,6,8,128]{4,3,2,1,0:T(8,128)S(1)} collective-permute-done((f32[2,4,6,8,128]{4,3,2,1,0:T(8,128)S(1)}, f32[2,4,6,8,128]{4,3,2,1,0:T(8,128)S(1)}, u32[]{:S(2)}, u32[]{:S(2)}) %collective-permute-start.11) | collective-permute-done | bytes 196640 | tf_op jit(solution)/shard_map/ppermute | solution.py:19
  54.5 3.7 %shard_map.48 = (f32[2,4,6,32,128]{4,3,2,1,0:T(8,128)S(1)}, f32[2,4,6,8,128]{4,3,2,1,0:T(8,128)S(1)}, f32[2,4,6,8,128]{4,3,2,1,0:T(8,128)S(1)}) custom-call(s32[2]{0:T(128)S(1)} %pad_add_fusion.place, f32[2,54,32,128]{3,2,1,0:T(8,128)S(1)} %get-tuple-element.24.links.refs_0_, f32[2,54,32,128]{3,2,1,0:T(8,128)S(1)} %shard_map.42.refs_1_, ...), custom_call_target="tpu_custom_call" | custom-call | flops 14745600 | bytes 2359296 | tf_op jit(solution)/shard_map/pallas_call | solution.py:315
  58.4 4.7 %collective-permute-start.13 = (f32[2,4,6,8,128]{4,3,2,1,0:T(8,128)S(1)}, f32[2,4,6,8,128]{4,3,2,1,0:T(8,128)S(1)}, u32[]{:S(2)}, u32[]{:S(2)}) collective-permute-start(f32[2,4,6,8,128]{4,3,2,1,0:T(8,128)S(1)} %get-tuple-element.42), channel_id=1, source_target_pairs={{0,7},{1,0},{2,1},{3,2},{4,3},{5,4},{6,5},{7,6},{8,15},{9,8},{10,9... | collective-permute-start | bytes 589832 | tf_op jit(solution)/shard_map/ppermute | solution.py:19
  63.0 3.7 %shard_map.45 = (f32[2,4,6,32,128]{4,3,2,1,0:T(8,128)S(1)}, f32[2,4,6,8,128]{4,3,2,1,0:T(8,128)S(1)}, f32[2,4,6,8,128]{4,3,2,1,0:T(8,128)S(1)}) custom-call(s32[2]{0:T(128)S(1)} %pad_add_fusion.place, f32[2,54,32,128]{3,2,1,0:T(8,128)S(1)} %get-tuple-element.24.links.refs_0_, f32[2,54,32,128]{3,2,1,0:T(8,128)S(1)} %shard_map.42.refs_1_, ...), custom_call_target="tpu_custom_call" | custom-call | flops 14745600 | bytes 2359296 | tf_op jit(solution)/shard_map/pallas_call | solution.py:315
  66.8 4.7 %collective-permute-start.7 = (f32[2,4,6,8,128]{4,3,2,1,0:T(8,128)S(1)}, f32[2,4,6,8,128]{4,3,2,1,0:T(8,128)S(1)}, u32[]{:S(2)}, u32[]{:S(2)}) collective-permute-start(f32[2,4,6,8,128]{4,3,2,1,0:T(8,128)S(1)} %get-tuple-element.33), channel_id=1, source_target_pairs={{0,7},{1,0},{2,1},{3,2},{4,3},{5,4},{6,5},{7,6},{8,15},{9,8},{10,9... | collective-permute-start | bytes 589832 | tf_op jit(solution)/shard_map/ppermute | solution.py:19
  71.8 4.4 %shard_map.49 = (f32[2,4,6,32,128]{4,3,2,1,0:T(8,128)S(1)}, f32[2,4,6,8,128]{4,3,2,1,0:T(8,128)}, f32[2,4,6,8,128]{4,3,2,1,0:T(8,128)S(1)}) custom-call(s32[2]{0:T(128)S(1)} %pad_add_fusion.place, f32[2,54,32,128]{3,2,1,0:T(8,128)S(1)} %get-tuple-element.24.links.refs_0_, f32[2,54,32,128]{3,2,1,0:T(8,128)S(1)} %shard_map.42.refs_1_, ...), custom_call_target="tpu_custom_call" | custom-call | flops 14745600 | bytes 2359296 | tf_op jit(solution)/shard_map/pallas_call | solution.py:315
  76.2 1.5 %collective-permute-start.17 = (f32[2,4,6,32,128]{4,3,2,1,0:T(8,128)S(1)}, f32[2,4,6,32,128]{4,3,2,1,0:T(8,128)S(1)}, u32[]{:S(2)}, u32[]{:S(2)}) collective-permute-start(f32[2,4,6,32,128]{4,3,2,1,0:T(8,128)S(1)} %get-tuple-element.43.vec.refs_1_.refs_3_), channel_id=1, source_target_pairs={{0,16},{16,0},{1,17},{17,1},{2,18},{18,2},{3,19},{19,3},{4,20},{20... | collective-permute-start | bytes 2359304 | tf_op jit(solution)/shard_map/ppermute | solution.py:19
  77.7 4.4 %shard_map.46 = (f32[2,4,6,32,128]{4,3,2,1,0:T(8,128)S(1)}, f32[2,4,6,8,128]{4,3,2,1,0:T(8,128)}, f32[2,4,6,8,128]{4,3,2,1,0:T(8,128)S(1)}) custom-call(s32[2]{0:T(128)S(1)} %pad_add_fusion.place, f32[2,54,32,128]{3,2,1,0:T(8,128)S(1)} %get-tuple-element.24.links.refs_0_, f32[2,54,32,128]{3,2,1,0:T(8,128)S(1)} %shard_map.42.refs_1_, ...), custom_call_target="tpu_custom_call" | custom-call | flops 14745600 | bytes 2359296 | tf_op jit(solution)/shard_map/pallas_call | solution.py:315
  82.6 3.1 %collective-permute-start.15 = (f32[2,4,6,8,128]{4,3,2,1,0:T(8,128)S(1)}, f32[2,4,6,8,128]{4,3,2,1,0:T(8,128)S(1)}, u32[]{:S(2)}, u32[]{:S(2)}) collective-permute-start(f32[2,4,6,8,128]{4,3,2,1,0:T(8,128)S(1)} %get-tuple-element.45), channel_id=1, source_target_pairs={{0,7},{1,0},{2,1},{3,2},{4,3},{5,4},{6,5},{7,6},{8,15},{9,8},{10,9... | collective-permute-start | bytes 589832 | tf_op jit(solution)/shard_map/ppermute | solution.py:19
  85.8 1.9 %collective-permute-start.14 = (f32[2,4,6,8,128]{4,3,2,1,0:T(8,128)S(1)}, f32[2,4,6,8,128]{4,3,2,1,0:T(8,128)S(1)}, u32[]{:S(2)}, u32[]{:S(2)}) collective-permute-start(f32[2,4,6,8,128]{4,3,2,1,0:T(8,128)S(1)} %get-tuple-element.44), channel_id=1, source_target_pairs={{0,7},{1,0},{2,1},{3,2},{4,3},{5,4},{6,5},{7,6},{8,15},{9,8},{10,9... | collective-permute-start | bytes 589832 | tf_op jit(solution)/shard_map/ppermute | solution.py:19
  87.7 1.6 %collective-permute-done.15.high = f32[2,4,6,8,128]{4,3,2,1,0:T(8,128)S(1)} collective-permute-done((f32[2,4,6,8,128]{4,3,2,1,0:T(8,128)S(1)}, f32[2,4,6,8,128]{4,3,2,1,0:T(8,128)S(1)}, u32[]{:S(2)}, u32[]{:S(2)}) %collective-permute-start.15) | collective-permute-done | bytes 196640 | tf_op jit(solution)/shard_map/ppermute | solution.py:19
  89.3 1.6 %shard_map.51.refs_5_ = f32[2,4,6,32,128]{4,3,2,1,0:T(8,128)S(1)} custom-call(f32[2,54,32,128]{3,2,1,0:T(8,128)S(1)} %get-tuple-element.24.links.refs_0_, f32[2,4,6,32,128]{4,3,2,1,0:T(8,128)S(1)} %get-tuple-element.43.vec.refs_1_.refs_3_, f32[2,4,6,8,128]{4,3,2,1,0:T(8,128)S(1)} %collective-permute-done.15.high), custom_call_target="tpu_custom_call" | custom-call | flops 7208960 | bytes 1572864 | tf_op jit(solution)/shard_map/pallas_call | solution.py:315
  91.4 1.6 %shard_map.50.refs_4_ = f32[2,4,6,32,128]{4,3,2,1,0:T(8,128)S(1)} custom-call(f32[2,54,32,128]{3,2,1,0:T(8,128)S(1)} %get-tuple-element.24.links.refs_0_, f32[2,4,6,32,128]{4,3,2,1,0:T(8,128)S(1)} %get-tuple-element.34.vec.refs_0_.refs_2_, f32[2,4,6,8,128]{4,3,2,1,0:T(8,128)S(1)} %collective-permute-done.14.high), custom_call_target="tpu_custom_call" | custom-call | flops 7208960 | bytes 1572864 | tf_op jit(solution)/shard_map/pallas_call | solution.py:315
  93.1 2.7 %shard_map.52 = f32[2,16,32]{2,1,0:T(8,128)S(1)} custom-call(f32[2,4,6,32,128]{4,3,2,1,0:T(8,128)S(1)} %get-tuple-element.34.vec.refs_0_.refs_2_, f32[2,4,6,32,128]{4,3,2,1,0:T(8,128)S(1)} %get-tuple-element.43.vec.refs_1_.refs_3_, f32[2,4,6,32,128]{4,3,2,1,0:T(8,128)S(1)} %get-tuple-element.34.vec.refs_0_.refs_2_, ...), custom_call_target="tpu_custom_call" | custom-call | flops 201326592 | bytes 8192 | tf_op jit(solution)/shard_map/pallas_call | solution.py:315
  96.7 9.8 %collective-permute-done.16.refs_0_.refs_2_ = f32[2,4,6,32,128]{4,3,2,1,0:T(8,128)S(1)} collective-permute-done((f32[2,4,6,32,128]{4,3,2,1,0:T(8,128)S(1)}, f32[2,4,6,32,128]{4,3,2,1,0:T(8,128)S(1)}, u32[]{:S(2)}, u32[]{:S(2)}) %collective-permute-start.16) | collective-permute-done | bytes 786464 | tf_op jit(solution)/shard_map/ppermute | solution.py:19
  106.5 2.6 %shard_map.53 = f32[2,16,32]{2,1,0:T(8,128)S(1)} custom-call(f32[2,4,6,32,128]{4,3,2,1,0:T(8,128)S(1)} %collective-permute-done.16.refs_0_.refs_2_, f32[2,4,6,32,128]{4,3,2,1,0:T(8,128)S(1)} %collective-permute-done.17.refs_1_.refs_3_, f32[2,4,6,32,128]{4,3,2,1,0:T(8,128)S(1)} %get-tuple-element.34.vec.refs_0_.refs_2_, ...), custom_call_target="tpu_custom_call" | custom-call | flops 201326592 | bytes 8192 | tf_op jit(solution)/shard_map/pallas_call | solution.py:315
  109.3 14.3 %shard_map.54 = f32[2,16,128]{2,1,0:T(8,128)S(1)} custom-call(f32[16,128]{1,0:T(8,128)S(1)} %reshape.65.mine), custom_call_target="tpu_custom_call" | custom-call | tf_op jit(solution)/shard_map/pallas_call | solution.py:287
  125.3 3.0 %shard_map.55 = f32[2,16,6,32,128]{4,3,2,1,0:T(8,128)} custom-call(s32[2]{0:T(128)S(1)} %pad_add_fusion.place, f32[2,16]{1,0:T(2,128)S(1)} %rsqrt.3.inverse, f32[2,4,6,32,128]{4,3,2,1,0:T(8,128)S(1)} %get-tuple-element.34.vec.refs_0_.refs_2_, f32[2,4,6,32,128]{4,3,2,1,0:T(8,128)S(1)} %get-tuple-element.43.vec.refs_1_.refs_3_, ...), custom_call_target="tpu_custom_call" | custom-call | bytes 6291456 | tf_op jit(solution)/shard_map/pallas_call | solution.py:315
  (43 shorter events, 5.6 us)
Async XLA Ops:
  0.6 15.8 %copy-start.2 = (f32[4,3,2,3,3,4,512]{6,5,4,3,2,1,0:T(4,128)S(1)}, f32[4,3,2,3,3,4,512]{6,5,4,3,2,1,0:T(4,128)}, u32[]{:S(2)}) copy-start(f32[4,3,2,3,3,4,512]{6,5,4,3,2,1,0:T(4,128)} %param.2) | copy-start | bytes 5308420
  2.9 13.5 %collective-permute-start = (f32[2,54,16,128]{3,2,1,0:T(8,128)}, f32[2,54,16,128]{3,2,1,0:T(8,128)S(1)}, u32[]{:S(2)}, u32[]{:S(2)}) collective-permute-start(f32[2,54,16,128]{3,2,1,0:T(8,128)} %constant_dynamic-slice_fusion), channel_id=1, source_target_pairs={{0,8},{8,0},{1,9},{9,1},{2,10},{10,2},{3,11},{11,3},{4,12},{12,4},... | collective-permute-start | bytes 2654216 | tf_op jit(solution)/shard_map/ppermute | solution.py:19
  3.4 1.9 %copy-start = (f32[2,16,2,3,4,1024]{5,4,3,2,1,0:T(4,128)S(1)}, f32[2,16,2,3,4,1024]{5,4,3,2,1,0:T(4,128)}, u32[]{:S(2)}) copy-start(f32[2,16,2,3,4,1024]{5,4,3,2,1,0:T(4,128)} %param.3) | copy-start | bytes 9437188
  6.0 26.1 %collective-permute-start.8 = (f32[2,4,6,8,128]{4,3,2,1,0:T(8,128)S(1)}, f32[2,4,6,8,128]{4,3,2,1,0:T(8,128)S(1)}, u32[]{:S(2)}, u32[]{:S(2)}) collective-permute-start(f32[2,4,6,8,128]{4,3,2,1,0:T(8,128)S(1)} %get-tuple-element.35), channel_id=1, source_target_pairs={{0,1},{1,2},{2,3},{3,4},{4,5},{5,6},{6,7},{7,0},{8,9},{9,10},{10,1... | collective-permute-start | bytes 589832 | tf_op jit(solution)/shard_map/ppermute | solution.py:19
  8.6 23.5 %collective-permute-start.9 = (f32[2,4,6,8,128]{4,3,2,1,0:T(8,128)S(1)}, f32[2,4,6,8,128]{4,3,2,1,0:T(8,128)S(1)}, u32[]{:S(2)}, u32[]{:S(2)}) collective-permute-start(f32[2,4,6,8,128]{4,3,2,1,0:T(8,128)S(1)} %get-tuple-element.36), channel_id=1, source_target_pairs={{0,7},{1,0},{2,1},{3,2},{4,3},{5,4},{6,5},{7,6},{8,15},{9,8},{10,9... | collective-permute-start | bytes 589832 | tf_op jit(solution)/shard_map/ppermute | solution.py:19
  11.7 29.7 %collective-permute-start.2 = (f32[2,4,6,8,128]{4,3,2,1,0:T(8,128)S(1)}, f32[2,4,6,8,128]{4,3,2,1,0:T(8,128)S(1)}, u32[]{:S(2)}, u32[]{:S(2)}) collective-permute-start(f32[2,4,6,8,128]{4,3,2,1,0:T(8,128)S(1)} %get-tuple-element.26), channel_id=1, source_target_pairs={{0,1},{1,2},{2,3},{3,4},{4,5},{5,6},{6,7},{7,0},{8,9},{9,10},{10,1... | collective-permute-start | bytes 589832 | tf_op jit(solution)/shard_map/ppermute | solution.py:19
  11.7 29.7 %collective-permute-start.3 = (f32[2,4,6,8,128]{4,3,2,1,0:T(8,128)S(1)}, f32[2,4,6,8,128]{4,3,2,1,0:T(8,128)S(1)}, u32[]{:S(2)}, u32[]{:S(2)}) collective-permute-start(f32[2,4,6,8,128]{4,3,2,1,0:T(8,128)S(1)} %get-tuple-element.27), channel_id=1, source_target_pairs={{0,7},{1,0},{2,1},{3,2},{4,3},{5,4},{6,5},{7,6},{8,15},{9,8},{10,9... | collective-permute-start | bytes 589832 | tf_op jit(solution)/shard_map/ppermute | solution.py:19
  18.1 11.2 %collective-permute-start.1 = (f32[2,18,8,128]{3,2,1,0:T(8,128)S(1)}, f32[2,18,8,128]{3,2,1,0:T(8,128)S(1)}, u32[]{:S(2)}, u32[]{:S(2)}) collective-permute-start(f32[2,18,8,128]{3,2,1,0:T(8,128)S(1)} %get-tuple-element.25), channel_id=1, source_target_pairs={{0,1},{1,2},{2,3},{3,4},{4,5},{5,6},{6,7},{7,0},{8,9},{9,10},{10,1... | collective-permute-start | bytes 442376 | tf_op jit(solution)/shard_map/ppermute | solution.py:19
  29.2 2.9 %copy-start.1 = (f32[2,16,2,3,4,1024]{5,4,3,2,1,0:T(4,128)S(1)}, f32[2,16,2,3,4,1024]{5,4,3,2,1,0:T(4,128)}, u32[]{:S(2)}) copy-start(f32[2,16,2,3,4,1024]{5,4,3,2,1,0:T(4,128)} %param.3) | copy-start | bytes 9437188
  35.8 16.3 %collective-permute-start.10 = (f32[2,4,6,8,128]{4,3,2,1,0:T(8,128)S(1)}, f32[2,4,6,8,128]{4,3,2,1,0:T(8,128)S(1)}, u32[]{:S(2)}, u32[]{:S(2)}) collective-permute-start(f32[2,4,6,8,128]{4,3,2,1,0:T(8,128)S(1)} %get-tuple-element.38), channel_id=1, source_target_pairs={{0,1},{1,2},{2,3},{3,4},{4,5},{5,6},{6,7},{7,0},{8,9},{9,10},{10,1... | collective-permute-start | bytes 589832 | tf_op jit(solution)/shard_map/ppermute | solution.py:19
  38.3 16.2 %collective-permute-start.11 = (f32[2,4,6,8,128]{4,3,2,1,0:T(8,128)S(1)}, f32[2,4,6,8,128]{4,3,2,1,0:T(8,128)S(1)}, u32[]{:S(2)}, u32[]{:S(2)}) collective-permute-start(f32[2,4,6,8,128]{4,3,2,1,0:T(8,128)S(1)} %get-tuple-element.39), channel_id=1, source_target_pairs={{0,7},{1,0},{2,1},{3,2},{4,3},{5,4},{6,5},{7,6},{8,15},{9,8},{10,9... | collective-permute-start | bytes 589832 | tf_op jit(solution)/shard_map/ppermute | solution.py:19
  45.1 17.9 %collective-permute-start.4 = (f32[2,4,6,8,128]{4,3,2,1,0:T(8,128)S(1)}, f32[2,4,6,8,128]{4,3,2,1,0:T(8,128)S(1)}, u32[]{:S(2)}, u32[]{:S(2)}) collective-permute-start(f32[2,4,6,8,128]{4,3,2,1,0:T(8,128)S(1)} %get-tuple-element.29), channel_id=1, source_target_pairs={{0,1},{1,2},{2,3},{3,4},{4,5},{5,6},{6,7},{7,0},{8,9},{9,10},{10,1... | collective-permute-start | bytes 589832 | tf_op jit(solution)/shard_map/ppermute | solution.py:19
  45.2 17.9 %collective-permute-start.5 = (f32[2,4,6,8,128]{4,3,2,1,0:T(8,128)S(1)}, f32[2,4,6,8,128]{4,3,2,1,0:T(8,128)S(1)}, u32[]{:S(2)}, u32[]{:S(2)}) collective-permute-start(f32[2,4,6,8,128]{4,3,2,1,0:T(8,128)S(1)} %get-tuple-element.30), channel_id=1, source_target_pairs={{0,7},{1,0},{2,1},{3,2},{4,3},{5,4},{6,5},{7,6},{8,15},{9,8},{10,9... | collective-permute-start | bytes 589832 | tf_op jit(solution)/shard_map/ppermute | solution.py:19
  58.2 13.6 %collective-permute-start.12 = (f32[2,4,6,8,128]{4,3,2,1,0:T(8,128)S(1)}, f32[2,4,6,8,128]{4,3,2,1,0:T(8,128)S(1)}, u32[]{:S(2)}, u32[]{:S(2)}) collective-permute-start(f32[2,4,6,8,128]{4,3,2,1,0:T(8,128)S(1)} %get-tuple-element.41), channel_id=1, source_target_pairs={{0,1},{1,2},{2,3},{3,4},{4,5},{5,6},{6,7},{7,0},{8,9},{9,10},{10,1... | collective-permute-start | bytes 589832 | tf_op jit(solution)/shard_map/ppermute | solution.py:19
  58.4 13.5 %collective-permute-start.13 = (f32[2,4,6,8,128]{4,3,2,1,0:T(8,128)S(1)}, f32[2,4,6,8,128]{4,3,2,1,0:T(8,128)S(1)}, u32[]{:S(2)}, u32[]{:S(2)}) collective-permute-start(f32[2,4,6,8,128]{4,3,2,1,0:T(8,128)S(1)} %get-tuple-element.42), channel_id=1, source_target_pairs={{0,7},{1,0},{2,1},{3,2},{4,3},{5,4},{6,5},{7,6},{8,15},{9,8},{10,9... | collective-permute-start | bytes 589832 | tf_op jit(solution)/shard_map/ppermute | solution.py:19
  66.8 11.0 %collective-permute-start.6 = (f32[2,4,6,8,128]{4,3,2,1,0:T(8,128)S(1)}, f32[2,4,6,8,128]{4,3,2,1,0:T(8,128)S(1)}, u32[]{:S(2)}, u32[]{:S(2)}) collective-permute-start(f32[2,4,6,8,128]{4,3,2,1,0:T(8,128)S(1)} %get-tuple-element.32), channel_id=1, source_target_pairs={{0,1},{1,2},{2,3},{3,4},{4,5},{5,6},{6,7},{7,0},{8,9},{9,10},{10,1... | collective-permute-start | bytes 589832 | tf_op jit(solution)/shard_map/ppermute | solution.py:19
  66.8 10.9 %collective-permute-start.7 = (f32[2,4,6,8,128]{4,3,2,1,0:T(8,128)S(1)}, f32[2,4,6,8,128]{4,3,2,1,0:T(8,128)S(1)}, u32[]{:S(2)}, u32[]{:S(2)}) collective-permute-start(f32[2,4,6,8,128]{4,3,2,1,0:T(8,128)S(1)} %get-tuple-element.33), channel_id=1, source_target_pairs={{0,7},{1,0},{2,1},{3,2},{4,3},{5,4},{6,5},{7,6},{8,15},{9,8},{10,9... | collective-permute-start | bytes 589832 | tf_op jit(solution)/shard_map/ppermute | solution.py:19
  76.2 20.5 %collective-permute-start.17 = (f32[2,4,6,32,128]{4,3,2,1,0:T(8,128)S(1)}, f32[2,4,6,32,128]{4,3,2,1,0:T(8,128)S(1)}, u32[]{:S(2)}, u32[]{:S(2)}) collective-permute-start(f32[2,4,6,32,128]{4,3,2,1,0:T(8,128)S(1)} %get-tuple-element.43.vec.refs_1_.refs_3_), channel_id=1, source_target_pairs={{0,16},{16,0},{1,17},{17,1},{2,18},{18,2},{3,19},{19,3},{4,20},{20... | collective-permute-start | bytes 2359304 | tf_op jit(solution)/shard_map/ppermute | solution.py:19
  82.1 24.4 %collective-permute-start.16 = (f32[2,4,6,32,128]{4,3,2,1,0:T(8,128)S(1)}, f32[2,4,6,32,128]{4,3,2,1,0:T(8,128)S(1)}, u32[]{:S(2)}, u32[]{:S(2)}) collective-permute-start(f32[2,4,6,32,128]{4,3,2,1,0:T(8,128)S(1)} %get-tuple-element.34.vec.refs_0_.refs_2_), channel_id=1, source_target_pairs={{0,16},{16,0},{1,17},{17,1},{2,18},{18,2},{3,19},{19,3},{4,20},{20... | collective-permute-start | bytes 2359304 | tf_op jit(solution)/shard_map/ppermute | solution.py:19
  82.6 6.7 %collective-permute-start.15 = (f32[2,4,6,8,128]{4,3,2,1,0:T(8,128)S(1)}, f32[2,4,6,8,128]{4,3,2,1,0:T(8,128)S(1)}, u32[]{:S(2)}, u32[]{:S(2)}) collective-permute-start(f32[2,4,6,8,128]{4,3,2,1,0:T(8,128)S(1)} %get-tuple-element.45), channel_id=1, source_target_pairs={{0,7},{1,0},{2,1},{3,2},{4,3},{5,4},{6,5},{7,6},{8,15},{9,8},{10,9... | collective-permute-start | bytes 589832 | tf_op jit(solution)/shard_map/ppermute | solution.py:19
  85.8 5.7 %collective-permute-start.14 = (f32[2,4,6,8,128]{4,3,2,1,0:T(8,128)S(1)}, f32[2,4,6,8,128]{4,3,2,1,0:T(8,128)S(1)}, u32[]{:S(2)}, u32[]{:S(2)}) collective-permute-start(f32[2,4,6,8,128]{4,3,2,1,0:T(8,128)S(1)} %get-tuple-element.44), channel_id=1, source_target_pairs={{0,7},{1,0},{2,1},{3,2},{4,3},{5,4},{6,5},{7,6},{8,15},{9,8},{10,9... | collective-permute-start | bytes 589832 | tf_op jit(solution)/shard_map/ppermute | solution.py:19

commit v4 on v3

--- a/solution.py
+++ b/solution.py
@@ -84,39 +84,34 @@
         lax.fori_loop(0, part_n, body, 0)
 
 
-def join_links_kernel(nz, place, mine, theirs, out, top):
-    half = mine.shape[2]
-    chunks = 2 * half // nz
+def join_links_kernel(nz, place, mine, theirs, below_mine, below_theirs, out, back, below):
+    half, edge = mine.shape[2], below_mine.shape[2]
+    total, comps = out.shape[2], out.shape[1] // 3
     ahead = place[1] == 0
 
-    def body(comp, carry):
+    def join(comp, carry):
         a, b = mine[0, comp], theirs[0, comp]
         out[0, comp, pl.ds(0, half), :] = jnp.where(ahead, a, b)
         out[0, comp, pl.ds(half, half), :] = jnp.where(ahead, b, a)
         return carry
 
-    def edge(comp, carry):
-        first = out.shape[1] - top.shape[1]
-        top[0, comp] = out[0, first + comp, pl.ds(nz - 1, chunks, stride=nz), :]
+    def join_edge(comp, carry):
+        a, b = below_mine[0, comp], below_theirs[0, comp]
+        below[0, comp, pl.ds(0, edge), :] = jnp.where(ahead, a, b)
+        below[0, comp, pl.ds(edge, edge), :] = jnp.where(ahead, b, a)
         return carry
-
-    lax.fori_loop(0, out.shape[1], body, 0)
-    lax.fori_loop(0, top.shape[1], edge, 0)
-
-
-def back_links_kernel(nz, links, below, out):
-    total = links.shape[2]
-    comps = links.shape[1] // 3
 
     def body(comp, carry):
         for direction in range(3):
             where = direction * comps + comp
             for tile in range(total // TILE):
-                out[0, where, pl.ds(tile * TILE, TILE), :] = shifted(
-                    reader(links, 0, where), reader(below, 0, comp), total, nz, tile, direction, False
+                back[0, where, pl.ds(tile * TILE, TILE), :] = shifted(
+                    reader(out, 0, where), reader(below, 0, comp), total, nz, tile, direction, False
                 )
         return carry
 
+    lax.fori_loop(0, out.shape[1], join, 0)
+    lax.fori_loop(0, comps, join_edge, 0)
     lax.fori_loop(0, comps, body, 0)
 
 
@@ -341,21 +336,28 @@
 
 def join_links(links, place, nz):
     rows = to_rows(links.reshape((links.shape[0], 54) + links.shape[5:]))
-    count = lax.axis_size("ta")
-    if count != 2:
-        rows = lax.all_to_all(rows, "ta", split_axis=0, concat_axis=2, tiled=True)
-        return rows, rows[:, 36:, nz - 1 :: nz]
-    half = rows.shape[0] // 2
-    sent = lax.dynamic_slice_in_dim(rows, (1 - place[1]) * half, half, axis=0)
-    theirs = from_behind(sent, "ta", 1)
-    total = 2 * rows.shape[2]
+    half, part = rows.shape[0] // 2, rows.shape[2]
+    size = lax.axis_size("sa")
+    pairs = [
+        (ta * size + sa, (1 - ta) * size + (sa + 1) % size) for ta in range(2) for sa in range(size)
+    ]
+    start = place[1] * half
+    edge = links[:, 2, :, :, :, nz - 1].reshape(2 * half, 18, part // nz, LANES)
+    below_mine = from_behind(lax.dynamic_slice_in_dim(edge, start, half, axis=0), "sa", 1)
+    below_theirs = lax.ppermute(
+        lax.dynamic_slice_in_dim(edge, half - start, half, axis=0), ("ta", "sa"), pairs
+    )
+    theirs = from_behind(lax.dynamic_slice_in_dim(rows, half - start, half, axis=0), "ta", 1)
     block = ((1,) + rows.shape[1:], lambda t, place: (place[1] * half + t, 0, 0, 0))
+    shape = (half, 54, 2 * part, LANES)
     return call(
         functools.partial(join_links_kernel, nz),
-        (rows, theirs),
-        [(half, 54, total, LANES), (half, 18, total // nz, LANES)],
+        (rows, theirs, below_mine, below_theirs),
+        [shape, shape],
+        rows.size * 4,
         place=place,
         blocks={0: block},
+        scratch=[pltpu.VMEM((1, 18, 2 * part // nz, LANES), F32)],
     )
 
 
@@ -380,9 +382,7 @@
     lows = [from_behind(edges[2 * k], "sa", 1) for k in range(pieces)]
     highs = [from_behind(edges[2 * k + 1], "sa", -1) for k in range(pieces)]
 
-    rows, top_links = join_links(links, place, nz)
-    below = from_behind(top_links, "sa", 1)
-    (back,) = call(functools.partial(back_links_kernel, nz), (rows, below), [rows.shape], rows.size * 4)
+    rows, back = join_links(links, place, nz)
 
     work = count_t * part_n * total * LANES
     fields, older = [every] * pieces, [None] * pieces

time: 128 us -> 122 us (0.953)
  waiting for transfers between devices: 29 us -> 21.8 us
    ppermute x18, waiting for transfers between devices: 29 us -> 21.8 us  [from_behind(): lax.ppermute(x, axis, [(i, (i + by) % devices) for i in range(devices)])]
    ppermute x18, starting transfers between devices: 37.9 us -> 36.3 us  [from_behind(): lax.ppermute(x, axis, [(i, (i + by) % devices) for i in range(devices)])]
    ppermute x0 -> x1, starting transfers between devices: none -> 1.35 us  [join_links(): lax.ppermute(lax.dynamic_slice_in_dim(edge, half - start, half, axis=0),...]
    pallas_call x14 -> x13, Pallas kernels: 40.2 us -> 40.2 us  [call(): pl.pallas_call(kernel, grid_spec=pltpu.PrefetchScalarGridSpec(num_scalar_...]
  transfers between devices with their start and end apart: 18 -> 19, of which waited for: 8 -> 8; matrix products, arithmetic and copies ran while one was open for 0% -> 0% of each run, Pallas kernels for 27% -> 28%
where the time goes in v4:
time: 122 us; the launch traced here: 121 us
  Pallas kernels  55.1 us (45%)
  starting transfers between devices  37.7 us (31%)
  waiting for transfers between devices  21.8 us (18%)
  local copies, waits for them, and re-layouts  5.08 us (4%)
    pallas_call x13, Pallas kernels, call(): pl.pallas_call(kernel, grid_spec=pltpu.PrefetchScalarGridSpec(num_scalar_...  40.2 us
    ppermute x18, starting transfers between devices, from_behind(): lax.ppermute(x, axis, [(i, (i + by) % devices) for i in range(devices)])  36.3 us
    ppermute x18, waiting for transfers between devices, from_behind(): lax.ppermute(x, axis, [(i, (i + by) % devices) for i in range(devices)])  21.8 us
    pallas_call x1, Pallas kernels, sum_blocks(): pl.pallas_call(functools.partial(sum_kernel, groups, size), out_shape=jax...  14.9 us
  transfers between devices with their start and end apart: 19, of which 8 were waited for; matrix products, arithmetic and copies ran while one was open for 0% of the time, Pallas kernels for 28%

profile of v4, /device:TPU:0, one launch (start us, length us, event | category | flops | bytes accessed | tf_op | source)
XLA Modules:
  0.0 121.5 jit_solution(14411613365932137115)
XLA Ops:
  0.6 2.3 %constant_dynamic-slice_fusion.2 = f32[2,54,16,128]{3,2,1,0:T(8,128)} fusion(f32[4,54,16,128]{3,2,1,0:T(8,128)} %bitcast.58, s32[]{:T(128)S(6)} %select_n.11), kind=kLoop, calls=%fused_computation.26 | loop fusion | bytes 1769476 | tf_op jit(solution)/shard_map/dynamic_slice | solution.py:350
  3.6 2.6 %collective-permute-start.1 = (f32[2,18,4,128]{3,2,1,0:T(4,128)S(1)}, f32[2,18,4,128]{3,2,1,0:T(4,128)S(1)}, u32[]{:S(2)}, u32[]{:S(2)}) collective-permute-start(f32[2,18,4,128]{3,2,1,0:T(4,128)S(1)} %get-tuple-element.51), channel_id=1, source_target_pairs={{0,1},{1,2},{2,3},{3,4},{4,5},{5,6},{6,7},{7,0},{8,9},{9,10},{10,1... | collective-permute-start | bytes 221192 | tf_op jit(solution)/shard_map/ppermute | solution.py:19
  6.1 1.4 %collective-permute-start.2 = (f32[2,18,4,128]{3,2,1,0:T(4,128)S(1)}, f32[2,18,4,128]{3,2,1,0:T(4,128)S(1)}, u32[]{:S(2)}, u32[]{:S(2)}) collective-permute-start(f32[2,18,4,128]{3,2,1,0:T(4,128)S(1)} %get-tuple-element.50), channel_id=1, source_target_pairs={{0,9},{1,10},{2,11},{3,12},{4,13},{5,14},{6,15},{7,8},{8,1},{9,2},... | collective-permute-start | bytes 221192 | tf_op jit(solution)/shard_map/ppermute | solution.py:347
  7.6 1.9 %copy-done = f32[2,16,2,3,4,1024]{5,4,3,2,1,0:T(4,128)S(1)} copy-done((f32[2,16,2,3,4,1024]{5,4,3,2,1,0:T(4,128)S(1)}, f32[2,16,2,3,4,1024]{5,4,3,2,1,0:T(4,128)}, u32[]{:S(2)}) %copy-start) | copy-done | bytes 3145752
  10.1 3.3 %collective-permute-start.10 = (f32[2,4,6,8,128]{4,3,2,1,0:T(8,128)S(1)}, f32[2,4,6,8,128]{4,3,2,1,0:T(8,128)S(1)}, u32[]{:S(2)}, u32[]{:S(2)}) collective-permute-start(f32[2,4,6,8,128]{4,3,2,1,0:T(8,128)S(1)} %get-tuple-element.36), channel_id=1, source_target_pairs={{0,7},{1,0},{2,1},{3,2},{4,3},{5,4},{6,5},{7,6},{8,15},{9,8},{10,9... | collective-permute-start | bytes 589832 | tf_op jit(solution)/shard_map/ppermute | solution.py:19
  14.6 3.5 %collective-permute-start.4 = (f32[2,4,6,8,128]{4,3,2,1,0:T(8,128)S(1)}, f32[2,4,6,8,128]{4,3,2,1,0:T(8,128)S(1)}, u32[]{:S(2)}, u32[]{:S(2)}) collective-permute-start(f32[2,4,6,8,128]{4,3,2,1,0:T(8,128)S(1)} %get-tuple-element.27), channel_id=1, source_target_pairs={{0,7},{1,0},{2,1},{3,2},{4,3},{5,4},{6,5},{7,6},{8,15},{9,8},{10,9... | collective-permute-start | bytes 589832 | tf_op jit(solution)/shard_map/ppermute | solution.py:19
  18.2 4.5 %shard_map.41 = (f32[2,54,32,128]{3,2,1,0:T(8,128)S(1)}, f32[2,54,32,128]{3,2,1,0:T(8,128)S(1)}) custom-call(s32[2]{0:T(128)S(1)} %pad_add_fusion.place, f32[4,54,16,128]{3,2,1,0:T(8,128)S(1)} %bitcast.59, f32[2,54,16,128]{3,2,1,0:T(8,128)S(1)} %collective-permute-done.theirs, f32[2,18,4,128]{3,2,1,0:T(4,128)S(1)} %collective-permute-done.1.below_mine, ...), custom_call_target="tpu_custom_call" | custom-call | flops 1769472 | bytes 7077888 | tf_op jit(solution)/shard_map/pallas_call | solution.py:310
  22.7 3.0 %collective-permute-done.9.refs_3_ = f32[2,4,6,8,128]{4,3,2,1,0:T(8,128)S(1)} collective-permute-done((f32[2,4,6,8,128]{4,3,2,1,0:T(8,128)S(1)}, f32[2,4,6,8,128]{4,3,2,1,0:T(8,128)S(1)}, u32[]{:S(2)}, u32[]{:S(2)}) %collective-permute-start.9) | collective-permute-done | bytes 196640 | tf_op jit(solution)/shard_map/ppermute | solution.py:19
  25.7 3.6 %shard_map.46 = (f32[2,4,6,32,128]{4,3,2,1,0:T(8,128)S(1)}, f32[2,4,6,8,128]{4,3,2,1,0:T(8,128)S(1)}, f32[2,4,6,8,128]{4,3,2,1,0:T(8,128)S(1)}) custom-call(s32[2]{0:T(128)S(1)} %pad_add_fusion.place, f32[2,54,32,128]{3,2,1,0:T(8,128)S(1)} %get-tuple-element.24.refs_0_.links, f32[2,54,32,128]{3,2,1,0:T(8,128)S(1)} %get-tuple-element.25.refs_1_, ...), custom_call_target="tpu_custom_call" | custom-call | flops 14745600 | bytes 2359296 | tf_op jit(solution)/shard_map/pallas_call | solution.py:310
  29.4 2.5 %collective-permute-start.11 = (f32[2,4,6,8,128]{4,3,2,1,0:T(8,128)S(1)}, f32[2,4,6,8,128]{4,3,2,1,0:T(8,128)S(1)}, u32[]{:S(2)}, u32[]{:S(2)}) collective-permute-start(f32[2,4,6,8,128]{4,3,2,1,0:T(8,128)S(1)} %get-tuple-element.38), channel_id=1, source_target_pairs={{0,1},{1,2},{2,3},{3,4},{4,5},{5,6},{6,7},{7,0},{8,9},{9,10},{10,1... | collective-permute-start | bytes 589832 | tf_op jit(solution)/shard_map/ppermute | solution.py:19
  31.9 2.7 %collective-permute-start.12 = (f32[2,4,6,8,128]{4,3,2,1,0:T(8,128)S(1)}, f32[2,4,6,8,128]{4,3,2,1,0:T(8,128)S(1)}, u32[]{:S(2)}, u32[]{:S(2)}) collective-permute-start(f32[2,4,6,8,128]{4,3,2,1,0:T(8,128)S(1)} %get-tuple-element.39), channel_id=1, source_target_pairs={{0,7},{1,0},{2,1},{3,2},{4,3},{5,4},{6,5},{7,6},{8,15},{9,8},{10,9... | collective-permute-start | bytes 589832 | tf_op jit(solution)/shard_map/ppermute | solution.py:19
  34.6 3.6 %shard_map.43 = (f32[2,4,6,32,128]{4,3,2,1,0:T(8,128)S(1)}, f32[2,4,6,8,128]{4,3,2,1,0:T(8,128)S(1)}, f32[2,4,6,8,128]{4,3,2,1,0:T(8,128)S(1)}) custom-call(s32[2]{0:T(128)S(1)} %pad_add_fusion.place, f32[2,54,32,128]{3,2,1,0:T(8,128)S(1)} %get-tuple-element.24.refs_0_.links, f32[2,54,32,128]{3,2,1,0:T(8,128)S(1)} %get-tuple-element.25.refs_1_, ...), custom_call_target="tpu_custom_call" | custom-call | flops 14745600 | bytes 2359296 | tf_op jit(solution)/shard_map/pallas_call | solution.py:310
  38.3 4.7 %collective-permute-start.6 = (f32[2,4,6,8,128]{4,3,2,1,0:T(8,128)S(1)}, f32[2,4,6,8,128]{4,3,2,1,0:T(8,128)S(1)}, u32[]{:S(2)}, u32[]{:S(2)}) collective-permute-start(f32[2,4,6,8,128]{4,3,2,1,0:T(8,128)S(1)} %get-tuple-element.30), channel_id=1, source_target_pairs={{0,7},{1,0},{2,1},{3,2},{4,3},{5,4},{6,5},{7,6},{8,15},{9,8},{10,9... | collective-permute-start | bytes 589832 | tf_op jit(solution)/shard_map/ppermute | solution.py:19
  43.0 2.6 %collective-permute-done.11.refs_3_ = f32[2,4,6,8,128]{4,3,2,1,0:T(8,128)S(1)} collective-permute-done((f32[2,4,6,8,128]{4,3,2,1,0:T(8,128)S(1)}, f32[2,4,6,8,128]{4,3,2,1,0:T(8,128)S(1)}, u32[]{:S(2)}, u32[]{:S(2)}) %collective-permute-start.11) | collective-permute-done | bytes 196640 | tf_op jit(solution)/shard_map/ppermute | solution.py:19
  45.6 1.9 %collective-permute-done.12.refs_4_ = f32[2,4,6,8,128]{4,3,2,1,0:T(8,128)S(1)} collective-permute-done((f32[2,4,6,8,128]{4,3,2,1,0:T(8,128)S(1)}, f32[2,4,6,8,128]{4,3,2,1,0:T(8,128)S(1)}, u32[]{:S(2)}, u32[]{:S(2)}) %collective-permute-start.12) | collective-permute-done | bytes 196640 | tf_op jit(solution)/shard_map/ppermute | solution.py:19
  47.5 3.7 %shard_map.47 = (f32[2,4,6,32,128]{4,3,2,1,0:T(8,128)S(1)}, f32[2,4,6,8,128]{4,3,2,1,0:T(8,128)S(1)}, f32[2,4,6,8,128]{4,3,2,1,0:T(8,128)S(1)}) custom-call(s32[2]{0:T(128)S(1)} %pad_add_fusion.place, f32[2,54,32,128]{3,2,1,0:T(8,128)S(1)} %get-tuple-element.24.refs_0_.links, f32[2,54,32,128]{3,2,1,0:T(8,128)S(1)} %get-tuple-element.25.refs_1_, ...), custom_call_target="tpu_custom_call" | custom-call | flops 14745600 | bytes 2359296 | tf_op jit(solution)/shard_map/pallas_call | solution.py:310
  51.9 4.1 %collective-permute-start.14 = (f32[2,4,6,8,128]{4,3,2,1,0:T(8,128)S(1)}, f32[2,4,6,8,128]{4,3,2,1,0:T(8,128)S(1)}, u32[]{:S(2)}, u32[]{:S(2)}) collective-permute-start(f32[2,4,6,8,128]{4,3,2,1,0:T(8,128)S(1)} %get-tuple-element.42), channel_id=1, source_target_pairs={{0,7},{1,0},{2,1},{3,2},{4,3},{5,4},{6,5},{7,6},{8,15},{9,8},{10,9... | collective-permute-start | bytes 589832 | tf_op jit(solution)/shard_map/ppermute | solution.py:19
  56.0 3.7 %shard_map.44 = (f32[2,4,6,32,128]{4,3,2,1,0:T(8,128)S(1)}, f32[2,4,6,8,128]{4,3,2,1,0:T(8,128)S(1)}, f32[2,4,6,8,128]{4,3,2,1,0:T(8,128)S(1)}) custom-call(s32[2]{0:T(128)S(1)} %pad_add_fusion.place, f32[2,54,32,128]{3,2,1,0:T(8,128)S(1)} %get-tuple-element.24.refs_0_.links, f32[2,54,32,128]{3,2,1,0:T(8,128)S(1)} %get-tuple-element.25.refs_1_, ...), custom_call_target="tpu_custom_call" | custom-call | flops 14745600 | bytes 2359296 | tf_op jit(solution)/shard_map/pallas_call | solution.py:310
  59.8 4.7 %collective-permute-start.8 = (f32[2,4,6,8,128]{4,3,2,1,0:T(8,128)S(1)}, f32[2,4,6,8,128]{4,3,2,1,0:T(8,128)S(1)}, u32[]{:S(2)}, u32[]{:S(2)}) collective-permute-start(f32[2,4,6,8,128]{4,3,2,1,0:T(8,128)S(1)} %get-tuple-element.33), channel_id=1, source_target_pairs={{0,7},{1,0},{2,1},{3,2},{4,3},{5,4},{6,5},{7,6},{8,15},{9,8},{10,9... | collective-permute-start | bytes 589832 | tf_op jit(solution)/shard_map/ppermute | solution.py:19
  65.4 4.4 %shard_map.48 = (f32[2,4,6,32,128]{4,3,2,1,0:T(8,128)S(1)}, f32[2,4,6,8,128]{4,3,2,1,0:T(8,128)}, f32[2,4,6,8,128]{4,3,2,1,0:T(8,128)S(1)}) custom-call(s32[2]{0:T(128)S(1)} %pad_add_fusion.place, f32[2,54,32,128]{3,2,1,0:T(8,128)S(1)} %get-tuple-element.24.refs_0_.links, f32[2,54,32,128]{3,2,1,0:T(8,128)S(1)} %get-tuple-element.25.refs_1_, ...), custom_call_target="tpu_custom_call" | custom-call | flops 14745600 | bytes 2359296 | tf_op jit(solution)/shard_map/pallas_call | solution.py:310
  69.8 1.5 %collective-permute-start.18 = (f32[2,4,6,32,128]{4,3,2,1,0:T(8,128)S(1)}, f32[2,4,6,32,128]{4,3,2,1,0:T(8,128)S(1)}, u32[]{:S(2)}, u32[]{:S(2)}) collective-permute-start(f32[2,4,6,32,128]{4,3,2,1,0:T(8,128)S(1)} %get-tuple-element.43.vec.refs_1_.refs_3_), channel_id=1, source_target_pairs={{0,16},{16,0},{1,17},{17,1},{2,18},{18,2},{3,19},{19,3},{4,20},{20... | collective-permute-start | bytes 2359304 | tf_op jit(solution)/shard_map/ppermute | solution.py:19
  71.3 4.4 %shard_map.45 = (f32[2,4,6,32,128]{4,3,2,1,0:T(8,128)S(1)}, f32[2,4,6,8,128]{4,3,2,1,0:T(8,128)}, f32[2,4,6,8,128]{4,3,2,1,0:T(8,128)S(1)}) custom-call(s32[2]{0:T(128)S(1)} %pad_add_fusion.place, f32[2,54,32,128]{3,2,1,0:T(8,128)S(1)} %get-tuple-element.24.refs_0_.links, f32[2,54,32,128]{3,2,1,0:T(8,128)S(1)} %get-tuple-element.25.refs_1_, ...), custom_call_target="tpu_custom_call" | custom-call | flops 14745600 | bytes 2359296 | tf_op jit(solution)/shard_map/pallas_call | solution.py:310
  76.2 2.6 %collective-permute-start.16 = (f32[2,4,6,8,128]{4,3,2,1,0:T(8,128)S(1)}, f32[2,4,6,8,128]{4,3,2,1,0:T(8,128)S(1)}, u32[]{:S(2)}, u32[]{:S(2)}) collective-permute-start(f32[2,4,6,8,128]{4,3,2,1,0:T(8,128)S(1)} %get-tuple-element.45), channel_id=1, source_target_pairs={{0,7},{1,0},{2,1},{3,2},{4,3},{5,4},{6,5},{7,6},{8,15},{9,8},{10,9... | collective-permute-start | bytes 589832 | tf_op jit(solution)/shard_map/ppermute | solution.py:19
  79.9 2.4 %collective-permute-done.16.high = f32[2,4,6,8,128]{4,3,2,1,0:T(8,128)S(1)} collective-permute-done((f32[2,4,6,8,128]{4,3,2,1,0:T(8,128)S(1)}, f32[2,4,6,8,128]{4,3,2,1,0:T(8,128)S(1)}, u32[]{:S(2)}, u32[]{:S(2)}) %collective-permute-start.16) | collective-permute-done | bytes 196640 | tf_op jit(solution)/shard_map/ppermute | solution.py:19
  82.3 1.6 %shard_map.50.refs_5_ = f32[2,4,6,32,128]{4,3,2,1,0:T(8,128)S(1)} custom-call(f32[2,54,32,128]{3,2,1,0:T(8,128)S(1)} %get-tuple-element.24.refs_0_.links, f32[2,4,6,32,128]{4,3,2,1,0:T(8,128)S(1)} %get-tuple-element.43.vec.refs_1_.refs_3_, f32[2,4,6,8,128]{4,3,2,1,0:T(8,128)S(1)} %collective-permute-done.16.high), custom_call_target="tpu_custom_call" | custom-call | flops 7208960 | bytes 1572864 | tf_op jit(solution)/shard_map/pallas_call | solution.py:310
  84.4 1.6 %shard_map.49.refs_4_ = f32[2,4,6,32,128]{4,3,2,1,0:T(8,128)S(1)} custom-call(f32[2,54,32,128]{3,2,1,0:T(8,128)S(1)} %get-tuple-element.24.refs_0_.links, f32[2,4,6,32,128]{4,3,2,1,0:T(8,128)S(1)} %get-tuple-element.34.vec.refs_0_.refs_2_, f32[2,4,6,8,128]{4,3,2,1,0:T(8,128)S(1)} %collective-permute-done.15.high), custom_call_target="tpu_custom_call" | custom-call | flops 7208960 | bytes 1572864 | tf_op jit(solution)/shard_map/pallas_call | solution.py:310
  86.0 2.6 %shard_map.51 = f32[2,16,32]{2,1,0:T(8,128)S(1)} custom-call(f32[2,4,6,32,128]{4,3,2,1,0:T(8,128)S(1)} %get-tuple-element.34.vec.refs_0_.refs_2_, f32[2,4,6,32,128]{4,3,2,1,0:T(8,128)S(1)} %get-tuple-element.43.vec.refs_1_.refs_3_, f32[2,4,6,32,128]{4,3,2,1,0:T(8,128)S(1)} %get-tuple-element.34.vec.refs_0_.refs_2_, ...), custom_call_target="tpu_custom_call" | custom-call | flops 201326592 | bytes 8192 | tf_op jit(solution)/shard_map/pallas_call | solution.py:310
  88.7 1.5 %collective-permute-done.18.refs_1_.refs_3_ = f32[2,4,6,32,128]{4,3,2,1,0:T(8,128)S(1)} collective-permute-done((f32[2,4,6,32,128]{4,3,2,1,0:T(8,128)S(1)}, f32[2,4,6,32,128]{4,3,2,1,0:T(8,128)S(1)}, u32[]{:S(2)}, u32[]{:S(2)}) %collective-permute-start.18) | collective-permute-done | bytes 786464 | tf_op jit(solution)/shard_map/ppermute | solution.py:19
  90.2 8.9 %collective-permute-done.17.refs_0_.refs_2_ = f32[2,4,6,32,128]{4,3,2,1,0:T(8,128)S(1)} collective-permute-done((f32[2,4,6,32,128]{4,3,2,1,0:T(8,128)S(1)}, f32[2,4,6,32,128]{4,3,2,1,0:T(8,128)S(1)}, u32[]{:S(2)}, u32[]{:S(2)}) %collective-permute-start.17) | collective-permute-done | bytes 786464 | tf_op jit(solution)/shard_map/ppermute | solution.py:19
  99.2 2.6 %shard_map.52 = f32[2,16,32]{2,1,0:T(8,128)S(1)} custom-call(f32[2,4,6,32,128]{4,3,2,1,0:T(8,128)S(1)} %collective-permute-done.17.refs_0_.refs_2_, f32[2,4,6,32,128]{4,3,2,1,0:T(8,128)S(1)} %collective-permute-done.18.refs_1_.refs_3_, f32[2,4,6,32,128]{4,3,2,1,0:T(8,128)S(1)} %get-tuple-element.34.vec.refs_0_.refs_2_, ...), custom_call_target="tpu_custom_call" | custom-call | flops 201326592 | bytes 8192 | tf_op jit(solution)/shard_map/pallas_call | solution.py:310
  101.9 14.9 %shard_map.53 = f32[2,16,128]{2,1,0:T(8,128)S(1)} custom-call(f32[16,128]{1,0:T(8,128)S(1)} %reshape.65.mine), custom_call_target="tpu_custom_call" | custom-call | tf_op jit(solution)/shard_map/pallas_call | solution.py:282
  118.5 3.0 %shard_map.54 = f32[2,16,6,32,128]{4,3,2,1,0:T(8,128)} custom-call(s32[2]{0:T(128)S(1)} %pad_add_fusion.place, f32[2,16]{1,0:T(2,128)S(1)} %rsqrt.3.inverse, f32[2,4,6,32,128]{4,3,2,1,0:T(8,128)S(1)} %get-tuple-element.34.vec.refs_0_.refs_2_, f32[2,4,6,32,128]{4,3,2,1,0:T(8,128)S(1)} %get-tuple-element.43.vec.refs_1_.refs_3_, ...), custom_call_target="tpu_custom_call" | custom-call | bytes 6291456 | tf_op jit(solution)/shard_map/pallas_call | solution.py:310
  (46 shorter events, 8.2 us)
Async XLA Ops:
  0.6 2.7 %copy-start.2 = (f32[4,3,2,3,3,4,512]{6,5,4,3,2,1,0:T(4,128)S(1)}, f32[4,3,2,3,3,4,512]{6,5,4,3,2,1,0:T(4,128)}, u32[]{:S(2)}) copy-start(f32[4,3,2,3,3,4,512]{6,5,4,3,2,1,0:T(4,128)} %param.2) | copy-start | bytes 5308420
  2.9 15.3 %collective-permute-start = (f32[2,54,16,128]{3,2,1,0:T(8,128)}, f32[2,54,16,128]{3,2,1,0:T(8,128)S(1)}, u32[]{:S(2)}, u32[]{:S(2)}) collective-permute-start(f32[2,54,16,128]{3,2,1,0:T(8,128)} %constant_dynamic-slice_fusion.2), channel_id=1, source_target_pairs={{0,8},{8,0},{1,9},{9,1},{2,10},{10,2},{3,11},{11,3},{4,12},{12,4},... | collective-permute-start | bytes 2654216 | tf_op jit(solution)/shard_map/ppermute | solution.py:19
  3.6 9.8 %collective-permute-start.1 = (f32[2,18,4,128]{3,2,1,0:T(4,128)S(1)}, f32[2,18,4,128]{3,2,1,0:T(4,128)S(1)}, u32[]{:S(2)}, u32[]{:S(2)}) collective-permute-start(f32[2,18,4,128]{3,2,1,0:T(4,128)S(1)} %get-tuple-element.51), channel_id=1, source_target_pairs={{0,1},{1,2},{2,3},{3,4},{4,5},{5,6},{6,7},{7,0},{8,9},{9,10},{10,1... | collective-permute-start | bytes 221192 | tf_op jit(solution)/shard_map/ppermute | solution.py:19
  6.1 8.5 %collective-permute-start.2 = (f32[2,18,4,128]{3,2,1,0:T(4,128)S(1)}, f32[2,18,4,128]{3,2,1,0:T(4,128)S(1)}, u32[]{:S(2)}, u32[]{:S(2)}) collective-permute-start(f32[2,18,4,128]{3,2,1,0:T(4,128)S(1)} %get-tuple-element.50), channel_id=1, source_target_pairs={{0,9},{1,10},{2,11},{3,12},{4,13},{5,14},{6,15},{7,8},{8,1},{9,2},... | collective-permute-start | bytes 221192 | tf_op jit(solution)/shard_map/ppermute | solution.py:347
  7.6 1.9 %copy-start = (f32[2,16,2,3,4,1024]{5,4,3,2,1,0:T(4,128)S(1)}, f32[2,16,2,3,4,1024]{5,4,3,2,1,0:T(4,128)}, u32[]{:S(2)}) copy-start(f32[2,16,2,3,4,1024]{5,4,3,2,1,0:T(4,128)} %param.3) | copy-start | bytes 9437188
  9.4 16.3 %copy-start.1 = (f32[2,16,2,3,4,1024]{5,4,3,2,1,0:T(4,128)S(1)}, f32[2,16,2,3,4,1024]{5,4,3,2,1,0:T(4,128)}, u32[]{:S(2)}) copy-start(f32[2,16,2,3,4,1024]{5,4,3,2,1,0:T(4,128)} %param.3) | copy-start | bytes 9437188
  10.1 12.5 %collective-permute-start.10 = (f32[2,4,6,8,128]{4,3,2,1,0:T(8,128)S(1)}, f32[2,4,6,8,128]{4,3,2,1,0:T(8,128)S(1)}, u32[]{:S(2)}, u32[]{:S(2)}) collective-permute-start(f32[2,4,6,8,128]{4,3,2,1,0:T(8,128)S(1)} %get-tuple-element.36), channel_id=1, source_target_pairs={{0,7},{1,0},{2,1},{3,2},{4,3},{5,4},{6,5},{7,6},{8,15},{9,8},{10,9... | collective-permute-start | bytes 589832 | tf_op jit(solution)/shard_map/ppermute | solution.py:19
  13.4 12.3 %collective-permute-start.9 = (f32[2,4,6,8,128]{4,3,2,1,0:T(8,128)S(1)}, f32[2,4,6,8,128]{4,3,2,1,0:T(8,128)S(1)}, u32[]{:S(2)}, u32[]{:S(2)}) collective-permute-start(f32[2,4,6,8,128]{4,3,2,1,0:T(8,128)S(1)} %get-tuple-element.35), channel_id=1, source_target_pairs={{0,1},{1,2},{2,3},{3,4},{4,5},{5,6},{6,7},{7,0},{8,9},{9,10},{10,1... | collective-permute-start | bytes 589832 | tf_op jit(solution)/shard_map/ppermute | solution.py:19
  13.4 21.2 %collective-permute-start.3 = (f32[2,4,6,8,128]{4,3,2,1,0:T(8,128)S(1)}, f32[2,4,6,8,128]{4,3,2,1,0:T(8,128)S(1)}, u32[]{:S(2)}, u32[]{:S(2)}) collective-permute-start(f32[2,4,6,8,128]{4,3,2,1,0:T(8,128)S(1)} %get-tuple-element.26), channel_id=1, source_target_pairs={{0,1},{1,2},{2,3},{3,4},{4,5},{5,6},{6,7},{7,0},{8,9},{9,10},{10,1... | collective-permute-start | bytes 589832 | tf_op jit(solution)/shard_map/ppermute | solution.py:19
  14.6 19.9 %collective-permute-start.4 = (f32[2,4,6,8,128]{4,3,2,1,0:T(8,128)S(1)}, f32[2,4,6,8,128]{4,3,2,1,0:T(8,128)S(1)}, u32[]{:S(2)}, u32[]{:S(2)}) collective-permute-start(f32[2,4,6,8,128]{4,3,2,1,0:T(8,128)S(1)} %get-tuple-element.27), channel_id=1, source_target_pairs={{0,7},{1,0},{2,1},{3,2},{4,3},{5,4},{6,5},{7,6},{8,15},{9,8},{10,9... | collective-permute-start | bytes 589832 | tf_op jit(solution)/shard_map/ppermute | solution.py:19
  29.4 16.2 %collective-permute-start.11 = (f32[2,4,6,8,128]{4,3,2,1,0:T(8,128)S(1)}, f32[2,4,6,8,128]{4,3,2,1,0:T(8,128)S(1)}, u32[]{:S(2)}, u32[]{:S(2)}) collective-permute-start(f32[2,4,6,8,128]{4,3,2,1,0:T(8,128)S(1)} %get-tuple-element.38), channel_id=1, source_target_pairs={{0,1},{1,2},{2,3},{3,4},{4,5},{5,6},{6,7},{7,0},{8,9},{9,10},{10,1... | collective-permute-start | bytes 589832 | tf_op jit(solution)/shard_map/ppermute | solution.py:19
  31.9 15.6 %collective-permute-start.12 = (f32[2,4,6,8,128]{4,3,2,1,0:T(8,128)S(1)}, f32[2,4,6,8,128]{4,3,2,1,0:T(8,128)S(1)}, u32[]{:S(2)}, u32[]{:S(2)}) collective-permute-start(f32[2,4,6,8,128]{4,3,2,1,0:T(8,128)S(1)} %get-tuple-element.39), channel_id=1, source_target_pairs={{0,7},{1,0},{2,1},{3,2},{4,3},{5,4},{6,5},{7,6},{8,15},{9,8},{10,9... | collective-permute-start | bytes 589832 | tf_op jit(solution)/shard_map/ppermute | solution.py:19
  38.2 17.8 %collective-permute-start.5 = (f32[2,4,6,8,128]{4,3,2,1,0:T(8,128)S(1)}, f32[2,4,6,8,128]{4,3,2,1,0:T(8,128)S(1)}, u32[]{:S(2)}, u32[]{:S(2)}) collective-permute-start(f32[2,4,6,8,128]{4,3,2,1,0:T(8,128)S(1)} %get-tuple-element.29), channel_id=1, source_target_pairs={{0,1},{1,2},{2,3},{3,4},{4,5},{5,6},{6,7},{7,0},{8,9},{9,10},{10,1... | collective-permute-start | bytes 589832 | tf_op jit(solution)/shard_map/ppermute | solution.py:19
  38.3 17.7 %collective-permute-start.6 = (f32[2,4,6,8,128]{4,3,2,1,0:T(8,128)S(1)}, f32[2,4,6,8,128]{4,3,2,1,0:T(8,128)S(1)}, u32[]{:S(2)}, u32[]{:S(2)}) collective-permute-start(f32[2,4,6,8,128]{4,3,2,1,0:T(8,128)S(1)} %get-tuple-element.30), channel_id=1, source_target_pairs={{0,7},{1,0},{2,1},{3,2},{4,3},{5,4},{6,5},{7,6},{8,15},{9,8},{10,9... | collective-permute-start | bytes 589832 | tf_op jit(solution)/shard_map/ppermute | solution.py:19
  51.2 14.2 %collective-permute-start.13 = (f32[2,4,6,8,128]{4,3,2,1,0:T(8,128)S(1)}, f32[2,4,6,8,128]{4,3,2,1,0:T(8,128)S(1)}, u32[]{:S(2)}, u32[]{:S(2)}) collective-permute-start(f32[2,4,6,8,128]{4,3,2,1,0:T(8,128)S(1)} %get-tuple-element.41), channel_id=1, source_target_pairs={{0,1},{1,2},{2,3},{3,4},{4,5},{5,6},{6,7},{7,0},{8,9},{9,10},{10,1... | collective-permute-start | bytes 589832 | tf_op jit(solution)/shard_map/ppermute | solution.py:19
  51.9 13.5 %collective-permute-start.14 = (f32[2,4,6,8,128]{4,3,2,1,0:T(8,128)S(1)}, f32[2,4,6,8,128]{4,3,2,1,0:T(8,128)S(1)}, u32[]{:S(2)}, u32[]{:S(2)}) collective-permute-start(f32[2,4,6,8,128]{4,3,2,1,0:T(8,128)S(1)} %get-tuple-element.42), channel_id=1, source_target_pairs={{0,7},{1,0},{2,1},{3,2},{4,3},{5,4},{6,5},{7,6},{8,15},{9,8},{10,9... | collective-permute-start | bytes 589832 | tf_op jit(solution)/shard_map/ppermute | solution.py:19
  59.7 11.5 %collective-permute-start.7 = (f32[2,4,6,8,128]{4,3,2,1,0:T(8,128)S(1)}, f32[2,4,6,8,128]{4,3,2,1,0:T(8,128)S(1)}, u32[]{:S(2)}, u32[]{:S(2)}) collective-permute-start(f32[2,4,6,8,128]{4,3,2,1,0:T(8,128)S(1)} %get-tuple-element.32), channel_id=1, source_target_pairs={{0,1},{1,2},{2,3},{3,4},{4,5},{5,6},{6,7},{7,0},{8,9},{9,10},{10,1... | collective-permute-start | bytes 589832 | tf_op jit(solution)/shard_map/ppermute | solution.py:19
  59.8 11.5 %collective-permute-start.8 = (f32[2,4,6,8,128]{4,3,2,1,0:T(8,128)S(1)}, f32[2,4,6,8,128]{4,3,2,1,0:T(8,128)S(1)}, u32[]{:S(2)}, u32[]{:S(2)}) collective-permute-start(f32[2,4,6,8,128]{4,3,2,1,0:T(8,128)S(1)} %get-tuple-element.33), channel_id=1, source_target_pairs={{0,7},{1,0},{2,1},{3,2},{4,3},{5,4},{6,5},{7,6},{8,15},{9,8},{10,9... | collective-permute-start | bytes 589832 | tf_op jit(solution)/shard_map/ppermute | solution.py:19
  69.8 20.5 %collective-permute-start.18 = (f32[2,4,6,32,128]{4,3,2,1,0:T(8,128)S(1)}, f32[2,4,6,32,128]{4,3,2,1,0:T(8,128)S(1)}, u32[]{:S(2)}, u32[]{:S(2)}) collective-permute-start(f32[2,4,6,32,128]{4,3,2,1,0:T(8,128)S(1)} %get-tuple-element.43.vec.refs_1_.refs_3_), channel_id=1, source_target_pairs={{0,16},{16,0},{1,17},{17,1},{2,18},{18,2},{3,19},{19,3},{4,20},{20... | collective-permute-start | bytes 2359304 | tf_op jit(solution)/shard_map/ppermute | solution.py:19
  75.6 23.5 %collective-permute-start.17 = (f32[2,4,6,32,128]{4,3,2,1,0:T(8,128)S(1)}, f32[2,4,6,32,128]{4,3,2,1,0:T(8,128)S(1)}, u32[]{:S(2)}, u32[]{:S(2)}) collective-permute-start(f32[2,4,6,32,128]{4,3,2,1,0:T(8,128)S(1)} %get-tuple-element.34.vec.refs_0_.refs_2_), channel_id=1, source_target_pairs={{0,16},{16,0},{1,17},{17,1},{2,18},{18,2},{3,19},{19,3},{4,20},{20... | collective-permute-start | bytes 2359304 | tf_op jit(solution)/shard_map/ppermute | solution.py:19
  76.2 6.1 %collective-permute-start.16 = (f32[2,4,6,8,128]{4,3,2,1,0:T(8,128)S(1)}, f32[2,4,6,8,128]{4,3,2,1,0:T(8,128)S(1)}, u32[]{:S(2)}, u32[]{:S(2)}) collective-permute-start(f32[2,4,6,8,128]{4,3,2,1,0:T(8,128)S(1)} %get-tuple-element.45), channel_id=1, source_target_pairs={{0,7},{1,0},{2,1},{3,2},{4,3},{5,4},{6,5},{7,6},{8,15},{9,8},{10,9... | collective-permute-start | bytes 589832 | tf_op jit(solution)/shard_map/ppermute | solution.py:19
  78.7 5.7 %collective-permute-start.15 = (f32[2,4,6,8,128]{4,3,2,1,0:T(8,128)S(1)}, f32[2,4,6,8,128]{4,3,2,1,0:T(8,128)S(1)}, u32[]{:S(2)}, u32[]{:S(2)}) collective-permute-start(f32[2,4,6,8,128]{4,3,2,1,0:T(8,128)S(1)} %get-tuple-element.44), channel_id=1, source_target_pairs={{0,7},{1,0},{2,1},{3,2},{4,3},{5,4},{6,5},{7,6},{8,15},{9,8},{10,9... | collective-permute-start | bytes 589832 | tf_op jit(solution)/shard_map/ppermute | solution.py:19

commit v5 on v4

--- a/solution.py
+++ b/solution.py
@@ -379,6 +379,7 @@
     edges = call(
         functools.partial(edges_kernel, nz, pieces), (every,), [edge] * (2 * pieces), place=place, blocks={0: own_block}
     )
+    links, edges = lax.optimization_barrier((links, edges))
     lows = [from_behind(edges[2 * k], "sa", 1) for k in range(pieces)]
     highs = [from_behind(edges[2 * k + 1], "sa", -1) for k in range(pieces)]
 

time: 122 us -> 127 us (1.041)
  local copies, waits for them, and re-layouts: 5.08 us -> 9.45 us
  waiting for transfers between devices: 21.8 us -> 26 us
  Pallas kernels: 55.1 us -> 51.9 us
    pallas_call x1, Pallas kernels: 14.9 us -> 10.7 us  [sum_blocks(): pl.pallas_call(functools.partial(sum_kernel, groups, size), out_shape=jax...]
    ppermute x18, waiting for transfers between devices: 21.8 us -> 24.6 us  [from_behind(): lax.ppermute(x, axis, [(i, (i + by) % devices) for i in range(devices)])]
    unnamed x6 -> x12, local copies, waits for them, and re-layouts: 1.9 us -> 4.71 us
    slice x1, local copies, waits for them, and re-layouts: 0.15 us -> 2.1 us  [join_links(): edge = links[:, 2, :, :, :, nz - 1].reshape(2 * half, 18, part // nz, LANES)]
    ppermute x1, waiting for transfers between devices: 0.01 us -> 1.33 us  [join_links(): lax.ppermute(lax.dynamic_slice_in_dim(edge, half - start, half, axis=0),...]
    dynamic_slice x1, local copies, waits for them, and re-layouts: 2.27 us -> 0.97 us  [join_links(): lax.dynamic_slice_in_dim(rows, half - start, half, axis=0)]
  transfers between devices with their start and end apart: 19 -> 19, of which waited for: 8 -> 8; matrix products, arithmetic and copies ran while one was open for 0% -> 2% of each run, Pallas kernels for 28% -> 28%
where the time goes in v5:
time: 127 us; the launch traced here: 126 us
  Pallas kernels  51.9 us (41%)
  starting transfers between devices  37.2 us (29%)
  waiting for transfers between devices  26 us (20%)
  local copies, waits for them, and re-layouts  9.45 us (7%)
    pallas_call x13, Pallas kernels, call(): pl.pallas_call(kernel, grid_spec=pltpu.PrefetchScalarGridSpec(num_scalar_...  41.2 us
    ppermute x18, starting transfers between devices, from_behind(): lax.ppermute(x, axis, [(i, (i + by) % devices) for i in range(devices)])  35.8 us
    ppermute x18, waiting for transfers between devices, from_behind(): lax.ppermute(x, axis, [(i, (i + by) % devices) for i in range(devices)])  24.6 us
    pallas_call x1, Pallas kernels, sum_blocks(): pl.pallas_call(functools.partial(sum_kernel, groups, size), out_shape=jax...  10.7 us
    unnamed x12, local copies, waits for them, and re-layouts  4.71 us
  transfers between devices with their start and end apart: 19, of which 8 were waited for; matrix products, arithmetic and copies ran while one was open for 2% of the time, Pallas kernels for 28%

profile of v5, /device:TPU:0, one launch (start us, length us, event | category | flops | bytes accessed | tf_op | source)
XLA Modules:
  0.0 126.5 jit_solution(5794691156811175627)
XLA Ops:
  0.7 1.9 %copy-done = f32[2,16,2,3,4,1024]{5,4,3,2,1,0:T(4,128)S(1)} copy-done((f32[2,16,2,3,4,1024]{5,4,3,2,1,0:T(4,128)S(1)}, f32[2,16,2,3,4,1024]{5,4,3,2,1,0:T(4,128)}, u32[]{:S(2)}) %copy-start) | copy-done | bytes 3145752
  6.1 2.1 %slice.48 = f32[4,1,2,3,3,1,512]{6,5,4,3,2,1,0:T(1,128)} slice(f32[4,3,2,3,3,4,512]{6,5,4,3,2,1,0:T(4,128)} %param.2), slice={[0:4], [2:3], [0:2], [0:3], [0:3], [3:4], [0:512]} | slice | bytes 294912 | tf_op jit(solution)/shard_map/slice | solution.py:345
  9.1 2.5 %collective-permute-start.1 = (f32[2,18,4,128]{3,2,1,0:T(4,128)S(1)}, f32[2,18,4,128]{3,2,1,0:T(4,128)S(1)}, u32[]{:S(2)}, u32[]{:S(2)}) collective-permute-start(f32[2,18,4,128]{3,2,1,0:T(4,128)S(1)} %get-tuple-element.61), channel_id=1, source_target_pairs={{0,1},{1,2},{2,3},{3,4},{4,5},{5,6},{6,7},{7,0},{8,9},{9,10},{10,1... | collective-permute-start | bytes 221192 | tf_op jit(solution)/shard_map/ppermute | solution.py:19
  13.1 3.2 %collective-permute-start.10 = (f32[2,4,6,8,128]{4,3,2,1,0:T(8,128)}, f32[2,4,6,8,128]{4,3,2,1,0:T(8,128)S(1)}, u32[]{:S(2)}, u32[]{:S(2)}) collective-permute-start(f32[2,4,6,8,128]{4,3,2,1,0:T(8,128)} %copy-done.5), channel_id=1, source_target_pairs={{0,7},{1,0},{2,1},{3,2},{4,3},{5,4},{6,5},{7,6},{8,15},{9,8},{10,9... | collective-permute-start | bytes 589832 | tf_op jit(solution)/shard_map/ppermute | solution.py:19
  16.3 1.6 %collective-permute-done.1.below_mine = f32[2,18,4,128]{3,2,1,0:T(4,128)S(1)} collective-permute-done((f32[2,18,4,128]{3,2,1,0:T(4,128)S(1)}, f32[2,18,4,128]{3,2,1,0:T(4,128)S(1)}, u32[]{:S(2)}, u32[]{:S(2)}) %collective-permute-start.1) | collective-permute-done | bytes 73760 | tf_op jit(solution)/shard_map/ppermute | solution.py:19
  19.2 3.4 %collective-permute-start.4 = (f32[2,4,6,8,128]{4,3,2,1,0:T(8,128)S(1)}, f32[2,4,6,8,128]{4,3,2,1,0:T(8,128)S(1)}, u32[]{:S(2)}, u32[]{:S(2)}) collective-permute-start(f32[2,4,6,8,128]{4,3,2,1,0:T(8,128)S(1)} %get-tuple-element.37), channel_id=1, source_target_pairs={{0,7},{1,0},{2,1},{3,2},{4,3},{5,4},{6,5},{7,6},{8,15},{9,8},{10,9... | collective-permute-start | bytes 589832 | tf_op jit(solution)/shard_map/ppermute | solution.py:19
  22.6 1.5 %copy-done.3 = f32[4,3,2,3,3,4,512]{6,5,4,3,2,1,0:T(4,128)S(1)} copy-done((f32[4,3,2,3,3,4,512]{6,5,4,3,2,1,0:T(4,128)S(1)}, f32[4,3,2,3,3,4,512]{6,5,4,3,2,1,0:T(4,128)}, u32[]{:S(2)}) %copy-start.3) | copy-done | bytes 1769496
  24.1 5.5 %shard_map.42 = (f32[2,54,32,128]{3,2,1,0:T(8,128)S(1)}, f32[2,54,32,128]{3,2,1,0:T(8,128)S(1)}) custom-call(s32[2]{0:T(128)S(1)} %pad_add_fusion.place, f32[4,54,16,128]{3,2,1,0:T(8,128)S(1)} %bitcast.59, f32[2,54,16,128]{3,2,1,0:T(8,128)} %collective-permute-done.theirs, f32[2,18,4,128]{3,2,1,0:T(4,128)S(1)} %collective-permute-done.1.below_mine, ...), custom_call_target="tpu_custom_call" | custom-call | flops 1769472 | bytes 7077888 | tf_op jit(solution)/shard_map/pallas_call | solution.py:310
  29.5 2.5 %collective-permute-done.10.refs_4_ = f32[2,4,6,8,128]{4,3,2,1,0:T(8,128)S(1)} collective-permute-done((f32[2,4,6,8,128]{4,3,2,1,0:T(8,128)}, f32[2,4,6,8,128]{4,3,2,1,0:T(8,128)S(1)}, u32[]{:S(2)}, u32[]{:S(2)}) %collective-permute-start.10) | collective-permute-done | bytes 196640 | tf_op jit(solution)/shard_map/ppermute | solution.py:19
  32.0 3.7 %shard_map.46 = (f32[2,4,6,32,128]{4,3,2,1,0:T(8,128)S(1)}, f32[2,4,6,8,128]{4,3,2,1,0:T(8,128)S(1)}, f32[2,4,6,8,128]{4,3,2,1,0:T(8,128)S(1)}) custom-call(s32[2]{0:T(128)S(1)} %pad_add_fusion.place, f32[2,54,32,128]{3,2,1,0:T(8,128)S(1)} %get-tuple-element.34.refs_0_.links, f32[2,54,32,128]{3,2,1,0:T(8,128)S(1)} %get-tuple-element.35.refs_1_, ...), custom_call_target="tpu_custom_call" | custom-call | flops 14745600 | bytes 2359296 | tf_op jit(solution)/shard_map/pallas_call | solution.py:310
  35.8 4.7 %collective-permute-start.12 = (f32[2,4,6,8,128]{4,3,2,1,0:T(8,128)S(1)}, f32[2,4,6,8,128]{4,3,2,1,0:T(8,128)S(1)}, u32[]{:S(2)}, u32[]{:S(2)}) collective-permute-start(f32[2,4,6,8,128]{4,3,2,1,0:T(8,128)S(1)} %get-tuple-element.49), channel_id=1, source_target_pairs={{0,7},{1,0},{2,1},{3,2},{4,3},{5,4},{6,5},{7,6},{8,15},{9,8},{10,9... | collective-permute-start | bytes 589832 | tf_op jit(solution)/shard_map/ppermute | solution.py:19
  40.5 3.7 %shard_map.43 = (f32[2,4,6,32,128]{4,3,2,1,0:T(8,128)S(1)}, f32[2,4,6,8,128]{4,3,2,1,0:T(8,128)S(1)}, f32[2,4,6,8,128]{4,3,2,1,0:T(8,128)S(1)}) custom-call(s32[2]{0:T(128)S(1)} %pad_add_fusion.place, f32[2,54,32,128]{3,2,1,0:T(8,128)S(1)} %get-tuple-element.34.refs_0_.links, f32[2,54,32,128]{3,2,1,0:T(8,128)S(1)} %get-tuple-element.35.refs_1_, ...), custom_call_target="tpu_custom_call" | custom-call | flops 14745600 | bytes 2359296 | tf_op jit(solution)/shard_map/pallas_call | solution.py:310
  44.2 4.7 %collective-permute-start.6 = (f32[2,4,6,8,128]{4,3,2,1,0:T(8,128)S(1)}, f32[2,4,6,8,128]{4,3,2,1,0:T(8,128)S(1)}, u32[]{:S(2)}, u32[]{:S(2)}) collective-permute-start(f32[2,4,6,8,128]{4,3,2,1,0:T(8,128)S(1)} %get-tuple-element.40), channel_id=1, source_target_pairs={{0,7},{1,0},{2,1},{3,2},{4,3},{5,4},{6,5},{7,6},{8,15},{9,8},{10,9... | collective-permute-start | bytes 589832 | tf_op jit(solution)/shard_map/ppermute | solution.py:19
  49.1 3.7 %shard_map.47 = (f32[2,4,6,32,128]{4,3,2,1,0:T(8,128)S(1)}, f32[2,4,6,8,128]{4,3,2,1,0:T(8,128)S(1)}, f32[2,4,6,8,128]{4,3,2,1,0:T(8,128)S(1)}) custom-call(s32[2]{0:T(128)S(1)} %pad_add_fusion.place, f32[2,54,32,128]{3,2,1,0:T(8,128)S(1)} %get-tuple-element.34.refs_0_.links, f32[2,54,32,128]{3,2,1,0:T(8,128)S(1)} %get-tuple-element.35.refs_1_, ...), custom_call_target="tpu_custom_call" | custom-call | flops 14745600 | bytes 2359296 | tf_op jit(solution)/shard_map/pallas_call | solution.py:310
  52.8 2.5 %collective-permute-start.13 = (f32[2,4,6,8,128]{4,3,2,1,0:T(8,128)S(1)}, f32[2,4,6,8,128]{4,3,2,1,0:T(8,128)S(1)}, u32[]{:S(2)}, u32[]{:S(2)}) collective-permute-start(f32[2,4,6,8,128]{4,3,2,1,0:T(8,128)S(1)} %get-tuple-element.51), channel_id=1, source_target_pairs={{0,1},{1,2},{2,3},{3,4},{4,5},{5,6},{6,7},{7,0},{8,9},{9,10},{10,1... | collective-permute-start | bytes 589832 | tf_op jit(solution)/shard_map/ppermute | solution.py:19
  55.3 2.2 %collective-permute-start.14 = (f32[2,4,6,8,128]{4,3,2,1,0:T(8,128)S(1)}, f32[2,4,6,8,128]{4,3,2,1,0:T(8,128)S(1)}, u32[]{:S(2)}, u32[]{:S(2)}) collective-permute-start(f32[2,4,6,8,128]{4,3,2,1,0:T(8,128)S(1)} %get-tuple-element.52), channel_id=1, source_target_pairs={{0,7},{1,0},{2,1},{3,2},{4,3},{5,4},{6,5},{7,6},{8,15},{9,8},{10,9... | collective-permute-start | bytes 589832 | tf_op jit(solution)/shard_map/ppermute | solution.py:19
  57.6 3.7 %shard_map.44 = (f32[2,4,6,32,128]{4,3,2,1,0:T(8,128)S(1)}, f32[2,4,6,8,128]{4,3,2,1,0:T(8,128)S(1)}, f32[2,4,6,8,128]{4,3,2,1,0:T(8,128)S(1)}) custom-call(s32[2]{0:T(128)S(1)} %pad_add_fusion.place, f32[2,54,32,128]{3,2,1,0:T(8,128)S(1)} %get-tuple-element.34.refs_0_.links, f32[2,54,32,128]{3,2,1,0:T(8,128)S(1)} %get-tuple-element.35.refs_1_, ...), custom_call_target="tpu_custom_call" | custom-call | flops 14745600 | bytes 2359296 | tf_op jit(solution)/shard_map/pallas_call | solution.py:310
  61.4 4.7 %collective-permute-start.8 = (f32[2,4,6,8,128]{4,3,2,1,0:T(8,128)S(1)}, f32[2,4,6,8,128]{4,3,2,1,0:T(8,128)S(1)}, u32[]{:S(2)}, u32[]{:S(2)}) collective-permute-start(f32[2,4,6,8,128]{4,3,2,1,0:T(8,128)S(1)} %get-tuple-element.43), channel_id=1, source_target_pairs={{0,7},{1,0},{2,1},{3,2},{4,3},{5,4},{6,5},{7,6},{8,15},{9,8},{10,9... | collective-permute-start | bytes 589832 | tf_op jit(solution)/shard_map/ppermute | solution.py:19
  66.1 3.8 %collective-permute-done.14.refs_4_ = f32[2,4,6,8,128]{4,3,2,1,0:T(8,128)S(1)} collective-permute-done((f32[2,4,6,8,128]{4,3,2,1,0:T(8,128)S(1)}, f32[2,4,6,8,128]{4,3,2,1,0:T(8,128)S(1)}, u32[]{:S(2)}, u32[]{:S(2)}) %collective-permute-start.14) | collective-permute-done | bytes 196640 | tf_op jit(solution)/shard_map/ppermute | solution.py:19
  69.9 4.4 %shard_map.48 = (f32[2,4,6,32,128]{4,3,2,1,0:T(8,128)S(1)}, f32[2,4,6,8,128]{4,3,2,1,0:T(8,128)}, f32[2,4,6,8,128]{4,3,2,1,0:T(8,128)S(1)}) custom-call(s32[2]{0:T(128)S(1)} %pad_add_fusion.place, f32[2,54,32,128]{3,2,1,0:T(8,128)S(1)} %get-tuple-element.34.refs_0_.links, f32[2,54,32,128]{3,2,1,0:T(8,128)S(1)} %get-tuple-element.35.refs_1_, ...), custom_call_target="tpu_custom_call" | custom-call | flops 14745600 | bytes 2359296 | tf_op jit(solution)/shard_map/pallas_call | solution.py:310
  74.2 1.5 %collective-permute-start.18 = (f32[2,4,6,32,128]{4,3,2,1,0:T(8,128)S(1)}, f32[2,4,6,32,128]{4,3,2,1,0:T(8,128)S(1)}, u32[]{:S(2)}, u32[]{:S(2)}) collective-permute-start(f32[2,4,6,32,128]{4,3,2,1,0:T(8,128)S(1)} %get-tuple-element.53.vec.refs_1_.refs_3_), channel_id=1, source_target_pairs={{0,16},{16,0},{1,17},{17,1},{2,18},{18,2},{3,19},{19,3},{4,20},{20... | collective-permute-start | bytes 2359304 | tf_op jit(solution)/shard_map/ppermute | solution.py:19
  75.7 4.4 %shard_map.45 = (f32[2,4,6,32,128]{4,3,2,1,0:T(8,128)S(1)}, f32[2,4,6,8,128]{4,3,2,1,0:T(8,128)}, f32[2,4,6,8,128]{4,3,2,1,0:T(8,128)S(1)}) custom-call(s32[2]{0:T(128)S(1)} %pad_add_fusion.place, f32[2,54,32,128]{3,2,1,0:T(8,128)S(1)} %get-tuple-element.34.refs_0_.links, f32[2,54,32,128]{3,2,1,0:T(8,128)S(1)} %get-tuple-element.35.refs_1_, ...), custom_call_target="tpu_custom_call" | custom-call | flops 14745600 | bytes 2359296 | tf_op jit(solution)/shard_map/pallas_call | solution.py:310
  80.6 2.6 %collective-permute-start.16 = (f32[2,4,6,8,128]{4,3,2,1,0:T(8,128)S(1)}, f32[2,4,6,8,128]{4,3,2,1,0:T(8,128)S(1)}, u32[]{:S(2)}, u32[]{:S(2)}) collective-permute-start(f32[2,4,6,8,128]{4,3,2,1,0:T(8,128)S(1)} %get-tuple-element.55), channel_id=1, source_target_pairs={{0,7},{1,0},{2,1},{3,2},{4,3},{5,4},{6,5},{7,6},{8,15},{9,8},{10,9... | collective-permute-start | bytes 589832 | tf_op jit(solution)/shard_map/ppermute | solution.py:19
  83.3 2.5 %collective-permute-start.15 = (f32[2,4,6,8,128]{4,3,2,1,0:T(8,128)S(1)}, f32[2,4,6,8,128]{4,3,2,1,0:T(8,128)S(1)}, u32[]{:S(2)}, u32[]{:S(2)}) collective-permute-start(f32[2,4,6,8,128]{4,3,2,1,0:T(8,128)S(1)} %get-tuple-element.54), channel_id=1, source_target_pairs={{0,7},{1,0},{2,1},{3,2},{4,3},{5,4},{6,5},{7,6},{8,15},{9,8},{10,9... | collective-permute-start | bytes 589832 | tf_op jit(solution)/shard_map/ppermute | solution.py:19
  85.8 2.7 %collective-permute-done.16.high = f32[2,4,6,8,128]{4,3,2,1,0:T(8,128)S(1)} collective-permute-done((f32[2,4,6,8,128]{4,3,2,1,0:T(8,128)S(1)}, f32[2,4,6,8,128]{4,3,2,1,0:T(8,128)S(1)}, u32[]{:S(2)}, u32[]{:S(2)}) %collective-permute-start.16) | collective-permute-done | bytes 196640 | tf_op jit(solution)/shard_map/ppermute | solution.py:19
  88.5 1.6 %shard_map.50.refs_5_ = f32[2,4,6,32,128]{4,3,2,1,0:T(8,128)S(1)} custom-call(f32[2,54,32,128]{3,2,1,0:T(8,128)S(1)} %get-tuple-element.34.refs_0_.links, f32[2,4,6,32,128]{4,3,2,1,0:T(8,128)S(1)} %get-tuple-element.53.vec.refs_1_.refs_3_, f32[2,4,6,8,128]{4,3,2,1,0:T(8,128)S(1)} %collective-permute-done.16.high), custom_call_target="tpu_custom_call" | custom-call | flops 7208960 | bytes 1572864 | tf_op jit(solution)/shard_map/pallas_call | solution.py:310
  90.6 1.6 %shard_map.49.refs_4_ = f32[2,4,6,32,128]{4,3,2,1,0:T(8,128)S(1)} custom-call(f32[2,54,32,128]{3,2,1,0:T(8,128)S(1)} %get-tuple-element.34.refs_0_.links, f32[2,4,6,32,128]{4,3,2,1,0:T(8,128)S(1)} %get-tuple-element.44.vec.refs_0_.refs_2_, f32[2,4,6,8,128]{4,3,2,1,0:T(8,128)S(1)} %collective-permute-done.15.high), custom_call_target="tpu_custom_call" | custom-call | flops 7208960 | bytes 1572864 | tf_op jit(solution)/shard_map/pallas_call | solution.py:310
  92.2 2.7 %shard_map.51 = f32[2,16,32]{2,1,0:T(8,128)S(1)} custom-call(f32[2,4,6,32,128]{4,3,2,1,0:T(8,128)S(1)} %get-tuple-element.44.vec.refs_0_.refs_2_, f32[2,4,6,32,128]{4,3,2,1,0:T(8,128)S(1)} %get-tuple-element.53.vec.refs_1_.refs_3_, f32[2,4,6,32,128]{4,3,2,1,0:T(8,128)S(1)} %get-tuple-element.44.vec.refs_0_.refs_2_, ...), custom_call_target="tpu_custom_call" | custom-call | flops 201326592 | bytes 8192 | tf_op jit(solution)/shard_map/pallas_call | solution.py:310
  94.9 13.4 %collective-permute-done.17.refs_0_.refs_2_ = f32[2,4,6,32,128]{4,3,2,1,0:T(8,128)S(1)} collective-permute-done((f32[2,4,6,32,128]{4,3,2,1,0:T(8,128)S(1)}, f32[2,4,6,32,128]{4,3,2,1,0:T(8,128)S(1)}, u32[]{:S(2)}, u32[]{:S(2)}) %collective-permute-start.17) | collective-permute-done | bytes 786464 | tf_op jit(solution)/shard_map/ppermute | solution.py:19
  108.3 2.7 %shard_map.52 = f32[2,16,32]{2,1,0:T(8,128)S(1)} custom-call(f32[2,4,6,32,128]{4,3,2,1,0:T(8,128)S(1)} %collective-permute-done.17.refs_0_.refs_2_, f32[2,4,6,32,128]{4,3,2,1,0:T(8,128)S(1)} %collective-permute-done.18.refs_1_.refs_3_, f32[2,4,6,32,128]{4,3,2,1,0:T(8,128)S(1)} %get-tuple-element.44.vec.refs_0_.refs_2_, ...), custom_call_target="tpu_custom_call" | custom-call | flops 201326592 | bytes 8192 | tf_op jit(solution)/shard_map/pallas_call | solution.py:310
  111.1 10.7 %shard_map.53 = f32[2,16,128]{2,1,0:T(8,128)S(1)} custom-call(f32[16,128]{1,0:T(8,128)S(1)} %reshape.65.mine), custom_call_target="tpu_custom_call" | custom-call | tf_op jit(solution)/shard_map/pallas_call | solution.py:282
  123.5 3.0 %shard_map.54 = f32[2,16,6,32,128]{4,3,2,1,0:T(8,128)} custom-call(s32[2]{0:T(128)S(1)} %pad_add_fusion.place, f32[2,16]{1,0:T(2,128)S(1)} %rsqrt.3.inverse, f32[2,4,6,32,128]{4,3,2,1,0:T(8,128)S(1)} %get-tuple-element.44.vec.refs_0_.refs_2_, f32[2,4,6,32,128]{4,3,2,1,0:T(8,128)S(1)} %get-tuple-element.53.vec.refs_1_.refs_3_, ...), custom_call_target="tpu_custom_call" | custom-call | bytes 6291456 | tf_op jit(solution)/shard_map/pallas_call | solution.py:310
  (52 shorter events, 10.4 us)
Async XLA Ops:
  0.7 1.9 %copy-start = (f32[2,16,2,3,4,1024]{5,4,3,2,1,0:T(4,128)S(1)}, f32[2,16,2,3,4,1024]{5,4,3,2,1,0:T(4,128)}, u32[]{:S(2)}) copy-start(f32[2,16,2,3,4,1024]{5,4,3,2,1,0:T(4,128)} %param.3) | copy-start | bytes 9437188
  2.6 2.0 %copy-start.2 = (f32[4,3,2,3,3,4,512]{6,5,4,3,2,1,0:T(4,128)S(1)}, f32[4,3,2,3,3,4,512]{6,5,4,3,2,1,0:T(4,128)}, u32[]{:S(2)}) copy-start(f32[4,3,2,3,3,4,512]{6,5,4,3,2,1,0:T(4,128)} %param.2) | copy-start | bytes 5308420
  3.3 0.7 copy-start.4
  4.0 0.7 copy-start.5
  5.6 26.4 %copy-start.1 = (f32[2,16,2,3,4,1024]{5,4,3,2,1,0:T(4,128)S(1)}, f32[2,16,2,3,4,1024]{5,4,3,2,1,0:T(4,128)}, u32[]{:S(2)}) copy-start(f32[2,16,2,3,4,1024]{5,4,3,2,1,0:T(4,128)} %param.3) | copy-start | bytes 9437188
  5.6 17.0 %collective-permute-start = (f32[2,54,16,128]{3,2,1,0:T(8,128)}, f32[2,54,16,128]{3,2,1,0:T(8,128)}, u32[]{:S(2)}, u32[]{:S(2)}) collective-permute-start(f32[2,54,16,128]{3,2,1,0:T(8,128)} %constant_dynamic-slice_fusion.2), channel_id=1, source_target_pairs={{0,8},{8,0},{1,9},{9,1},{2,10},{10,2},{3,11},{11,3},{4,12},{12,4},... | collective-permute-start | bytes 2654216 | tf_op jit(solution)/shard_map/ppermute | solution.py:19
  9.1 8.7 %collective-permute-start.1 = (f32[2,18,4,128]{3,2,1,0:T(4,128)S(1)}, f32[2,18,4,128]{3,2,1,0:T(4,128)S(1)}, u32[]{:S(2)}, u32[]{:S(2)}) collective-permute-start(f32[2,18,4,128]{3,2,1,0:T(4,128)S(1)} %get-tuple-element.61), channel_id=1, source_target_pairs={{0,1},{1,2},{2,3},{3,4},{4,5},{5,6},{6,7},{7,0},{8,9},{9,10},{10,1... | collective-permute-start | bytes 221192 | tf_op jit(solution)/shard_map/ppermute | solution.py:19
  11.6 7.6 %collective-permute-start.2 = (f32[2,18,4,128]{3,2,1,0:T(4,128)S(1)}, f32[2,18,4,128]{3,2,1,0:T(4,128)S(1)}, u32[]{:S(2)}, u32[]{:S(2)}) collective-permute-start(f32[2,18,4,128]{3,2,1,0:T(4,128)S(1)} %get-tuple-element.60), channel_id=1, source_target_pairs={{0,9},{1,10},{2,11},{3,12},{4,13},{5,14},{6,15},{7,8},{8,1},{9,2},... | collective-permute-start | bytes 221192 | tf_op jit(solution)/shard_map/ppermute | solution.py:347
  13.1 18.9 %collective-permute-start.10 = (f32[2,4,6,8,128]{4,3,2,1,0:T(8,128)}, f32[2,4,6,8,128]{4,3,2,1,0:T(8,128)S(1)}, u32[]{:S(2)}, u32[]{:S(2)}) collective-permute-start(f32[2,4,6,8,128]{4,3,2,1,0:T(8,128)} %copy-done.5), channel_id=1, source_target_pairs={{0,7},{1,0},{2,1},{3,2},{4,3},{5,4},{6,5},{7,6},{8,15},{9,8},{10,9... | collective-permute-start | bytes 589832 | tf_op jit(solution)/shard_map/ppermute | solution.py:19
  16.3 15.7 %collective-permute-start.9 = (f32[2,4,6,8,128]{4,3,2,1,0:T(8,128)}, f32[2,4,6,8,128]{4,3,2,1,0:T(8,128)S(1)}, u32[]{:S(2)}, u32[]{:S(2)}) collective-permute-start(f32[2,4,6,8,128]{4,3,2,1,0:T(8,128)} %copy-done.4), channel_id=1, source_target_pairs={{0,1},{1,2},{2,3},{3,4},{4,5},{5,6},{6,7},{7,0},{8,9},{9,10},{10,1... | collective-permute-start | bytes 589832 | tf_op jit(solution)/shard_map/ppermute | solution.py:19
  17.9 22.6 %collective-permute-start.3 = (f32[2,4,6,8,128]{4,3,2,1,0:T(8,128)S(1)}, f32[2,4,6,8,128]{4,3,2,1,0:T(8,128)S(1)}, u32[]{:S(2)}, u32[]{:S(2)}) collective-permute-start(f32[2,4,6,8,128]{4,3,2,1,0:T(8,128)S(1)} %get-tuple-element.36), channel_id=1, source_target_pairs={{0,1},{1,2},{2,3},{3,4},{4,5},{5,6},{6,7},{7,0},{8,9},{9,10},{10,1... | collective-permute-start | bytes 589832 | tf_op jit(solution)/shard_map/ppermute | solution.py:19
  19.2 21.3 %collective-permute-start.4 = (f32[2,4,6,8,128]{4,3,2,1,0:T(8,128)S(1)}, f32[2,4,6,8,128]{4,3,2,1,0:T(8,128)S(1)}, u32[]{:S(2)}, u32[]{:S(2)}) collective-permute-start(f32[2,4,6,8,128]{4,3,2,1,0:T(8,128)S(1)} %get-tuple-element.37), channel_id=1, source_target_pairs={{0,7},{1,0},{2,1},{3,2},{4,3},{5,4},{6,5},{7,6},{8,15},{9,8},{10,9... | collective-permute-start | bytes 589832 | tf_op jit(solution)/shard_map/ppermute | solution.py:19
  22.6 1.5 %copy-start.3 = (f32[4,3,2,3,3,4,512]{6,5,4,3,2,1,0:T(4,128)S(1)}, f32[4,3,2,3,3,4,512]{6,5,4,3,2,1,0:T(4,128)}, u32[]{:S(2)}) copy-start(f32[4,3,2,3,3,4,512]{6,5,4,3,2,1,0:T(4,128)} %param.2) | copy-start | bytes 5308420
  35.7 13.4 %collective-permute-start.11 = (f32[2,4,6,8,128]{4,3,2,1,0:T(8,128)S(1)}, f32[2,4,6,8,128]{4,3,2,1,0:T(8,128)S(1)}, u32[]{:S(2)}, u32[]{:S(2)}) collective-permute-start(f32[2,4,6,8,128]{4,3,2,1,0:T(8,128)S(1)} %get-tuple-element.48), channel_id=1, source_target_pairs={{0,1},{1,2},{2,3},{3,4},{4,5},{5,6},{6,7},{7,0},{8,9},{9,10},{10,1... | collective-permute-start | bytes 589832 | tf_op jit(solution)/shard_map/ppermute | solution.py:19
  35.8 13.3 %collective-permute-start.12 = (f32[2,4,6,8,128]{4,3,2,1,0:T(8,128)S(1)}, f32[2,4,6,8,128]{4,3,2,1,0:T(8,128)S(1)}, u32[]{:S(2)}, u32[]{:S(2)}) collective-permute-start(f32[2,4,6,8,128]{4,3,2,1,0:T(8,128)S(1)} %get-tuple-element.49), channel_id=1, source_target_pairs={{0,7},{1,0},{2,1},{3,2},{4,3},{5,4},{6,5},{7,6},{8,15},{9,8},{10,9... | collective-permute-start | bytes 589832 | tf_op jit(solution)/shard_map/ppermute | solution.py:19
  44.1 13.4 %collective-permute-start.5 = (f32[2,4,6,8,128]{4,3,2,1,0:T(8,128)S(1)}, f32[2,4,6,8,128]{4,3,2,1,0:T(8,128)S(1)}, u32[]{:S(2)}, u32[]{:S(2)}) collective-permute-start(f32[2,4,6,8,128]{4,3,2,1,0:T(8,128)S(1)} %get-tuple-element.39), channel_id=1, source_target_pairs={{0,1},{1,2},{2,3},{3,4},{4,5},{5,6},{6,7},{7,0},{8,9},{9,10},{10,1... | collective-permute-start | bytes 589832 | tf_op jit(solution)/shard_map/ppermute | solution.py:19
  44.2 13.4 %collective-permute-start.6 = (f32[2,4,6,8,128]{4,3,2,1,0:T(8,128)S(1)}, f32[2,4,6,8,128]{4,3,2,1,0:T(8,128)S(1)}, u32[]{:S(2)}, u32[]{:S(2)}) collective-permute-start(f32[2,4,6,8,128]{4,3,2,1,0:T(8,128)S(1)} %get-tuple-element.40), channel_id=1, source_target_pairs={{0,7},{1,0},{2,1},{3,2},{4,3},{5,4},{6,5},{7,6},{8,15},{9,8},{10,9... | collective-permute-start | bytes 589832 | tf_op jit(solution)/shard_map/ppermute | solution.py:19
  52.8 13.3 %collective-permute-start.13 = (f32[2,4,6,8,128]{4,3,2,1,0:T(8,128)S(1)}, f32[2,4,6,8,128]{4,3,2,1,0:T(8,128)S(1)}, u32[]{:S(2)}, u32[]{:S(2)}) collective-permute-start(f32[2,4,6,8,128]{4,3,2,1,0:T(8,128)S(1)} %get-tuple-element.51), channel_id=1, source_target_pairs={{0,1},{1,2},{2,3},{3,4},{4,5},{5,6},{6,7},{7,0},{8,9},{9,10},{10,1... | collective-permute-start | bytes 589832 | tf_op jit(solution)/shard_map/ppermute | solution.py:19
  55.3 14.5 %collective-permute-start.14 = (f32[2,4,6,8,128]{4,3,2,1,0:T(8,128)S(1)}, f32[2,4,6,8,128]{4,3,2,1,0:T(8,128)S(1)}, u32[]{:S(2)}, u32[]{:S(2)}) collective-permute-start(f32[2,4,6,8,128]{4,3,2,1,0:T(8,128)S(1)} %get-tuple-element.52), channel_id=1, source_target_pairs={{0,7},{1,0},{2,1},{3,2},{4,3},{5,4},{6,5},{7,6},{8,15},{9,8},{10,9... | collective-permute-start | bytes 589832 | tf_op jit(solution)/shard_map/ppermute | solution.py:19
  61.3 14.4 %collective-permute-start.7 = (f32[2,4,6,8,128]{4,3,2,1,0:T(8,128)S(1)}, f32[2,4,6,8,128]{4,3,2,1,0:T(8,128)S(1)}, u32[]{:S(2)}, u32[]{:S(2)}) collective-permute-start(f32[2,4,6,8,128]{4,3,2,1,0:T(8,128)S(1)} %get-tuple-element.42), channel_id=1, source_target_pairs={{0,1},{1,2},{2,3},{3,4},{4,5},{5,6},{6,7},{7,0},{8,9},{9,10},{10,1... | collective-permute-start | bytes 589832 | tf_op jit(solution)/shard_map/ppermute | solution.py:19
  61.4 14.3 %collective-permute-start.8 = (f32[2,4,6,8,128]{4,3,2,1,0:T(8,128)S(1)}, f32[2,4,6,8,128]{4,3,2,1,0:T(8,128)S(1)}, u32[]{:S(2)}, u32[]{:S(2)}) collective-permute-start(f32[2,4,6,8,128]{4,3,2,1,0:T(8,128)S(1)} %get-tuple-element.43), channel_id=1, source_target_pairs={{0,7},{1,0},{2,1},{3,2},{4,3},{5,4},{6,5},{7,6},{8,15},{9,8},{10,9... | collective-permute-start | bytes 589832 | tf_op jit(solution)/shard_map/ppermute | solution.py:19
  74.2 20.7 %collective-permute-start.18 = (f32[2,4,6,32,128]{4,3,2,1,0:T(8,128)S(1)}, f32[2,4,6,32,128]{4,3,2,1,0:T(8,128)S(1)}, u32[]{:S(2)}, u32[]{:S(2)}) collective-permute-start(f32[2,4,6,32,128]{4,3,2,1,0:T(8,128)S(1)} %get-tuple-element.53.vec.refs_1_.refs_3_), channel_id=1, source_target_pairs={{0,16},{16,0},{1,17},{17,1},{2,18},{18,2},{3,19},{19,3},{4,20},{20... | collective-permute-start | bytes 2359304 | tf_op jit(solution)/shard_map/ppermute | solution.py:19
  80.1 28.2 %collective-permute-start.17 = (f32[2,4,6,32,128]{4,3,2,1,0:T(8,128)S(1)}, f32[2,4,6,32,128]{4,3,2,1,0:T(8,128)S(1)}, u32[]{:S(2)}, u32[]{:S(2)}) collective-permute-start(f32[2,4,6,32,128]{4,3,2,1,0:T(8,128)S(1)} %get-tuple-element.44.vec.refs_0_.refs_2_), channel_id=1, source_target_pairs={{0,16},{16,0},{1,17},{17,1},{2,18},{18,2},{3,19},{19,3},{4,20},{20... | collective-permute-start | bytes 2359304 | tf_op jit(solution)/shard_map/ppermute | solution.py:19
  80.6 7.8 %collective-permute-start.16 = (f32[2,4,6,8,128]{4,3,2,1,0:T(8,128)S(1)}, f32[2,4,6,8,128]{4,3,2,1,0:T(8,128)S(1)}, u32[]{:S(2)}, u32[]{:S(2)}) collective-permute-start(f32[2,4,6,8,128]{4,3,2,1,0:T(8,128)S(1)} %get-tuple-element.55), channel_id=1, source_target_pairs={{0,7},{1,0},{2,1},{3,2},{4,3},{5,4},{6,5},{7,6},{8,15},{9,8},{10,9... | collective-permute-start | bytes 589832 | tf_op jit(solution)/shard_map/ppermute | solution.py:19
  83.3 7.3 %collective-permute-start.15 = (f32[2,4,6,8,128]{4,3,2,1,0:T(8,128)S(1)}, f32[2,4,6,8,128]{4,3,2,1,0:T(8,128)S(1)}, u32[]{:S(2)}, u32[]{:S(2)}) collective-permute-start(f32[2,4,6,8,128]{4,3,2,1,0:T(8,128)S(1)} %get-tuple-element.54), channel_id=1, source_target_pairs={{0,7},{1,0},{2,1},{3,2},{4,3},{5,4},{6,5},{7,6},{8,15},{9,8},{10,9... | collective-permute-start | bytes 589832 | tf_op jit(solution)/shard_map/ppermute | solution.py:19
